TPU v7x, 128 devices: a whole 4x4x4 slice. The times are simulated.
128 devices in a mesh: wide: 64 (over z, y, x), narrow: 2 (over core).
Axes of the slice: x: 4, y: 4, z: 4, core: 2. Of those that a mesh axis runs over, the one named last changes fastest.
Arguments:
- grid_state: bfloat16 [262144, 100], P(('wide', 'narrow')), may hold values from -6 to 6
- latent_init: bfloat16 [32768, 1024], P(('wide', 'narrow')), may hold values from -6 to 6
- enc_src: int32 [32768, 16], P(('wide', 'narrow')), may hold values from 0 to 4095, as said below
- enc_count: int32 [32768], P(('wide', 'narrow')), may hold values from 4 to 16
- dec_src: int32 [262144, 3], P(('wide', 'narrow')), may hold values from 0 to 32767, as said below
- w_in: bfloat16 [100, 1024], replicated, may hold values from -0.625 to 0.625
- enc_w: bfloat16 [4, 1024, 1024], replicated, may hold values from -0.1875 to 0.1875
- proc_w: bfloat16 [4, 1024, 1024], replicated, may hold values from -0.1875 to 0.1875
- dec_w: bfloat16 [4, 1024, 1024], replicated, may hold values from -0.1875 to 0.1875
- w_out: bfloat16 [1024, 100], replicated, may hold values from -0.1875 to 0.1875
- logit_scale: float32 [3, 16], replicated, may hold values from 0.5 to 3
Outputs:
- tendency: bfloat16 [262144, 100], P(('wide', 'narrow'))
Inputs may be any that keep to these rules, and one draw needn't show every extreme that they name: Row i, with d = i // 256, names grid point d * 2048 - 1024 + enc_src[i, e], which always lies in the grid; slots at or past enc_count[i] are padding. `dec_src`: row g, with d = g // 2048, names latent nodes from d * 256 - 128 to (d + 1) * 256 + 127, clipped to the latent nodes.
All inputs are finite; a program needn't handle non-finite values.
Results may differ from a plain program's by a relative error of at most 0.025.
Values may be sent and summed in bfloat16 or wider, within the bound.
No kernel may reach another device: no remote copies, remote signals or barrier semaphores. Data moves between devices by JAX's collectives and lax.ppermute only.
A program may use at most 256 MiB of HBM per device.

v0:
```python
import math

import jax
import jax.numpy as jnp
from jax import lax
from jax.sharding import PartitionSpec as P

WIN = 512
BG = 1024
BL = 128


def padded(cells, sides, width):
    for axis, dim in sides:
        count = lax.axis_size(axis)
        ends = count - 1
        head = lax.slice_in_dim(cells, 0, width, axis=dim)
        tail = lax.slice_in_dim(cells, cells.shape[dim] - width, cells.shape[dim], axis=dim)
        cells = jnp.concatenate(
            [
                lax.ppermute(tail, axis, [(i, (i + 1) % count) for i in range(ends)]),
                cells,
                lax.ppermute(head, axis, [((i + 1) % count, i) for i in range(ends)]),
            ],
            axis=dim,
        )
    return cells


def layer_norm(values):
    center = values - jnp.mean(values, axis=-1, keepdims=True)
    spread = jnp.mean(center * center, axis=-1, keepdims=True)
    return center * lax.rsqrt(spread + 1e-05)


def edge_attend(query, keys, values, scale, valid):
    rows, degree, width = keys.shape
    heads = scale.shape[0]
    size = width // heads
    product = query.astype(jnp.float32)[:, None, :] * keys.astype(jnp.float32)
    scores = product.reshape(rows, degree, heads, size).sum(axis=-1) * (scale / math.sqrt(size))
    scores = jnp.where(valid[:, :, None], scores, -1e30)
    highest = jnp.max(scores, axis=1, keepdims=True)
    expo = jnp.where(valid[:, :, None], jnp.exp(scores - highest), 0.0)
    weights = expo / jnp.sum(expo, axis=1, keepdims=True)
    spread_weights = jnp.repeat(weights, size, axis=2)
    return jnp.sum(spread_weights * values.astype(jnp.float32), axis=1)


def window_attend(query, keys_wide, values_wide, scale, first, total):
    rows, width = query.shape
    heads = scale.shape[0]
    size = width // heads
    groups = heads // 4
    length = min(512, rows)
    span = length + WIN
    reach = WIN // 2
    factor = scale / math.sqrt(size)

    def one_block(number):
        begin = number * length
        queries = query.reshape(length, groups, 4, size)
        near_keys = keys_wide.reshape(span, groups, 4, size)
        near_values = values_wide.reshape(span, groups, 4, size)
        query_place = first + begin + jnp.arange(length, dtype=jnp.int32)
        key_place = first + begin - reach + jnp.arange(span, dtype=jnp.int32)
        inside = (
            (jnp.abs(key_place[None, :] - query_place[:, None]) <= reach)
            & (key_place[None, :] >= 0)
            & (key_place[None, :] < total)
        )

        def one_group(group):
            group_queries = lax.dynamic_index_in_dim(queries, group, 1, keepdims=False)
            group_keys = lax.dynamic_index_in_dim(near_keys, group, 1, keepdims=False)
            group_values = lax.dynamic_index_in_dim(near_values, group, 1, keepdims=False)
            group_factor = lax.dynamic_slice_in_dim(factor, group * 4, 4, 0)
            scores = (
                jnp.einsum(
                    "qhd,khd->hqk", group_queries, group_keys, preferred_element_type=jnp.float32
                )
                * group_factor[:, None, None]
            )
            scores = jnp.where(inside[None], scores, -1e30)
            highest = jnp.max(scores, axis=-1, keepdims=True)
            expo = jnp.where(inside[None], jnp.exp(scores - highest), 0.0)
            weights = (expo / jnp.sum(expo, axis=-1, keepdims=True)).astype(jnp.bfloat16)
            return jnp.einsum(
                "hqk,khd->qhd", weights, group_values, preferred_element_type=jnp.float32
            )

        mixed = lax.map(one_group, jnp.arange(groups, dtype=jnp.int32))
        return jnp.transpose(mixed, (1, 0, 2, 3)).reshape(length, width)

    result = lax.map(one_block, jnp.arange(rows // length, dtype=jnp.int32))
    return result.reshape(rows, width)


def project(rows, weight):
    return jnp.dot(rows, weight, preferred_element_type=jnp.float32)


def on_device(
    grid_state,
    latent_init,
    enc_src,
    enc_count,
    dec_src,
    w_in,
    enc_w,
    proc_w,
    dec_w,
    w_out,
    logit_scale,
):
    grid_rows = grid_state.shape[0]
    latent_rows = latent_init.shape[0]
    width = latent_init.shape[1]
    place = lax.axis_index(("wide", "narrow"))
    total = latent_rows * lax.axis_size(("wide", "narrow"))
    embed = project(grid_state, w_in).astype(jnp.bfloat16)
    enc_pair = jnp.concatenate([enc_w[1], enc_w[2]], axis=1)
    own_pairs = project(embed, enc_pair).astype(jnp.bfloat16)
    grid_pairs = padded(own_pairs, ((("wide", "narrow"), 0),), BG)
    local_source = enc_src.reshape(-1)
    gathered = jnp.take(grid_pairs, local_source, axis=0).reshape(
        latent_rows, enc_src.shape[1], 2 * width
    )
    enc_query = project(latent_init, enc_w[0]).astype(jnp.bfloat16)
    valid = jnp.arange(enc_src.shape[1], dtype=jnp.int32)[None, :] < enc_count[:, None]
    encoded = edge_attend(
        enc_query, gathered[:, :, :width], gathered[:, :, width:], logit_scale[0], valid
    ).astype(jnp.bfloat16)
    latent = (latent_init.astype(jnp.float32) + project(encoded, enc_w[3])).astype(jnp.bfloat16)
    normed = layer_norm(latent.astype(jnp.float32)).astype(jnp.bfloat16)
    window_query = project(normed, proc_w[0]).astype(jnp.bfloat16)
    proc_pair = jnp.concatenate([proc_w[1], proc_w[2]], axis=1)
    reach = WIN // 2
    own_window = project(normed, proc_pair).astype(jnp.bfloat16)
    window_wide = padded(own_window, ((("wide", "narrow"), 0),), reach)
    windowed = window_attend(
        window_query,
        window_wide[:, :width],
        window_wide[:, width:],
        logit_scale[1],
        place * latent_rows,
        total,
    ).astype(jnp.bfloat16)
    latent_out = (latent.astype(jnp.float32) + project(windowed, proc_w[3])).astype(jnp.bfloat16)
    dec_pair = jnp.concatenate([dec_w[1], dec_w[2]], axis=1)
    own_mesh = project(latent_out, dec_pair).astype(jnp.bfloat16)
    mesh_wide = padded(own_mesh, ((("wide", "narrow"), 0),), BL)
    mesh_source = (dec_src - (place * latent_rows - BL)).reshape(-1)
    picked = jnp.take(mesh_wide, mesh_source, axis=0).reshape(
        grid_rows, dec_src.shape[1], 2 * width
    )
    dec_query = project(embed, dec_w[0]).astype(jnp.bfloat16)
    every = jnp.ones((grid_rows, dec_src.shape[1]), dtype=bool)
    decoded = edge_attend(
        dec_query, picked[:, :, :width], picked[:, :, width:], logit_scale[2], every
    ).astype(jnp.bfloat16)
    update = (embed.astype(jnp.float32) + project(decoded, dec_w[3])).astype(jnp.bfloat16)
    return project(update, w_out).astype(jnp.bfloat16)


def solution(mesh):
    placed = (
        P(("wide", "narrow"), None),
        P(("wide", "narrow"), None),
        P(("wide", "narrow"), None),
        P(("wide", "narrow")),
        P(("wide", "narrow"), None),
        P(),
        P(),
        P(),
        P(),
        P(),
        P(),
    )
    return jax.shard_map(
        on_device,
        mesh=mesh,
        in_specs=placed,
        out_specs=P(("wide", "narrow"), None),
        check_vma=False,
    )
```

profile of v0, /device:TPU:96, one launch (start us, length us, event | category | flops | bytes accessed | tf_op | source)
XLA Modules:
  0.0 542.3 jit_solution(6921389142917632476)
XLA Ops:
  0.0 2.7 slice_bitcast_fusion.5
  4.1 9.4 %convolution_convert_fusion = bf16[2048,2048]{1,0:T(8,128)(2,1)S(1)} fusion(bf16[2048,1024]{1,0:T(8,128)(2,1)S(1)} %convolution_convert_fusion.1, bf16[1024,1024]{1,0:T(8,128)(2,1)S(1)} %get-tuple-element.137, bf16[1024,1024]{1,0:T(8,128)(2,1)S(1)} %get-tuple-element.136), kind=kOutput, calls=%fused_computation.38 | convolution fusion | flops 8602517504 | bytes 16777216 | tf_op jit(solution)/shard_map/dot_general | solution.py:100
  13.5 3.8 fusion.108
  17.3 1.9 copy-done.2
  19.2 1.9 collective-permute-start
  21.1 7.9 %collective-permute-start.1 = (bf16[1024,2048]{1,0:T(8,128)(2,1)}, bf16[1024,2048]{1,0:T(8,128)(2,1)}, u32[]{:S(2)}, u32[]{:S(2)}) collective-permute-start(bf16[1024,2048]{1,0:T(8,128)(2,1)} %get-tuple-element.135), channel_id=1, source_target_pairs={{1,0},{2,1},{3,2},{4,3},{5,4},{6,5},{7,6},{8,7},{9,8},{10,9},{11,1... | collective-permute-start | bytes 12582920 | tf_op jit(solution)/shard_map/ppermute | solution.py:23
  30.4 2.3 fusion.82
  34.7 4.7 slice_bitcast_fusion.3
  39.4 34.1 %collective-permute-done = bf16[1024,2048]{1,0:T(8,128)(2,1)} collective-permute-done((bf16[1024,2048]{1,0:T(8,128)(2,1)}, bf16[1024,2048]{1,0:T(8,128)(2,1)}, u32[]{:S(2)}, u32[]{:S(2)}) %collective-permute-start) | collective-permute-done | bytes 4194336 | tf_op jit(solution)/shard_map/ppermute | solution.py:21
  73.5 1.8 collective-permute-done.1
  75.3 14.2 %pad_maximum_fusion = bf16[4096,2048]{1,0:T(8,128)(2,1)} fusion(bf16[1024,2048]{1,0:T(8,128)(2,1)} %collective-permute-done.1, bf16[2048,2048]{1,0:T(8,128)(2,1)} %copy-done.2, bf16[1024,2048]{1,0:T(8,128)(2,1)} %collective-permute-done), kind=kLoop, calls=%fused_computation.31 | loop fusion | flops 50331648 | bytes 33554432 | tf_op jit(solution)/shard_map/concatenate | solution.py:19
  89.5 39.3 %gather_fusion = bf16[4096,2048]{1,0:T(8,128)(2,1)} fusion(bf16[4096,2048]{1,0:T(8,128)(2,1)} %pad_maximum_fusion, s32[4096]{0:T(1024)S(1)} %broadcast_clamp_fusion.1), kind=kCustom, calls=%fused_computation | custom fusion | bytes 33570816 | tf_op jit(solution)/shard_map/jit(_take)/gather | solution.py:126
  128.7 23.8 %copy.30 = bf16[256,16,2048]{0,2,1:T(8,128)(2,1)} copy(bf16[256,16,2048]{2,1,0:T(8,128)(2,1)} %bitcast.112) | data formatting | bytes 33554432 | tf_op jit(solution)/shard_map/jit(_take)/gather | solution.py:126
  152.5 8.8 %broadcast_select_fusion.1 = bf16[256,16,2048]{0,2,1:T(8,128)(2,1)S(1)} fusion(bf16[256,16,2048]{0,2,1:T(8,128)(2,1)} %copy.30, pred[256,16]{0,1:T(8,128)(4,1)S(1)} %compare_and_fusion.1), kind=kLoop, calls=%fused_computation.36 | loop fusion | flops 8388608 | bytes 33558528 | tf_op jit(solution)/shard_map/jit(_take)/select_n | solution.py:126
  161.3 4.7 bitcast_reduce_fusion.1
  166.4 2.5 fusion.22
  168.9 2.8 convert_reduce_fusion
  173.5 8.0 %collective-permute-start.3 = (bf16[256,2048]{1,0:T(8,128)(2,1)S(1)}, bf16[256,2048]{1,0:T(8,128)(2,1)}, u32[]{:S(2)}, u32[]{:S(2)}) collective-permute-start(bf16[256,2048]{1,0:T(8,128)(2,1)S(1)} %fusion.40), channel_id=1, source_target_pairs={{1,0},{2,1},{3,2},{4,3},{5,4},{6,5},{7,6},{8,7},{9,8},{10,9},{11,1... | collective-permute-start | bytes 3145736 | tf_op jit(solution)/shard_map/ppermute | solution.py:23
  181.5 2.1 collective-permute-start.2
  183.7 4.6 slice_bitcast_fusion.1
  188.3 2.3 fusion.79
  190.9 2.9 collective-permute-done.3
  193.8 8.1 %collective-permute-done.2 = bf16[256,2048]{1,0:T(8,128)(2,1)} collective-permute-done((bf16[256,2048]{1,0:T(8,128)(2,1)S(1)}, bf16[256,2048]{1,0:T(8,128)(2,1)}, u32[]{:S(2)}, u32[]{:S(2)}) %collective-permute-start.2) | collective-permute-done | bytes 1048608 | tf_op jit(solution)/shard_map/ppermute | solution.py:21
  203.6 2.0 fusion.109
  205.7 1.7 copy.33
  207.4 2.6 copy.31
  210.0 35.3 %while.18 = (s32[]{:T(128)}, bf16[4,256,4,64]{1,3,2,0:T(8,128)(2,1)}, s32[4]{0:T(128)S(1)}, bf16[768,4,4,64]{0,3,2,1:T(8,128)(2,1)}, bf16[256,4,4,64]{0,3,2,1:T(...) while((s32[]{:T(128)}, ...), condition=%wide.region_9.10_spmd.clone, body=%wide.region_6.9_spmd.clone.sunk | while | flops 209388288 | bytes 18365284 | solution.py:92
  214.4 1.9 fusion.132
  216.3 1.7 fusion.133
  223.3 1.9 fusion.132
  225.1 1.7 fusion.133
  232.1 1.9 fusion.132
  234.0 1.7 fusion.133
  240.9 1.9 fusion.132
  245.3 4.8 fusion.37
  250.3 1.9 collective-permute-start.4
  252.2 8.1 %collective-permute-start.5 = (bf16[128,2048]{1,0:T(8,128)(2,1)S(1)}, bf16[128,2048]{1,0:T(8,128)(2,1)}, u32[]{:S(2)}, u32[]{:S(2)}) collective-permute-start(bf16[128,2048]{1,0:T(8,128)(2,1)S(1)} %get-tuple-element.145), channel_id=1, source_target_pairs={{1,0},{2,1},{3,2},{4,3},{5,4},{6,5},{7,6},{8,7},{9,8},{10,9},{11,1... | collective-permute-start | bytes 1572872 | tf_op jit(solution)/shard_map/ppermute | solution.py:23
  260.3 10.6 %convert_convert_fusion = f32[2048,1024]{1,0:T(8,128)} fusion(bf16[2048,1024]{1,0:T(8,128)(2,1)} %copy-done.3, bf16[4,1024,1024]{2,1,0:T(8,128)(2,1)} %param.21), kind=kOutput, calls=%fused_computation.53 | convolution fusion | flops 4299161600 | bytes 14680064 | tf_op jit(solution)/shard_map/dot_general | solution.py:100
  272.9 30.9 %gather_fusion.1 = bf16[6144,2048]{1,0:T(8,128)(2,1)} fusion(bf16[512,2048]{1,0:T(8,128)(2,1)S(1)} %pad_maximum_fusion.2, s32[6144]{0:T(1024)S(1)} %broadcast_clamp_fusion), kind=kCustom, calls=%fused_computation.1 | custom fusion | bytes 50356224 | tf_op jit(solution)/shard_map/jit(_take)/gather | solution.py:154
  303.8 63.4 %gather.15 = bf16[2048,3,2048]{2,1,0:T(4,128)(2,1)} reshape(bf16[6144,2048]{1,0:T(8,128)(2,1)} %gather_fusion.1) | data formatting | bytes 50331648 | tf_op jit(solution)/shard_map/jit(_take)/gather | solution.py:154
  367.2 22.6 %broadcast_select_fusion = bf16[2048,3,2048]{2,1,0:T(4,128)(2,1)} fusion(bf16[2048,3,2048]{2,1,0:T(4,128)(2,1)} %gather.15, pred[2048,3]{1,0:T(8,128)(4,1)S(1)} %copy.27), kind=kLoop, calls=%fused_computation.29 | loop fusion | flops 12582912 | bytes 50337792 | tf_op jit(solution)/shard_map/jit(_take)/select_n | solution.py:154
  389.8 19.8 %convert_multiply_fusion = f32[2048,3,1024]{2,1,0:T(4,128)} fusion(bf16[2048,3,2048]{2,1,0:T(4,128)(2,1)} %broadcast_select_fusion, f32[2048,1024]{1,0:T(8,128)} %convert_convert_fusion), kind=kLoop, calls=%fused_computation.28 | loop fusion | flops 12582912 | bytes 46137344 | tf_op jit(solution)/shard_map/mul | solution.py:40
  409.6 34.3 %copy.35 = f32[2048,3,1024]{0,2,1:T(8,128)} copy(f32[2048,3,1024]{2,1,0:T(4,128)} %convert_multiply_fusion) | data formatting | bytes 50331648 | tf_op jit(solution)/shard_map/mul | solution.py:40
  443.9 9.5 %bitcast_reduce_fusion = f32[2048,3,16]{0,2,1:T(8,128)S(1)} fusion(f32[2048,3,1024]{0,2,1:T(8,128)} %copy.35), kind=kLoop, calls=%fused_computation.30 | loop fusion | flops 6193152 | bytes 25559040 | tf_op jit(solution)/shard_map/reduce_sum | solution.py:41
  453.8 11.5 %broadcast_in_dim.115 = f32[2048,3,16,64]{0,3,2,1:T(8,128)} broadcast(f32[2048,3,16]{0,2,1:T(8,128)S(1)} %fusion.95), dimensions={0,1,2} | broadcast | bytes 25559040 | tf_op jit(solution)/shard_map/broadcast_in_dim | solution.py:46
  465.3 35.9 %copy.36 = f32[2048,3,1024]{2,1,0:T(4,128)} copy(f32[2048,3,1024]{0,2,1:T(8,128)} %bitcast.111) | data formatting | bytes 50331648 | tf_op jit(solution)/shard_map/reshape | solution.py:46
  501.2 30.2 %multiply_reduce_fusion = bf16[2048,1024]{1,0:T(8,128)(2,1)} fusion(f32[2048,3,1024]{2,1,0:T(4,128)} %copy.36, bf16[2048,3,2048]{2,1,0:T(4,128)(2,1)} %broadcast_select_fusion), kind=kLoop, calls=%fused_computation.27 | loop fusion | flops 16777216 | bytes 41943040 | tf_op jit(solution)/shard_map/reduce_sum | solution.py:47
  531.4 10.6 %fusion.43 = bf16[2048,100]{0,1:T(8,128)(2,1)} fusion(bf16[1024,100]{0,1:T(8,128)(2,1)S(1)} %copy-done.14, bf16[2048,1024]{1,0:T(8,128)(2,1)} %copy-done.3, bf16[2048,1024]{1,0:T(8,128)(2,1)} %multiply_reduce_fusion, bf16[4,1024,1024]{2,1,0:T(8,128)(2,1)} %param.21), kind=kOutput, calls=%fused_computation.58 | convolution fusion | flops 4720893952 | bytes 11100160 | tf_op jit(solution)/shard_map/dot_general | solution.py:100
  (98 shorter events, 22.7 us)
Async XLA Ops:
  0.0 2.7 copy-start
  0.0 2.7 copy-start.7
  4.1 9.4 %copy-start.3 = (bf16[2048,1024]{1,0:T(8,128)(2,1)}, bf16[2048,1024]{1,0:T(8,128)(2,1)S(1)}, u32[]{:S(2)}) copy-start(bf16[2048,1024]{1,0:T(8,128)(2,1)S(1)} %convolution_convert_fusion.1) | copy-start | bytes 12582916
  13.5 5.7 %copy-start.2 = (bf16[2048,2048]{1,0:T(8,128)(2,1)}, bf16[2048,2048]{1,0:T(8,128)(2,1)S(1)}, u32[]{:S(2)}) copy-start(bf16[2048,2048]{1,0:T(8,128)(2,1)S(1)} %convolution_convert_fusion) | copy-start | bytes 25165828
  13.5 15.5 %copy-start.8 = (s32[256,16]{0,1:T(8,128)S(1)}, s32[256,16]{0,1:T(8,128)}, u32[]{:S(2)}) copy-start(s32[256,16]{0,1:T(8,128)} %param.15) | copy-start | bytes 49156
  13.5 15.8 %copy-start.9 = (s32[2048,3]{0,1:T(4,128)S(1)}, s32[2048,3]{0,1:T(4,128)}, u32[]{:S(2)}) copy-start(s32[2048,3]{0,1:T(4,128)} %param.17) | copy-start | bytes 73732
  13.5 16.9 %copy-start.13 = (bf16[256,1024]{1,0:T(8,128)(2,1)S(1)}, bf16[256,1024]{1,0:T(8,128)(2,1)}, u32[]{:S(2)}) copy-start(bf16[256,1024]{1,0:T(8,128)(2,1)} %param.14) | copy-start | bytes 1572868
  19.2 54.3 %collective-permute-start = (bf16[1024,2048]{1,0:T(8,128)(2,1)}, bf16[1024,2048]{1,0:T(8,128)(2,1)}, u32[]{:S(2)}, u32[]{:S(2)}) collective-permute-start(bf16[1024,2048]{1,0:T(8,128)(2,1)} %get-tuple-element.134), channel_id=1, source_target_pairs={{0,1},{1,2},{2,3},{3,4},{4,5},{5,6},{6,7},{7,8},{8,9},{9,10},{10,1... | collective-permute-start | bytes 12582920 | tf_op jit(solution)/shard_map/ppermute | solution.py:21
  21.1 54.2 %collective-permute-start.1 = (bf16[1024,2048]{1,0:T(8,128)(2,1)}, bf16[1024,2048]{1,0:T(8,128)(2,1)}, u32[]{:S(2)}, u32[]{:S(2)}) collective-permute-start(bf16[1024,2048]{1,0:T(8,128)(2,1)} %get-tuple-element.135), channel_id=1, source_target_pairs={{1,0},{2,1},{3,2},{4,3},{5,4},{6,5},{7,6},{8,7},{9,8},{10,9},{11,1... | collective-permute-start | bytes 12582920 | tf_op jit(solution)/shard_map/ppermute | solution.py:23
  29.2 4.8 copy-start.11
  29.3 5.3 copy-start.12
  168.9 3.1 copy-start.5
  168.9 3.2 copy-start.6
  173.5 20.3 %collective-permute-start.3 = (bf16[256,2048]{1,0:T(8,128)(2,1)S(1)}, bf16[256,2048]{1,0:T(8,128)(2,1)}, u32[]{:S(2)}, u32[]{:S(2)}) collective-permute-start(bf16[256,2048]{1,0:T(8,128)(2,1)S(1)} %fusion.40), channel_id=1, source_target_pairs={{1,0},{2,1},{3,2},{4,3},{5,4},{6,5},{7,6},{8,7},{9,8},{10,9},{11,1... | collective-permute-start | bytes 3145736 | tf_op jit(solution)/shard_map/ppermute | solution.py:23
  181.5 20.4 %collective-permute-start.2 = (bf16[256,2048]{1,0:T(8,128)(2,1)S(1)}, bf16[256,2048]{1,0:T(8,128)(2,1)}, u32[]{:S(2)}, u32[]{:S(2)}) collective-permute-start(bf16[256,2048]{1,0:T(8,128)(2,1)S(1)} %fusion.40), channel_id=1, source_target_pairs={{0,1},{1,2},{2,3},{3,4},{4,5},{5,6},{6,7},{7,8},{8,9},{9,10},{10,1... | collective-permute-start | bytes 3145736 | tf_op jit(solution)/shard_map/ppermute | solution.py:21
  214.4 1.9 copy-start.15
  218.0 0.8 copy-start.16
  223.2 1.9 copy-start.15
  226.8 0.8 copy-start.16
  232.1 1.9 copy-start.15
  235.7 0.8 copy-start.16
  240.9 1.9 copy-start.15
  244.5 0.8 copy-start.16
  250.1 20.7 %copy-start.4 = (bf16[256,2048]{1,0:T(8,128)(2,1)}, bf16[256,2048]{1,0:T(8,128)(2,1)S(1)}, u32[]{:S(2)}) copy-start(bf16[256,2048]{1,0:T(8,128)(2,1)S(1)} %fusion.37) | copy-start | bytes 3145732
  250.3 21.1 %collective-permute-start.4 = (bf16[128,2048]{1,0:T(8,128)(2,1)S(1)}, bf16[128,2048]{1,0:T(8,128)(2,1)S(1)}, u32[]{:S(2)}, u32[]{:S(2)}) collective-permute-start(bf16[128,2048]{1,0:T(8,128)(2,1)S(1)} %get-tuple-element.144), channel_id=1, source_target_pairs={{0,1},{1,2},{2,3},{3,4},{4,5},{5,6},{6,7},{7,8},{8,9},{9,10},{10,1... | collective-permute-start | bytes 1572872 | tf_op jit(solution)/shard_map/ppermute | solution.py:21
  252.2 19.2 %collective-permute-start.5 = (bf16[128,2048]{1,0:T(8,128)(2,1)S(1)}, bf16[128,2048]{1,0:T(8,128)(2,1)}, u32[]{:S(2)}, u32[]{:S(2)}) collective-permute-start(bf16[128,2048]{1,0:T(8,128)(2,1)S(1)} %get-tuple-element.145), channel_id=1, source_target_pairs={{1,0},{2,1},{3,2},{4,3},{5,4},{6,5},{7,6},{8,7},{9,8},{10,9},{11,1... | collective-permute-start | bytes 1572872 | tf_op jit(solution)/shard_map/ppermute | solution.py:23
  443.9 9.5 %copy-start.10 = (f32[16]{0:T(128)S(1)}, f32[16]{0:T(128)}, u32[]{:S(2)}) copy-start(f32[16]{0:T(128)} %get-tuple-element.146) | copy-start | bytes 196
  501.2 30.2 %copy-start.14 = (bf16[1024,100]{0,1:T(8,128)(2,1)S(1)}, bf16[1024,100]{0,1:T(8,128)(2,1)}, u32[]{:S(2)}) copy-start(bf16[1024,100]{0,1:T(8,128)(2,1)} %param.22) | copy-start | bytes 614404
  531.4 10.6 %copy-start.1 = (bf16[2048,100]{0,1:T(8,128)(2,1)S(1)}, bf16[2048,100]{0,1:T(8,128)(2,1)}, u32[]{:S(2)}) copy-start(bf16[2048,100]{0,1:T(8,128)(2,1)} %param.13) | copy-start | bytes 1228804
where the time goes:
time: 552 us; the launch traced here: 542 us
  local copies, waits for them, and re-layouts  273 us (49%)
  other arithmetic  126 us (23%)
  matrix products  54.7 us (10%)
  waiting for transfers between devices  47 us (9%)
  starting transfers between devices  29.9 us (5%)
  loops' own time  11.1 us (2%)
    gather x2, local copies, waits for them, and re-layouts, on_device(): jnp.take(mesh_wide, mesh_source, axis=0)  94.3 us
    gather x2, local copies, waits for them, and re-layouts, on_device(): jnp.take(grid_pairs, local_source, axis=0)  63 us
    dot_general x9, matrix products, project(): return jnp.dot(rows, weight, preferred_element_type=jnp.float32)  45.5 us
    ppermute x3, waiting for transfers between devices, padded(): lax.ppermute(tail, axis, [(i, (i + 1) % count) for i in range(ends)])  42.3 us
    reshape x1, local copies, waits for them, and re-layouts, edge_attend(): spread_weights = jnp.repeat(weights, size, axis=2)  35.9 us
    mul x1, local copies, waits for them, and re-layouts, edge_attend(): product = query.astype(jnp.float32)[:, None, :] * keys.astype(jnp.float32)  34.3 us
    reduce_sum x2, other arithmetic, edge_attend(): return jnp.sum(spread_weights * values.astype(jnp.float32), axis=1)  32.7 us
    ppermute x3, starting transfers between devices, padded(): lax.ppermute(head, axis, [((i + 1) % count, i) for i in range(ends)])  24 us
  transfers between devices with their start and end apart: 6, of which 4 were waited for; matrix products, arithmetic and copies ran while one was open for 5% of the time, Pallas kernels for 0%

commit v1 on v0

v1 whole, which is shorter than its diff:
```python
import math

import jax
import jax.numpy as jnp
from jax import lax
from jax.experimental import pallas as pl
from jax.experimental.pallas import tpu as pltpu
from jax.sharding import PartitionSpec as P

WIN = 512
BG = 1024
BL = 128
HEADS = 16
SIZE = 64
PAIRS = HEADS // 2
CPAD = 128
LOG2E = math.log2(math.e)
NEG = -1e30
BF = jnp.bfloat16
F32 = jnp.float32

VM = pl.BlockSpec(memory_space=pltpu.VMEM)
SM = pl.BlockSpec(memory_space=pltpu.SMEM)
ANY = pl.BlockSpec(memory_space=pl.ANY)


def dot(a, b):
    return jnp.dot(a, b, preferred_element_type=F32)


def dot_t(a, b):
    return lax.dot_general(a, b, (((1,), (1,)), ((), ())), preferred_element_type=F32)


def low_half(shape):
    return lax.broadcasted_iota(jnp.int32, shape, len(shape) - 1) < SIZE


def params(mib):
    return pltpu.CompilerParams(vmem_limit_bytes=mib * 2**20)


def fetch(source, rows, buffers, sems):
    copies = [
        pltpu.make_async_copy(source.at[row], buf, sems.at[at])
        for row, buf, at in zip(rows, buffers, range(len(rows)))
    ]
    for copy in copies:
        copy.start()
    return copies


def fold_kernel(win, enc_w, lat, scale, qt, av, w0, w1, w2, sems):
    got = fetch(enc_w, (1, 0, 2), (w1, w0, w2), sems)
    got[0].wait()
    ak = dot(win[...], w1[...]).astype(BF)
    got[1].wait()
    q = (dot(lat[...], w0[...]) * scale[0:1, :]).astype(BF)
    low = low_half((1, 128))
    for pair in range(PAIRS):
        at = slice(pair * 128, pair * 128 + 128)
        keys = ak[:, at]
        both = q[:, at]
        zero = jnp.zeros_like(both)
        qt[2 * pair] = dot_t(jnp.where(low, both, zero), keys).astype(BF)
        qt[2 * pair + 1] = dot_t(jnp.where(low, zero, both), keys).astype(BF)
    got[2].wait()
    av[...] = dot(win[...], w2[...]).astype(BF)


def encode_kernel(
    idx, left, own, right, qt, bias, av, lat, enc_w, latent, normed, grid, ge, z, w3, sems
):
    got = fetch(enc_w, (3,), (w3,), sems)
    rows = lat.shape[0]
    at = 0
    for piece in (left, own, right):
        for begin in range(0, piece.shape[1], 512):
            grid[at : at + 512, :] = piece[:, begin : begin + 512].astype(F32).T
            at += 512
    row = lax.broadcasted_iota(jnp.int32, (256, 256), 0)
    col = lax.broadcasted_iota(jnp.int32, (256, 256), 1)
    diag = jnp.where(row % 16 == col % 16, 0.0, NEG)

    def group(number, carry):
        base = number * 16
        for slot in range(16):
            for node in range(16):
                edge = slot * 16 + node
                ge[pl.ds(edge, 1), :] = grid[pl.ds(idx[base + (slot * rows + node)], 1), :]
        points = ge[...].astype(BF)
        base = pl.multiple_of(base, 16)
        queries = qt[:, pl.ds(base, 16), :].reshape(256, CPAD)
        score = dot_t(queries, points) + (diag + bias[pl.ds(number, 1), :])
        expo = jnp.exp2(score - jnp.max(score, axis=1, keepdims=True)).astype(BF)
        mixed = dot(expo, points)
        mixed = mixed / mixed[:, 100:101]
        z[:, pl.ds(base, 16), :] = mixed.reshape(16, 16, CPAD).astype(BF)
        return carry

    lax.fori_loop(0, rows // 16, group, 0)
    low = low_half((1, 128))
    parts = []
    for pair in range(PAIRS):
        values = av[:, pair * 128 : pair * 128 + 128]
        zero = jnp.zeros_like(values)
        parts.append(
            dot(z[2 * pair], jnp.where(low, values, zero))
            + dot(z[2 * pair + 1], jnp.where(low, zero, values))
        )
    encoded = jnp.concatenate(parts, axis=1).astype(BF)
    got[0].wait()
    rounded = (lat[...].astype(F32) + dot(encoded, w3[...])).astype(BF)
    latent[...] = rounded
    wide = rounded.astype(F32)
    center = wide - jnp.mean(wide, axis=1, keepdims=True)
    spread = jnp.mean(center * center, axis=1, keepdims=True)
    normed[...] = (center * lax.rsqrt(spread + 1e-05)).astype(BF)


def project_kernel(
    normed, win, wout, scale, proc_w, dec_w, q, k, v, aq, bo, co, b0, b1, b2, b3, b4, sems
):
    got = fetch(proc_w, (0, 1, 2), (b0, b1, b2), sems)
    more = fetch(dec_w, (0, 3), (b3, b4), sems.at[pl.ds(3, 2)])
    rows = normed[...]
    got[0].wait()
    q[...] = (dot(rows, b0[...]) * scale[1:2, :]).astype(BF)
    got[1].wait()
    k[...] = dot(rows, b1[...]).astype(BF)
    got[2].wait()
    v[...] = dot(rows, b2[...]).astype(BF)
    co[...] = dot_t(win[...], wout[...]).astype(BF)
    more[0].wait()
    aq[...] = (dot(win[...], b3[...]) * scale[2:3, :]).astype(BF)
    more[1].wait()
    bo[...] = dot_t(b4[...], wout[...]).astype(BF)


def window_kernel(
    ends, q, k, v, nl, nr, latent, proc_w, out, keys, values, bias, mixed, wk, wv, wo, sems
):
    got = fetch(proc_w, (1, 2, 3), (wk, wv, wo), sems)
    rows = q.shape[0]
    half = rows // 2
    span = half + WIN
    keys[rows : 2 * rows, :] = k[...]
    values[rows : 2 * rows, :] = v[...]
    row = lax.broadcasted_iota(jnp.int32, (half, span), 0)
    col = lax.broadcasted_iota(jnp.int32, (half, span), 1)
    for side in range(2):
        place = col + side * half
        inside = (col >= row) & (col - row <= WIN) & (place >= ends[0]) & (place < ends[1])
        bias[side] = jnp.where(inside, 0.0, NEG)
    got[0].wait()
    keys[:rows, :] = dot(nl[...], wk[...]).astype(BF)
    keys[2 * rows :, :] = dot(nr[...], wk[...]).astype(BF)
    got[1].wait()
    values[:rows, :] = dot(nl[...], wv[...]).astype(BF)
    values[2 * rows :, :] = dot(nr[...], wv[...]).astype(BF)
    low = low_half((1, 128))

    def one_pair(pair, carry):
        lanes = pl.ds(pl.multiple_of(pair * 128, 128), 128)
        for side in range(2):
            these = slice(side * half, side * half + half)
            near = slice(side * half, side * half + span)
            both = q[these, lanes]
            near_keys = keys[near, lanes]
            near_values = values[near, lanes]
            parts = []
            for keep in (low, ~low):
                score = dot_t(jnp.where(keep, both, jnp.zeros_like(both)), near_keys) + bias[side]
                expo = jnp.exp2(score - jnp.max(score, axis=1, keepdims=True)).astype(BF)
                total = dot(expo, jnp.where(keep, near_values, jnp.ones_like(near_values)))
                parts.append(total / pltpu.roll(total, SIZE, 1))
            mixed[these, lanes] = jnp.where(low, parts[0], parts[1]).astype(BF)
        return carry

    lax.fori_loop(0, PAIRS, one_pair, 0)
    got[2].wait()
    out[...] = (latent[...].astype(F32) + dot(mixed[...], wo[...])).astype(BF)


CHUNK = 128


def decode_kernel(
    idx, left, own, right, grid, aq, bo, co, dec_w, out, kf, vf, qb, prod, wts, dec, wk, wv, sems
):
    got = fetch(dec_w, (1, 2), (wk, wv), sems)
    points = grid.shape[1]
    for copy, weight, tiles in ((got[0], wk, kf), (got[1], wv, vf)):
        copy.wait()
        begin = 0
        for piece in (left, own, right):
            count = piece.shape[0]
            for block in range(8):
                tiles[pl.ds(begin * 8 + block, count, stride=8), :] = dot(
                    piece[...], weight[:, block * 128 : block * 128 + 128]
                )
            begin += count
    same = (lax.broadcasted_iota(jnp.int32, (128, 128), 0) < SIZE) == (
        lax.broadcasted_iota(jnp.int32, (128, 128), 1) < SIZE
    )
    ones = jnp.where(same, 1.0, 0.0).astype(BF)
    unroll = 8

    def one_chunk(number, carry):
        first = pl.multiple_of(number * CHUNK, CHUNK)
        state = grid[:, pl.ds(first, CHUNK)].astype(F32).T.astype(BF)
        for block in range(8):
            qb[pl.ds(block, CHUNK, stride=8), :] = dot(state, aq[:, block * 128 : block * 128 + 128])

        def products(step, carry):
            for at in range(0, unroll, 2):
                begin = pl.multiple_of((step * unroll + at) * 8, 16)
                query = qb[pl.ds(begin, 16), :]
                for edge in range(3):
                    where = edge * points + first + step * unroll + at
                    one = kf[pl.ds(pl.multiple_of(idx[where], 8), 8), :]
                    two = kf[pl.ds(pl.multiple_of(idx[where + 1], 8), 8), :]
                    prod[edge, pl.ds(begin, 16), :] = (
                        query * jnp.concatenate([one, two], axis=0)
                    ).astype(BF)
            return carry

        lax.fori_loop(0, CHUNK // unroll, products, 0)
        scores = [dot(prod[edge], ones) for edge in range(3)]
        highest = jnp.maximum(jnp.maximum(scores[0], scores[1]), scores[2])
        expo = [jnp.exp2(score - highest) for score in scores]
        inverse = 1.0 / (expo[0] + expo[1] + expo[2])
        for edge in range(3):
            wts[edge] = expo[edge] * inverse

        def mixtures(step, carry):
            for at in range(unroll):
                begin = pl.multiple_of((step * unroll + at) * 8, 8)
                where = first + step * unroll + at
                total = None
                for edge in range(3):
                    source = pl.multiple_of(idx[edge * points + where], 8)
                    term = wts[edge, pl.ds(begin, 8), :] * vf[pl.ds(source, 8), :]
                    total = term if total is None else total + term
                dec[pl.ds(begin, 8), :] = total
            return carry

        lax.fori_loop(0, CHUNK // unroll, mixtures, 0)
        result = dot(state, co[...])
        for block in range(8):
            result += dot(
                dec[pl.ds(block, CHUNK, stride=8), :].astype(BF),
                bo[block * 128 : block * 128 + 128, :],
            )
        out[:, pl.ds(first, CHUNK)] = result.T[: out.shape[0], :].astype(BF)
        return carry

    lax.fori_loop(0, points // CHUNK, one_chunk, 0)


def shape(dims, kind=BF):
    return jax.ShapeDtypeStruct(dims, kind)


def neighbours(head, tail):
    axes = ("wide", "narrow")
    count = lax.axis_size(axes)
    after = lax.ppermute(tail, axes, [(i, i + 1) for i in range(count - 1)])
    before = lax.ppermute(head, axes, [(i + 1, i) for i in range(count - 1)])
    return after, before


def on_device(
    grid_state,
    latent_init,
    enc_src,
    enc_count,
    dec_src,
    w_in,
    enc_w,
    proc_w,
    dec_w,
    w_out,
    logit_scale,
):
    points, channels = grid_state.shape
    rows, width = latent_init.shape
    slots = enc_src.shape[1]
    place = lax.axis_index(("wide", "narrow"))
    total = rows * lax.axis_size(("wide", "narrow"))
    weight = pltpu.VMEM((width, width), BF)
    dma = pltpu.SemaphoreType.DMA

    grid = jnp.concatenate(
        [
            grid_state.T,
            jnp.ones((1, points), BF),
            jnp.zeros((CPAD - channels - 1, points), BF),
        ],
        axis=0,
    )
    grid_left, grid_right = neighbours(grid[:, :BG], grid[:, points - BG :])
    win = jnp.pad(w_in, ((0, CPAD - channels), (0, 0)))
    wout = jnp.pad(w_out.T, ((0, CPAD - channels), (0, 0)))
    scale = jnp.repeat(logit_scale * (LOG2E / math.sqrt(SIZE)), SIZE, axis=1)
    enc_idx = jnp.clip(enc_src.T, 0, points + 2 * BG - 1).reshape(-1)
    live = jnp.arange(slots, dtype=jnp.int32)[:, None] < enc_count[None, :]
    bias = jnp.where(live, 0.0, NEG).astype(F32)
    bias = bias.reshape(slots, rows // 16, 16).transpose(1, 0, 2).reshape(rows // 16, slots * 16)
    dec_idx = jnp.clip(dec_src.T - (place * rows - BL), 0, rows + 2 * BL - 1).reshape(-1) * 8
    ends = jnp.stack([WIN // 2 - place * rows, total + WIN // 2 - place * rows])

    qt, av = pl.pallas_call(
        fold_kernel,
        out_shape=(shape((HEADS, rows, CPAD)), shape((CPAD, width))),
        in_specs=[VM, ANY, VM, VM],
        out_specs=(VM, VM),
        scratch_shapes=[weight] * 3 + [dma((3,))],
        compiler_params=params(24),
        cost_estimate=pl.CostEstimate(flops=2 * 10**9, bytes_accessed=8 * 2**20, transcendentals=0),
        name="fold",
    )(win, enc_w, latent_init, scale)
    latent, normed = pl.pallas_call(
        encode_kernel,
        out_shape=(shape((rows, width)), shape((rows, width))),
        in_specs=[SM] + [VM] * 7 + [ANY],
        out_specs=(VM, VM),
        scratch_shapes=[
            pltpu.VMEM((points + 2 * BG, CPAD), F32),
            pltpu.VMEM((slots * 16, CPAD), F32),
            pltpu.VMEM((HEADS, rows, CPAD), BF),
            weight,
            dma((1,)),
        ],
        compiler_params=params(24),
        name="encode",
    )(enc_idx, grid_left, grid, grid_right, qt, bias, av, latent_init, enc_w)
    near_left, near_right = neighbours(normed, normed)
    q, k, v, aq, bo, co = pl.pallas_call(
        project_kernel,
        out_shape=(shape((rows, width)),) * 3
        + (shape((CPAD, width)), shape((width, CPAD)), shape((CPAD, CPAD))),
        in_specs=[VM] * 4 + [ANY] * 2,
        out_specs=(VM,) * 6,
        scratch_shapes=[weight] * 5 + [dma((5,))],
        compiler_params=params(24),
        cost_estimate=pl.CostEstimate(flops=3 * 10**9, bytes_accessed=12 * 2**20, transcendentals=0),
        name="project",
    )(normed, win, wout, scale, proc_w, dec_w)
    latent_out = pl.pallas_call(
        window_kernel,
        out_shape=shape((rows, width)),
        in_specs=[SM] + [VM] * 6 + [ANY],
        out_specs=VM,
        scratch_shapes=[
            pltpu.VMEM((rows + WIN, width), BF),
            pltpu.VMEM((rows + WIN, width), BF),
            pltpu.VMEM((2, rows // 2, rows // 2 + WIN), F32),
            pltpu.VMEM((rows, width), BF),
        ]
        + [weight] * 3
        + [dma((3,))],
        compiler_params=params(32),
        name="window",
    )(ends, q, k, v, near_left, near_right, latent, proc_w)
    mesh_left, mesh_right = neighbours(latent_out[:BL], latent_out[rows - BL :])
    nodes = rows + 2 * BL
    out = pl.pallas_call(
        decode_kernel,
        out_shape=shape((channels, points)),
        in_specs=[SM] + [VM] * 7 + [ANY],
        out_specs=VM,
        scratch_shapes=[
            pltpu.VMEM((nodes * 8, 128), F32),
            pltpu.VMEM((nodes * 8, 128), F32),
            pltpu.VMEM((CHUNK * 8, 128), F32),
            pltpu.VMEM((3, CHUNK * 8, 128), BF),
            pltpu.VMEM((3, CHUNK * 8, 128), F32),
            pltpu.VMEM((CHUNK * 8, 128), F32),
        ]
        + [weight] * 2
        + [dma((2,))],
        compiler_params=params(32),
        name="decode",
    )(dec_idx, mesh_left, latent_out, mesh_right, grid, aq, bo, co, dec_w)
    return out.T


def solution(mesh):
    both = ("wide", "narrow")
    placed = (
        P(both, None),
        P(both, None),
        P(both, None),
        P(both),
        P(both, None),
        P(),
        P(),
        P(),
        P(),
        P(),
        P(),
    )
    return jax.shard_map(
        on_device,
        mesh=mesh,
        in_specs=placed,
        out_specs=P(both, None),
        check_vma=False,
    )
```

time: 552 us -> 150 us (0.27); the launches traced: 542 us -> 148 us
  local copies, waits for them, and re-layouts: 273 us -> 30.3 us
  other arithmetic: 126 us -> 2.79 us
  Pallas kernels: 0 us -> 80.9 us
  matrix products: 54.7 us -> 0 us
  waiting for transfers between devices: 47 us -> 3.63 us
  loops' own time: 11.1 us -> 0 us
    gather x4 -> x0, local copies, waits for them, and re-layouts: 157 us -> none  [the longest x2 94.3 us: on_device(): jnp.take(mesh_wide, mesh_source, axis=0)]
    pallas_call x0 -> x5, Pallas kernels: none -> 80.9 us  [the longest x1 44 us: on_device(): pl.pallas_call(decode_kernel, out_shape=shape((channels, points)), in_spe...]
    dot_general x17 -> x0, matrix products: 54.7 us -> none  [the longest x9 45.5 us: project(): return jnp.dot(rows, weight, preferred_element_type=jnp.float32)]
    reduce_sum x7 -> x0, other arithmetic: 47.5 us -> none  [the longest x2 32.7 us: edge_attend(): return jnp.sum(spread_weights * values.astype(jnp.float32), axis=1)]
    ppermute x6, waiting for transfers between devices: 47 us -> 3.63 us  [the longest x3 1.87 us: neighbours(): after = lax.ppermute(tail, axes, [(i, i + 1) for i in range(count - 1)])]
    reshape x3 -> x1, local copies, waits for them, and re-layouts: 36.8 us -> 0.09 us  [on_device(): scale = jnp.repeat(logit_scale * (LOG2E / math.sqrt(SIZE)), SIZE, axis=1)]
    mul x1, local copies, waits for them, and re-layouts: 34.3 us -> 0.02 us  [on_device(): jnp.clip(dec_src.T - (place * rows - BL), 0, rows + 2 * BL - 1).reshape(-1)]
    select_n x4 -> x1, other arithmetic: 31.5 us -> 0.01 us  [on_device(): bias = jnp.where(live, 0.0, NEG).astype(F32)]
  transfers between devices with their start and end apart: 6 -> 6, of which waited for: 4 -> 2; matrix products, arithmetic and copies ran while one was open for 5% -> 3% of each run, Pallas kernels for 0% -> 4%
where the time goes in v1:
time: 150 us; the launch traced here: 148 us
  Pallas kernels  80.9 us (54%)
  local copies, waits for them, and re-layouts  30.3 us (20%)
  starting transfers between devices  29.5 us (20%)
  waiting for transfers between devices  3.63 us (2%)
  other arithmetic  2.79 us (2%)
    pallas_call x1, Pallas kernels, on_device(): pl.pallas_call(decode_kernel, out_shape=shape((channels, points)), in_spe...  44 us
    unnamed x37, local copies, waits for them, and re-layouts  27 us
    ppermute x3, starting transfers between devices, neighbours(): before = lax.ppermute(head, axes, [(i + 1, i) for i in range(count - 1)])  23.8 us
    pallas_call x1, Pallas kernels, on_device(): pl.pallas_call(window_kernel, out_shape=shape((rows, width)), in_specs=[S...  16.1 us
    pallas_call x1, Pallas kernels, on_device(): pl.pallas_call(encode_kernel, out_shape=(shape((rows, width)), shape((row...  14.3 us
    ppermute x3, starting transfers between devices, neighbours(): after = lax.ppermute(tail, axes, [(i, i + 1) for i in range(count - 1)])  5.75 us
    pallas_call x1, Pallas kernels, on_device(): pl.pallas_call(project_kernel, out_shape=(shape((rows, width)),) * 3 + (s...  4.28 us
  transfers between devices with their start and end apart: 6, of which 2 were waited for; matrix products, arithmetic and copies ran while one was open for 3% of the time, Pallas kernels for 4%

profile of v1, /device:TPU:96, one launch (start us, length us, event | category | flops | bytes accessed | tf_op | source)
XLA Modules:
  0.0 147.6 jit_solution(11884510351911544023)
XLA Ops:
  0.0 0.1 pad.11.clone
  0.1 0.1 pad.10.clone
  0.2 1.3 maximum_maximum_fusion.own.grid
  1.4 0.7 fusion.1
  2.2 1.9 %collective-permute-start = (bf16[128,1024]{1,0:T(8,128)(2,1)}, bf16[128,1024]{1,0:T(8,128)(2,1)S(1)}, u32[]{:S(2)}, u32[]{:S(2)}) collective-permute-start(bf16[128,1024]{1,0:T(8,128)(2,1)} %get-tuple-element.28), channel_id=1, source_target_pairs={{0,1},{1,2},{2,3},{3,4},{4,5},{5,6},{6,7},{7,8},{8,9},{9,10},{10,1... | collective-permute-start | bytes 786440 | tf_op jit(solution)/shard_map/ppermute | solution.py:268
  4.1 7.9 %collective-permute-start.1 = (bf16[128,1024]{1,0:T(8,128)(2,1)S(1)}, bf16[128,1024]{1,0:T(8,128)(2,1)S(1)}, u32[]{:S(2)}, u32[]{:S(2)}) collective-permute-start(bf16[128,1024]{1,0:T(8,128)(2,1)S(1)} %get-tuple-element.27), channel_id=1, source_target_pairs={{1,0},{2,1},{3,2},{4,3},{5,4},{6,5},{7,6},{8,7},{9,8},{10,9},{11,1... | collective-permute-start | bytes 786440 | tf_op jit(solution)/shard_map/ppermute | solution.py:269
  12.0 1.0 pad.7.win
  12.9 0.7 broadcast_multiply_fusion
  13.6 0.1 broadcast_in_dim.21
  13.7 0.1 reshape.23.scale
  13.8 0.7 clamp_bitcast_fusion
  14.5 3.4 %copy-done.4 = bf16[4,1024,1024]{2,1,0:T(8,128)(2,1)S(1)} copy-done((bf16[4,1024,1024]{2,1,0:T(8,128)(2,1)S(1)}, bf16[4,1024,1024]{2,1,0:T(8,128)(2,1)}, u32[]{:S(2)}) %copy-start.4) | copy-done | bytes 8388632
  17.9 1.0 copy-done.6
  18.9 2.3 %fold.1 = (bf16[16,256,128]{2,1,0:T(8,128)(2,1)S(1)}, bf16[128,1024]{1,0:T(8,128)(2,1)S(1)}) custom-call(bf16[128,1024]{1,0:T(8,128)(2,1)S(1)} %pad.7.win, bf16[4,1024,1024]{2,1,0:T(8,128)(2,1)S(1)} %copy-done.4, bf16[256,1024]{1,0:T(8,128)(2,1)S(1)} %copy-done.6, f32[3,1024]{1,0:T(4,128)S(1)} %reshape.23.scale), custom_call_target="tpu_custom_call" | custom-call | flops 2000000000 | bytes 8388608 | tf_op jit(solution)/shard_map/fold/pallas_call | solution.py:313
  21.3 0.0 copy-start.14
  21.3 0.7 copy-done.14
  22.0 0.1 lt.27
  22.1 0.1 lt.29
  22.2 0.1 lt.25
  22.3 0.0 collective-permute-done.left
  22.3 0.0 copy-start.10
  22.3 0.7 copy-done.10
  23.0 0.0 collective-permute-done.1.right
  23.0 0.7 copy-done.12
  23.7 3.4 %copy-done.5 = bf16[4,1024,1024]{2,1,0:T(8,128)(2,1)S(1)} copy-done((bf16[4,1024,1024]{2,1,0:T(8,128)(2,1)S(1)}, bf16[4,1024,1024]{2,1,0:T(8,128)(2,1)}, u32[]{:S(2)}) %copy-start.5) | copy-done | bytes 8388632
  27.1 0.9 copy-done.11
  28.1 0.9 copy-done.13
  29.0 0.9 copy-done.15
  30.0 14.3 %encode.1 = (bf16[256,1024]{1,0:T(8,128)(2,1)S(1)}, bf16[256,1024]{1,0:T(8,128)(2,1)S(1)}) custom-call(s32[4096]{0:T(1024)S(1)} %bitcast.12, bf16[128,1024]{1,0:T(8,128)(2,1)S(1)} %copy-done.11, bf16[128,2048]{1,0:T(8,128)(2,1)S(1)} %maximum_maximum_fusion.own.grid, bf16[128,1024]{1,0:T(8,128)(2,1)S(1)} %copy-done.13, ...), custom_call_target="tpu_custom_call" | custom-call | tf_op jit(solution)/shard_map/encode/pallas_call | solution.py:323
  44.3 1.9 %collective-permute-start.2 = (bf16[256,1024]{1,0:T(8,128)(2,1)S(1)}, bf16[256,1024]{1,0:T(8,128)(2,1)S(1)}, u32[]{:S(2)}, u32[]{:S(2)}) collective-permute-start(bf16[256,1024]{1,0:T(8,128)(2,1)S(1)} %get-tuple-element.17.normed), channel_id=1, source_target_pairs={{0,1},{1,2},{2,3},{3,4},{4,5},{5,6},{6,7},{7,8},{8,9},{9,10},{10,1... | collective-permute-start | bytes 1572872 | tf_op jit(solution)/shard_map/ppermute | solution.py:268
  46.2 7.9 %collective-permute-start.3 = (bf16[256,1024]{1,0:T(8,128)(2,1)S(1)}, bf16[256,1024]{1,0:T(8,128)(2,1)S(1)}, u32[]{:S(2)}, u32[]{:S(2)}) collective-permute-start(bf16[256,1024]{1,0:T(8,128)(2,1)S(1)} %get-tuple-element.17.normed), channel_id=1, source_target_pairs={{1,0},{2,1},{3,2},{4,3},{5,4},{6,5},{7,6},{8,7},{9,8},{10,9},{11,1... | collective-permute-start | bytes 1572872 | tf_op jit(solution)/shard_map/ppermute | solution.py:269
  54.1 1.0 pad.8.wout
  55.0 0.1 pad_add_fusion.ends
  55.1 3.4 %copy-done = bf16[4,1024,1024]{2,1,0:T(8,128)(2,1)S(1)} copy-done((bf16[4,1024,1024]{2,1,0:T(8,128)(2,1)S(1)}, bf16[4,1024,1024]{2,1,0:T(8,128)(2,1)}, u32[]{:S(2)}) %copy-start) | copy-done | bytes 8388632
  58.5 3.4 %copy-done.2 = bf16[4,1024,1024]{2,1,0:T(8,128)(2,1)S(1)} copy-done((bf16[4,1024,1024]{2,1,0:T(8,128)(2,1)S(1)}, bf16[4,1024,1024]{2,1,0:T(8,128)(2,1)}, u32[]{:S(2)}) %copy-start.2) | copy-done | bytes 8388632
  61.9 4.3 %project.1 = (bf16[256,1024]{1,0:T(8,128)(2,1)S(1)}, bf16[256,1024]{1,0:T(8,128)(2,1)S(1)}, bf16[256,1024]{1,0:T(8,128)(2,1)S(1)}, bf16[128,1024]{1,0:T(8,128)(2...) custom-call(bf16[256,1024]{1,0:T(8,128)(2,1)S(1)} %get-tuple-element.17.normed, ...), custom_call_target="tpu_custom_call" | custom-call | flops 3000000000 | bytes 12582912 | tf_op jit(solution)/shard_map/project/pallas_call | solution.py:339
  66.2 0.0 copy-start.8
  66.2 0.7 copy-done.8
  66.9 0.0 collective-permute-done.2.nl
  66.9 0.0 collective-permute-done.3.nr
  66.9 3.4 %copy-done.1 = bf16[4,1024,1024]{2,1,0:T(8,128)(2,1)S(1)} copy-done((bf16[4,1024,1024]{2,1,0:T(8,128)(2,1)S(1)}, bf16[4,1024,1024]{2,1,0:T(8,128)(2,1)}, u32[]{:S(2)}) %copy-start.1) | copy-done | bytes 8388632
  70.3 16.1 %window.1.own = bf16[256,1024]{1,0:T(8,128)(2,1)S(1)} custom-call(s32[2]{0:T(128)S(1)} %pad_add_fusion.ends, bf16[256,1024]{1,0:T(8,128)(2,1)S(1)} %get-tuple-element.18.q, bf16[256,1024]{1,0:T(8,128)(2,1)S(1)} %get-tuple-element.19.k, bf16[256,1024]{1,0:T(8,128)(2,1)S(1)} %get-tuple-element.20.v, bf16[256,1024]{1,0:T(8,128)(2,1)S(1)} %collective-permute-done.2.nl, ...), custom_call_target="tpu_custom_call" | custom-call | tf_op jit(solution)/shard_map/window/pallas_call | solution.py:350
  86.4 1.9 %collective-permute-start.4 = (bf16[128,1024]{1,0:T(8,128)(2,1)S(1)}, bf16[128,1024]{1,0:T(8,128)(2,1)S(1)}, u32[]{:S(2)}, u32[]{:S(2)}) collective-permute-start(bf16[128,1024]{1,0:T(8,128)(2,1)S(1)} %get-tuple-element.26), channel_id=1, source_target_pairs={{0,1},{1,2},{2,3},{3,4},{4,5},{5,6},{6,7},{7,8},{8,9},{9,10},{10,1... | collective-permute-start | bytes 786440 | tf_op jit(solution)/shard_map/ppermute | solution.py:268
  88.3 8.0 %collective-permute-start.5 = (bf16[128,1024]{1,0:T(8,128)(2,1)S(1)}, bf16[128,1024]{1,0:T(8,128)(2,1)S(1)}, u32[]{:S(2)}, u32[]{:S(2)}) collective-permute-start(bf16[128,1024]{1,0:T(8,128)(2,1)S(1)} %get-tuple-element.25), channel_id=1, source_target_pairs={{1,0},{2,1},{3,2},{4,3},{5,4},{6,5},{7,6},{8,7},{9,8},{10,9},{11,1... | collective-permute-start | bytes 786440 | tf_op jit(solution)/shard_map/ppermute | solution.py:269
  96.4 1.9 %collective-permute-done.4.left = bf16[128,1024]{1,0:T(8,128)(2,1)S(1)} collective-permute-done((bf16[128,1024]{1,0:T(8,128)(2,1)S(1)}, bf16[128,1024]{1,0:T(8,128)(2,1)S(1)}, u32[]{:S(2)}, u32[]{:S(2)}) %collective-permute-start.4) | collective-permute-done | bytes 262176 | tf_op jit(solution)/shard_map/ppermute | solution.py:268
  98.3 1.8 %collective-permute-done.5.right = bf16[128,1024]{1,0:T(8,128)(2,1)S(1)} collective-permute-done((bf16[128,1024]{1,0:T(8,128)(2,1)S(1)}, bf16[128,1024]{1,0:T(8,128)(2,1)S(1)}, u32[]{:S(2)}, u32[]{:S(2)}) %collective-permute-start.5) | collective-permute-done | bytes 262176 | tf_op jit(solution)/shard_map/ppermute | solution.py:269
  100.1 3.4 %copy-done.3 = bf16[4,1024,1024]{2,1,0:T(8,128)(2,1)S(1)} copy-done((bf16[4,1024,1024]{2,1,0:T(8,128)(2,1)S(1)}, bf16[4,1024,1024]{2,1,0:T(8,128)(2,1)}, u32[]{:S(2)}) %copy-start.3) | copy-done | bytes 8388632
  103.4 44.0 %decode.1 = bf16[100,2048]{1,0:T(8,128)(2,1)} custom-call(s32[6144]{0:T(1024)S(1)} %mul.29.idx, bf16[128,1024]{1,0:T(8,128)(2,1)S(1)} %collective-permute-done.4.left, bf16[256,1024]{1,0:T(8,128)(2,1)S(1)} %window.1.own, bf16[128,1024]{1,0:T(8,128)(2,1)S(1)} %collective-permute-done.5.right, bf16[128,2048]{1,0:T(8,128)(2,1)S(1)} %maximum_maximum_fusion.own.grid, ...), custom_call_target="tpu_custom_call" | custom-call | tf_op jit(solution)/shard_map/decode/pallas_call | solution.py:368
  (27 shorter events, 0.1 us)
Async XLA Ops:
  0.0 23.7 %copy-start.7 = (bf16[256,1024]{1,0:T(8,128)(2,1)S(1)}, bf16[256,1024]{1,0:T(8,128)(2,1)}, u32[]{:S(2)}) copy-start(bf16[256,1024]{1,0:T(8,128)(2,1)} %lat.3) | copy-start | bytes 1572868
  0.0 22.0 %copy-start.17 = (s32[256]{0:T(256)S(1)}, s32[256]{0:T(256)}, u32[]{:S(2)}) copy-start(s32[256]{0:T(256)} %param.14) | copy-start | bytes 3076
  2.2 20.1 %collective-permute-start = (bf16[128,1024]{1,0:T(8,128)(2,1)}, bf16[128,1024]{1,0:T(8,128)(2,1)S(1)}, u32[]{:S(2)}, u32[]{:S(2)}) collective-permute-start(bf16[128,1024]{1,0:T(8,128)(2,1)} %get-tuple-element.28), channel_id=1, source_target_pairs={{0,1},{1,2},{2,3},{3,4},{4,5},{5,6},{6,7},{7,8},{8,9},{9,10},{10,1... | collective-permute-start | bytes 786440 | tf_op jit(solution)/shard_map/ppermute | solution.py:268
  4.1 18.9 %collective-permute-start.1 = (bf16[128,1024]{1,0:T(8,128)(2,1)S(1)}, bf16[128,1024]{1,0:T(8,128)(2,1)S(1)}, u32[]{:S(2)}, u32[]{:S(2)}) collective-permute-start(bf16[128,1024]{1,0:T(8,128)(2,1)S(1)} %get-tuple-element.27), channel_id=1, source_target_pairs={{1,0},{2,1},{3,2},{4,3},{5,4},{6,5},{7,6},{8,7},{9,8},{10,9},{11,1... | collective-permute-start | bytes 786440 | tf_op jit(solution)/shard_map/ppermute | solution.py:269
  14.5 3.4 %copy-start.4 = (bf16[4,1024,1024]{2,1,0:T(8,128)(2,1)S(1)}, bf16[4,1024,1024]{2,1,0:T(8,128)(2,1)}, u32[]{:S(2)}) copy-start(bf16[4,1024,1024]{2,1,0:T(8,128)(2,1)} %enc_w.3) | copy-start | bytes 25165828
  17.9 1.0 copy-start.6
  21.3 0.7 copy-start.14
  22.3 0.7 copy-start.10
  23.0 0.7 copy-start.12
  23.7 3.4 %copy-start.5 = (bf16[4,1024,1024]{2,1,0:T(8,128)(2,1)S(1)}, bf16[4,1024,1024]{2,1,0:T(8,128)(2,1)}, u32[]{:S(2)}) copy-start(bf16[4,1024,1024]{2,1,0:T(8,128)(2,1)} %enc_w.3) | copy-start | bytes 25165828
  27.1 0.9 copy-start.11
  28.1 0.9 copy-start.13
  29.0 0.9 copy-start.15
  44.3 22.6 %collective-permute-start.2 = (bf16[256,1024]{1,0:T(8,128)(2,1)S(1)}, bf16[256,1024]{1,0:T(8,128)(2,1)S(1)}, u32[]{:S(2)}, u32[]{:S(2)}) collective-permute-start(bf16[256,1024]{1,0:T(8,128)(2,1)S(1)} %get-tuple-element.17.normed), channel_id=1, source_target_pairs={{0,1},{1,2},{2,3},{3,4},{4,5},{5,6},{6,7},{7,8},{8,9},{9,10},{10,1... | collective-permute-start | bytes 1572872 | tf_op jit(solution)/shard_map/ppermute | solution.py:268
  46.2 20.7 %collective-permute-start.3 = (bf16[256,1024]{1,0:T(8,128)(2,1)S(1)}, bf16[256,1024]{1,0:T(8,128)(2,1)S(1)}, u32[]{:S(2)}, u32[]{:S(2)}) collective-permute-start(bf16[256,1024]{1,0:T(8,128)(2,1)S(1)} %get-tuple-element.17.normed), channel_id=1, source_target_pairs={{1,0},{2,1},{3,2},{4,3},{5,4},{6,5},{7,6},{8,7},{9,8},{10,9},{11,1... | collective-permute-start | bytes 1572872 | tf_op jit(solution)/shard_map/ppermute | solution.py:269
  55.1 3.4 %copy-start = (bf16[4,1024,1024]{2,1,0:T(8,128)(2,1)S(1)}, bf16[4,1024,1024]{2,1,0:T(8,128)(2,1)}, u32[]{:S(2)}) copy-start(bf16[4,1024,1024]{2,1,0:T(8,128)(2,1)} %proc_w.3) | copy-start | bytes 25165828
  58.5 3.4 %copy-start.2 = (bf16[4,1024,1024]{2,1,0:T(8,128)(2,1)S(1)}, bf16[4,1024,1024]{2,1,0:T(8,128)(2,1)}, u32[]{:S(2)}) copy-start(bf16[4,1024,1024]{2,1,0:T(8,128)(2,1)} %dec_w.3) | copy-start | bytes 25165828
  61.9 34.5 %copy-start.16 = (s32[2048,3]{0,1:T(4,128)S(1)}, s32[2048,3]{0,1:T(4,128)}, u32[]{:S(2)}) copy-start(s32[2048,3]{0,1:T(4,128)} %param.15) | copy-start | bytes 73732
  66.2 0.7 copy-start.8
  66.9 3.4 %copy-start.1 = (bf16[4,1024,1024]{2,1,0:T(8,128)(2,1)S(1)}, bf16[4,1024,1024]{2,1,0:T(8,128)(2,1)}, u32[]{:S(2)}) copy-start(bf16[4,1024,1024]{2,1,0:T(8,128)(2,1)} %proc_w.3) | copy-start | bytes 25165828
  70.3 29.8 %copy-start.9 = (bf16[1024,128]{1,0:T(8,128)(2,1)S(1)}, bf16[1024,128]{1,0:T(8,128)(2,1)}, u32[]{:S(2)}) copy-start(bf16[1024,128]{1,0:T(8,128)(2,1)} %copy-done.8) | copy-start | bytes 786436
  86.4 11.9 %collective-permute-start.4 = (bf16[128,1024]{1,0:T(8,128)(2,1)S(1)}, bf16[128,1024]{1,0:T(8,128)(2,1)S(1)}, u32[]{:S(2)}, u32[]{:S(2)}) collective-permute-start(bf16[128,1024]{1,0:T(8,128)(2,1)S(1)} %get-tuple-element.26), channel_id=1, source_target_pairs={{0,1},{1,2},{2,3},{3,4},{4,5},{5,6},{6,7},{7,8},{8,9},{9,10},{10,1... | collective-permute-start | bytes 786440 | tf_op jit(solution)/shard_map/ppermute | solution.py:268
  88.3 11.7 %collective-permute-start.5 = (bf16[128,1024]{1,0:T(8,128)(2,1)S(1)}, bf16[128,1024]{1,0:T(8,128)(2,1)S(1)}, u32[]{:S(2)}, u32[]{:S(2)}) collective-permute-start(bf16[128,1024]{1,0:T(8,128)(2,1)S(1)} %get-tuple-element.25), channel_id=1, source_target_pairs={{1,0},{2,1},{3,2},{4,3},{5,4},{6,5},{7,6},{8,7},{9,8},{10,9},{11,1... | collective-permute-start | bytes 786440 | tf_op jit(solution)/shard_map/ppermute | solution.py:269
  100.1 3.4 %copy-start.3 = (bf16[4,1024,1024]{2,1,0:T(8,128)(2,1)S(1)}, bf16[4,1024,1024]{2,1,0:T(8,128)(2,1)}, u32[]{:S(2)}) copy-start(bf16[4,1024,1024]{2,1,0:T(8,128)(2,1)} %dec_w.3) | copy-start | bytes 25165828

commit v2 on v1

v2 whole, which is shorter than its diff:
```python
import math

import jax
import jax.numpy as jnp
from jax import lax
from jax.experimental import pallas as pl
from jax.experimental.pallas import tpu as pltpu
from jax.sharding import PartitionSpec as P

WIN = 512
BG = 1024
BL = 128
HEADS = 16
SIZE = 64
PAIRS = HEADS // 2
CPAD = 128
LOG2E = math.log2(math.e)
NEG = -1e30
BF = jnp.bfloat16
F32 = jnp.float32

VM = pl.BlockSpec(memory_space=pltpu.VMEM)
SM = pl.BlockSpec(memory_space=pltpu.SMEM)
HBM = pl.BlockSpec(memory_space=pltpu.HBM)


def dot(a, b):
    return jnp.dot(a, b, preferred_element_type=F32)


def dot_t(a, b):
    return lax.dot_general(a, b, (((1,), (1,)), ((), ())), preferred_element_type=F32)


def low_half(shape):
    return lax.broadcasted_iota(jnp.int32, shape, len(shape) - 1) < SIZE


def params(mib):
    return pltpu.CompilerParams(vmem_limit_bytes=mib * 2**20)


def fetch(source, rows, buffers, sems):
    copies = [
        pltpu.make_async_copy(source.at[row], buf, sems.at[at])
        for row, buf, at in zip(rows, buffers, range(len(rows)))
    ]
    for copy in copies:
        copy.start()
    return copies


def fold_kernel(win, enc_w, lat, scale, qt, av, w0, w1, w2, sems):
    got = fetch(enc_w, (1, 0, 2), (w1, w0, w2), sems)
    got[0].wait()
    ak = dot(win[...], w1[...]).astype(BF)
    got[1].wait()
    q = (dot(lat[...], w0[...]) * scale[0:1, :]).astype(BF)
    low = low_half((1, 128))
    for pair in range(PAIRS):
        at = slice(pair * 128, pair * 128 + 128)
        keys = ak[:, at]
        both = q[:, at]
        zero = jnp.zeros_like(both)
        qt[2 * pair] = dot_t(jnp.where(low, both, zero), keys).astype(BF)
        qt[2 * pair + 1] = dot_t(jnp.where(low, zero, both), keys).astype(BF)
    got[2].wait()
    av[...] = dot(win[...], w2[...]).astype(BF)


def encode_kernel(
    idx, left, own, right, qt, bias, av, lat, enc_w, proc_w, dec_w,
    latent, normed, pw0, pw1, pw2, pw3, dw0, dw1, dw2, dw3,
    grid, ge0, ge1, z, w3, sems,
):
    got = fetch(enc_w, (3,), (w3,), sems.at[pl.ds(0, 1)])
    later = fetch(proc_w, (0, 1, 2, 3), (pw0, pw1, pw2, pw3), sems.at[pl.ds(1, 4)])
    later += fetch(dec_w, (0, 3, 1, 2), (dw0, dw3, dw1, dw2), sems.at[pl.ds(5, 4)])
    rows = lat.shape[0]
    groups = rows // 16
    at = 0
    for piece in (left, own, right):
        for begin in range(0, piece.shape[1], 512):
            grid[at : at + 512, :] = piece[:, begin : begin + 512].astype(F32).T
            at += 512
    row = lax.broadcasted_iota(jnp.int32, (256, 256), 0)
    col = lax.broadcasted_iota(jnp.int32, (256, 256), 1)
    diag = jnp.where(row % 16 == col % 16, 0.0, NEG)

    def collect(number, ge):
        base = number * 16
        for slot in range(16):
            for node in range(16):
                edge = slot * 16 + node
                ge[pl.ds(edge, 1), :] = grid[pl.ds(idx[base + (slot * rows + node)], 1), :]

    def attend(number, ge):
        points = ge[...].astype(BF)
        base = pl.multiple_of(number * 16, 16)
        queries = qt[:, pl.ds(base, 16), :].reshape(256, CPAD)
        score = dot_t(queries, points) + (diag + bias[pl.ds(number, 1), :])
        expo = jnp.exp2(score - jnp.max(score, axis=1, keepdims=True)).astype(BF)
        mixed = dot(expo, points)
        mixed = mixed / mixed[:, 100:101]
        z[:, pl.ds(base, 16), :] = mixed.reshape(16, 16, CPAD).astype(BF)

    collect(0, ge0)

    def two_groups(step, carry):
        number = step * 2
        attend(number, ge0)
        collect(number + 1, ge1)
        attend(number + 1, ge1)
        collect(jnp.minimum(number + 2, groups - 1), ge0)
        return carry

    lax.fori_loop(0, groups // 2, two_groups, 0)
    low = low_half((1, 128))
    parts = []
    for pair in range(PAIRS):
        values = av[:, pair * 128 : pair * 128 + 128]
        zero = jnp.zeros_like(values)
        parts.append(
            dot(z[2 * pair], jnp.where(low, values, zero))
            + dot(z[2 * pair + 1], jnp.where(low, zero, values))
        )
    encoded = jnp.concatenate(parts, axis=1).astype(BF)
    got[0].wait()
    rounded = (lat[...].astype(F32) + dot(encoded, w3[...])).astype(BF)
    latent[...] = rounded
    wide = rounded.astype(F32)
    center = wide - jnp.mean(wide, axis=1, keepdims=True)
    spread = jnp.mean(center * center, axis=1, keepdims=True)
    normed[...] = (center * lax.rsqrt(spread + 1e-05)).astype(BF)
    for copy in later:
        copy.wait()


def project_kernel(normed, win, wout, scale, wq, wk, wv, dq, do, q, k, v, aq, bo, co):
    rows = normed[...]
    q[...] = (dot(rows, wq[...]) * scale[1:2, :]).astype(BF)
    k[...] = dot(rows, wk[...]).astype(BF)
    v[...] = dot(rows, wv[...]).astype(BF)
    co[...] = dot_t(wout[...], win[...]).astype(BF)
    aq[...] = (dot(win[...], dq[...]) * scale[2:3, :]).astype(BF)
    bo[...] = dot_t(do[...], wout[...]).astype(BF)


def window_kernel(
    ends, q, k, v, nl, nr, latent, wk, wv, wo, out, keys, values, bias, mixed
):
    rows = q.shape[0]
    half = rows // 2
    span = half + WIN
    keys[rows : 2 * rows, :] = k[...]
    values[rows : 2 * rows, :] = v[...]
    row = lax.broadcasted_iota(jnp.int32, (half, span), 0)
    col = lax.broadcasted_iota(jnp.int32, (half, span), 1)
    for side in range(2):
        place = col + side * half
        inside = (col >= row) & (col - row <= WIN) & (place >= ends[0]) & (place < ends[1])
        bias[side] = jnp.where(inside, 0.0, NEG)
    keys[:rows, :] = dot(nl[...], wk[...]).astype(BF)
    keys[2 * rows :, :] = dot(nr[...], wk[...]).astype(BF)
    values[:rows, :] = dot(nl[...], wv[...]).astype(BF)
    values[2 * rows :, :] = dot(nr[...], wv[...]).astype(BF)
    low = low_half((1, 128))

    def one_pair(pair, carry):
        lanes = pl.ds(pl.multiple_of(pair * 128, 128), 128)
        for side in range(2):
            these = slice(side * half, side * half + half)
            near = slice(side * half, side * half + span)
            both = q[these, lanes]
            zero = jnp.zeros_like(both)
            stacked = jnp.concatenate(
                [jnp.where(low, both, zero), jnp.where(low, zero, both)], axis=0
            )
            near_values = values[near, lanes]
            score = dot_t(stacked, keys[near, lanes]).reshape(2, half, span) + bias[side][None]
            score = score.reshape(2 * half, span)
            expo = jnp.exp2(score - jnp.max(score, axis=1, keepdims=True)).astype(BF)
            total = dot(
                expo, jnp.concatenate([near_values, jnp.ones_like(near_values)], axis=1)
            )
            part = total[:, :128] / total[:, 128:]
            mixed[these, lanes] = jnp.where(low, part[:half], part[half:]).astype(BF)
        return carry

    lax.fori_loop(0, PAIRS, one_pair, 0)
    out[...] = (latent[...].astype(F32) + dot(mixed[...], wo[...])).astype(BF)


CHUNK = 128


def to_tiles(rows, weight, tiles, begin):
    count = rows.shape[0]
    for block in range(8):
        tiles[pl.ds(begin * 8 + block, count, stride=8), :] = dot(
            rows, weight[:, block * 128 : block * 128 + 128]
        )


def prepare_kernel(own, state, aq, wk, wv, q, k, v):
    to_tiles(own[...], wk, k, 0)
    to_tiles(own[...], wv, v, 0)
    points = state.shape[1]
    for first in range(0, points, 512):
        to_tiles(state[:, first : first + 512].astype(F32).T.astype(BF), aq, q, first)


def decode_kernel(
    idx, left, right, ko, vo, q, grid, bo, co, wk, wv, out, kf, vf, prod, wts, dec
):
    points = grid.shape[1]
    side = left.shape[0]
    for weight, tiles, own in ((wk, kf, ko), (wv, vf, vo)):
        to_tiles(left[...], weight, tiles, 0)
        tiles[side * 8 : side * 8 + own.shape[0], :] = own[...]
        to_tiles(right[...], weight, tiles, side + own.shape[0] // 8)
    head_row = lax.broadcasted_iota(jnp.int32, (256, 256), 0) // SIZE
    head_col = lax.broadcasted_iota(jnp.int32, (256, 256), 1) // SIZE
    ones = jnp.where(head_row == head_col, 1.0, 0.0).astype(BF)
    sub = 128

    def one_chunk(number, carry):
        first = pl.multiple_of(number * CHUNK, CHUNK)

        def tile_of(tiles, edge, at):
            return tiles[pl.ds(pl.multiple_of(idx[edge * points + first + at], 8), 8), :]

        for quad in range(0, CHUNK, 4):
            mine = [
                q[pl.ds(pl.multiple_of((first + quad + at) * 8, 8), 8), :] for at in range(4)
            ]
            for edge in range(3):
                terms = [mine[at] * tile_of(kf, edge, quad + at) for at in range(4)]
                place = slice(quad * 4, quad * 4 + 16)
                prod[edge, place, 0:128] = jnp.concatenate([terms[0], terms[2]], axis=0).astype(BF)
                prod[edge, place, 128:256] = jnp.concatenate([terms[1], terms[3]], axis=0).astype(BF)
        for begin in range(0, CHUNK * 4, sub):
            score = dot(prod[:, begin : begin + sub, :].reshape(3 * sub, 256), ones)
            score = [score[edge * sub : edge * sub + sub] for edge in range(3)]
            highest = jnp.maximum(jnp.maximum(score[0], score[1]), score[2])
            expo = [jnp.exp2(part - highest) for part in score]
            inverse = 1.0 / (expo[0] + expo[1] + expo[2])
            for edge in range(3):
                wts[edge, begin : begin + sub, :] = expo[edge] * inverse
        for at in range(CHUNK):
            top = at // 4 * 16 + (at % 4) // 2 * 8
            lane = at % 2 * 128
            total = None
            for edge in range(3):
                term = wts[edge, top : top + 8, lane : lane + 128] * tile_of(vf, edge, at)
                total = term if total is None else total + term
            dec[pl.ds(pl.multiple_of((first + at) * 8, 8), 8), :] = total
        return carry

    lax.fori_loop(0, points // CHUNK, one_chunk, 0)
    block = 256
    for first in range(0, points, block):
        wide = jnp.concatenate(
            [dec[pl.ds(first * 8 + part, block, stride=8), :] for part in range(8)], axis=1
        ).astype(BF)
        result = dot(wide, bo[...]).T + dot(co[...], grid[:, first : first + block])
        out[:, first : first + block] = result[: out.shape[0], :].astype(BF)


def shape(dims, kind=BF):
    return jax.ShapeDtypeStruct(dims, kind)


def neighbours(head, tail):
    axes = ("wide", "narrow")
    count = lax.axis_size(axes)
    after = lax.ppermute(tail, axes, [(i, i + 1) for i in range(count - 1)])
    before = lax.ppermute(head, axes, [(i + 1, i) for i in range(count - 1)])
    return after, before


def on_device(
    grid_state,
    latent_init,
    enc_src,
    enc_count,
    dec_src,
    w_in,
    enc_w,
    proc_w,
    dec_w,
    w_out,
    logit_scale,
):
    points, channels = grid_state.shape
    rows, width = latent_init.shape
    slots = enc_src.shape[1]
    place = lax.axis_index(("wide", "narrow"))
    total = rows * lax.axis_size(("wide", "narrow"))
    weight = pltpu.VMEM((width, width), BF)
    dma = pltpu.SemaphoreType.DMA

    grid = jnp.concatenate(
        [
            grid_state.T,
            jnp.ones((1, points), BF),
            jnp.zeros((CPAD - channels - 1, points), BF),
        ],
        axis=0,
    )
    grid_left, grid_right = neighbours(grid[:, :BG], grid[:, points - BG :])
    win = jnp.pad(w_in, ((0, CPAD - channels), (0, 0)))
    wout = jnp.pad(w_out.T, ((0, CPAD - channels), (0, 0)))
    scale = jnp.repeat(logit_scale * (LOG2E / math.sqrt(SIZE)), SIZE, axis=1)
    enc_idx = jnp.clip(enc_src.T, 0, points + 2 * BG - 1).reshape(-1)
    live = jnp.arange(slots, dtype=jnp.int32)[:, None] < enc_count[None, :]
    bias = jnp.where(live, 0.0, NEG).astype(F32)
    bias = bias.reshape(slots, rows // 16, 16).transpose(1, 0, 2).reshape(rows // 16, slots * 16)
    dec_idx = jnp.clip(dec_src.T - (place * rows - BL), 0, rows + 2 * BL - 1).reshape(-1) * 8
    ends = jnp.stack([WIN // 2 - place * rows, total + WIN // 2 - place * rows])

    qt, av = pl.pallas_call(
        fold_kernel,
        out_shape=(shape((HEADS, rows, CPAD)), shape((CPAD, width))),
        in_specs=[VM, HBM, VM, VM],
        out_specs=(VM, VM),
        scratch_shapes=[weight] * 3 + [dma((3,))],
        compiler_params=params(56),
        cost_estimate=pl.CostEstimate(flops=2 * 10**9, bytes_accessed=8 * 2**20, transcendentals=0),
        name="fold",
    )(win, enc_w, latent_init, scale)
    square = shape((width, width))
    latent, normed, pw0, pw1, pw2, pw3, dw0, dw1, dw2, dw3 = pl.pallas_call(
        encode_kernel,
        out_shape=(shape((rows, width)),) * 2 + (square,) * 8,
        in_specs=[SM] + [VM] * 7 + [HBM] * 3,
        out_specs=(VM,) * 10,
        scratch_shapes=[
            pltpu.VMEM((points + 2 * BG, CPAD), F32),
            pltpu.VMEM((slots * 16, CPAD), F32),
            pltpu.VMEM((slots * 16, CPAD), F32),
            pltpu.VMEM((HEADS, rows, CPAD), BF),
            weight,
            dma((9,)),
        ],
        compiler_params=params(28),
        name="encode",
    )(enc_idx, grid_left, grid, grid_right, qt, bias, av, latent_init, enc_w, proc_w, dec_w)
    near_left, near_right = neighbours(normed, normed)
    q, k, v, aq, bo, co = pl.pallas_call(
        project_kernel,
        out_shape=(shape((rows, width)),) * 3
        + (shape((CPAD, width)), shape((width, CPAD)), shape((CPAD, CPAD))),
        in_specs=[VM] * 9,
        out_specs=(VM,) * 6,
        compiler_params=params(24),
        cost_estimate=pl.CostEstimate(flops=3 * 10**9, bytes_accessed=12 * 2**20, transcendentals=0),
        name="project",
    )(normed, win, wout, scale, pw0, pw1, pw2, dw0, dw3)
    latent_out = pl.pallas_call(
        window_kernel,
        out_shape=shape((rows, width)),
        in_specs=[SM] + [VM] * 9,
        out_specs=VM,
        scratch_shapes=[
            pltpu.VMEM((rows + WIN, width), BF),
            pltpu.VMEM((rows + WIN, width), BF),
            pltpu.VMEM((2, rows // 2, rows // 2 + WIN), F32),
            pltpu.VMEM((rows, width), BF),
        ],
        compiler_params=params(24),
        name="window",
    )(ends, q, k, v, near_left, near_right, latent, pw1, pw2, pw3)
    mesh_left, mesh_right = neighbours(latent_out[:BL], latent_out[rows - BL :])
    nodes = rows + 2 * BL
    dq, dk, dv = pl.pallas_call(
        prepare_kernel,
        out_shape=(
            shape((points * 8, 128), F32),
            shape((rows * 8, 128), F32),
            shape((rows * 8, 128), F32),
        ),
        in_specs=[VM] * 5,
        out_specs=(VM,) * 3,
        compiler_params=params(24),
        cost_estimate=pl.CostEstimate(flops=3 * 10**9, bytes_accessed=12 * 2**20, transcendentals=0),
        name="prepare",
    )(latent_out, grid, aq, dw1, dw2)
    out = pl.pallas_call(
        decode_kernel,
        out_shape=shape((channels, points)),
        in_specs=[SM] + [VM] * 10,
        out_specs=VM,
        scratch_shapes=[
            pltpu.VMEM((nodes * 8, 128), F32),
            pltpu.VMEM((nodes * 8, 128), F32),
            pltpu.VMEM((3, CHUNK * 4, 256), BF),
            pltpu.VMEM((3, CHUNK * 4, 256), F32),
            pltpu.VMEM((points * 8, 128), F32),
        ],
        compiler_params=params(32),
        name="decode",
    )(dec_idx, mesh_left, mesh_right, dk, dv, dq, grid, bo, co, dw1, dw2)
    return out.T


def solution(mesh):
    both = ("wide", "narrow")
    placed = (
        P(both, None),
        P(both, None),
        P(both, None),
        P(both),
        P(both, None),
        P(),
        P(),
        P(),
        P(),
        P(),
        P(),
    )
    return jax.shard_map(
        on_device,
        mesh=mesh,
        in_specs=placed,
        out_specs=P(both, None),
        check_vma=False,
    )
```

time: 150 us -> 114 us (0.76)
  Pallas kernels: 80.9 us -> 55.3 us
  local copies, waits for them, and re-layouts: 30.3 us -> 25.2 us
  waiting for transfers between devices: 3.63 us -> 0.02 us
    pallas_call x1, Pallas kernels: 44 us -> 19 us  [on_device(): pl.pallas_call(decode_kernel, out_shape=shape((channels, points)), in_spe...]
    unnamed x37 -> x63, local copies, waits for them, and re-layouts: 27 us -> 22.2 us
    pallas_call x1, Pallas kernels: 16.1 us -> 11.5 us  [on_device(): pl.pallas_call(window_kernel, out_shape=shape((rows, width)), in_specs=[S...]
    pallas_call x1, Pallas kernels: 2.35 us -> 5.57 us  [on_device(): pl.pallas_call(fold_kernel, out_shape=(shape((HEADS, rows, CPAD)), shape(...]
    ppermute x3, waiting for transfers between devices: 1.87 us -> 0.01 us  [neighbours(): after = lax.ppermute(tail, axes, [(i, i + 1) for i in range(count - 1)])]
    ppermute x3, waiting for transfers between devices: 1.76 us -> 0.01 us  [neighbours(): before = lax.ppermute(head, axes, [(i + 1, i) for i in range(count - 1)])]
    pallas_call x1 -> x2, Pallas kernels: 14.3 us -> 15.4 us  [the longest x1 11.2 us: on_device(): pl.pallas_call(encode_kernel, out_shape=(shape((rows, width)),) * 2 + (sq...]
  transfers between devices with their start and end apart: 6 -> 6, of which waited for: 2 -> 0; matrix products, arithmetic and copies ran while one was open for 3% -> 3% of each run, Pallas kernels for 4% -> 12%
where the time goes in v2:
time: 114 us; the launch traced here: 112 us
  Pallas kernels  55.3 us (49%)
  starting transfers between devices  29.5 us (26%)
  local copies, waits for them, and re-layouts  25.2 us (22%)
  other arithmetic  1.39 us (1%)
    ppermute x3, starting transfers between devices, neighbours(): before = lax.ppermute(head, axes, [(i + 1, i) for i in range(count - 1)])  23.8 us
    unnamed x63, local copies, waits for them, and re-layouts  22.2 us
    pallas_call x1, Pallas kernels, on_device(): pl.pallas_call(decode_kernel, out_shape=shape((channels, points)), in_spe...  19 us
    pallas_call x1, Pallas kernels, on_device(): pl.pallas_call(window_kernel, out_shape=shape((rows, width)), in_specs=[S...  11.5 us
    pallas_call x1, Pallas kernels, on_device(): pl.pallas_call(encode_kernel, out_shape=(shape((rows, width)),) * 2 + (sq...  11.2 us
    ppermute x3, starting transfers between devices, neighbours(): after = lax.ppermute(tail, axes, [(i, i + 1) for i in range(count - 1)])  5.75 us
    pallas_call x1, Pallas kernels, on_device(): pl.pallas_call(fold_kernel, out_shape=(shape((HEADS, rows, CPAD)), shape(...  5.57 us
    pallas_call x1, Pallas kernels, on_device(): pl.pallas_call(prepare_kernel, out_shape=(shape((points * 8, 128), F32),...  4.14 us
  transfers between devices with their start and end apart: 6, of which 0 were waited for; matrix products, arithmetic and copies ran while one was open for 3% of the time, Pallas kernels for 12%

profile of v2, /device:TPU:96, one launch (start us, length us, event | category | flops | bytes accessed | tf_op | source)
XLA Modules:
  0.0 111.7 jit_solution(9560183654206432323)
XLA Ops:
  0.0 0.1 pad.11.clone
  0.1 0.1 pad.10.clone
  0.2 1.3 %maximum_maximum_fusion.own.state.grid = bf16[128,2048]{1,0:T(8,128)(2,1)S(1)} fusion(bf16[100,2048]{1,0:T(8,128)(2,1)} %bitcast.13, bf16[128]{0:T(256)(128)(2,1)S(1)} %pad.11.clone, bf16[128]{0:T(256)(128)(2,1)S(1)} %pad.10.clone), kind=kLoop, calls=%fused_computation | loop fusion | flops 1572864 | bytes 934400 | tf_op jit(solution)/shard_map/concatenate | solution.py:303
  1.5 1.9 %collective-permute-start = (bf16[128,1024]{1,0:T(8,128)(2,1)S(1)}, bf16[128,1024]{1,0:T(8,128)(2,1)S(1)}, u32[]{:S(2)}, u32[]{:S(2)}) collective-permute-start(bf16[128,1024]{1,0:T(8,128)(2,1)S(1)} %get-tuple-element.50), channel_id=1, source_target_pairs={{0,1},{1,2},{2,3},{3,4},{4,5},{5,6},{6,7},{7,8},{8,9},{9,10},{10,1... | collective-permute-start | bytes 786440 | tf_op jit(solution)/shard_map/ppermute | solution.py:277
  3.4 7.9 %collective-permute-start.1 = (bf16[128,1024]{1,0:T(8,128)(2,1)S(1)}, bf16[128,1024]{1,0:T(8,128)(2,1)S(1)}, u32[]{:S(2)}, u32[]{:S(2)}) collective-permute-start(bf16[128,1024]{1,0:T(8,128)(2,1)S(1)} %get-tuple-element.49), channel_id=1, source_target_pairs={{1,0},{2,1},{3,2},{4,3},{5,4},{6,5},{7,6},{8,7},{9,8},{10,9},{11,1... | collective-permute-start | bytes 786440 | tf_op jit(solution)/shard_map/ppermute | solution.py:278
  11.3 0.7 pad.7.win
  12.0 0.1 broadcast_in_dim.21
  12.1 0.7 reshape.23.scale
  12.8 0.0 copy-start.10
  12.8 5.6 %fold.1 = (bf16[16,256,128]{2,1,0:T(8,128)(2,1)}, bf16[128,1024]{1,0:T(8,128)(2,1)}) custom-call(bf16[128,1024]{1,0:T(8,128)(2,1)} %pad.7.win, bf16[4,1024,1024]{2,1,0:T(8,128)(2,1)} %enc_w.3, bf16[256,1024]{1,0:T(8,128)(2,1)} %lat.3, f32[3,1024]{1,0:T(4,128)} %reshape.23.scale), custom_call_target="tpu_custom_call" | custom-call | flops 2000000000 | bytes 8388608 | tf_op jit(solution)/shard_map/fold/pallas_call | solution.py:322
  18.4 0.1 lt.27
  18.5 0.1 lt.29
  18.6 0.1 lt.25
  18.7 0.0 collective-permute-done.left
  18.8 0.0 copy-start.20
  18.8 0.7 copy-done.20
  19.5 0.0 collective-permute-done.1.right
  19.5 0.7 copy-done.22
  20.2 1.2 %copy-done.17 = bf16[16,256,128]{2,1,0:T(8,128)(2,1)S(1)} copy-done((bf16[16,256,128]{2,1,0:T(8,128)(2,1)S(1)}, bf16[16,256,128]{2,1,0:T(8,128)(2,1)}, u32[]{:S(2)}) %copy-start.17) | copy-done | bytes 1048600
  21.4 0.9 copy-done.21
  22.4 0.9 copy-done.23
  23.3 0.9 copy-done.24
  24.3 11.2 %encode.1 = (bf16[256,1024]{1,0:T(8,128)(2,1)S(1)}, bf16[256,1024]{1,0:T(8,128)(2,1)}, bf16[1024,1024]{1,0:T(8,128)(2,1)S(1)}, bf16[1024,1024]{1,0:T(8,128)(2,1)...) custom-call(s32[4096]{0:T(1024)S(1)} %bitcast.12, ...), custom_call_target="tpu_custom_call" | custom-call | tf_op jit(solution)/shard_map/encode/pallas_call | solution.py:333
  35.5 1.4 %copy-done = bf16[1024,1024]{1,0:T(8,128)(2,1)} copy-done((bf16[1024,1024]{1,0:T(8,128)(2,1)}, bf16[1024,1024]{1,0:T(8,128)(2,1)S(1)}, u32[]{:S(2)}) %copy-start) | copy-done | bytes 2097176
  36.9 1.4 %copy-done.4 = bf16[1024,1024]{1,0:T(8,128)(2,1)} copy-done((bf16[1024,1024]{1,0:T(8,128)(2,1)}, bf16[1024,1024]{1,0:T(8,128)(2,1)S(1)}, u32[]{:S(2)}) %copy-start.4) | copy-done | bytes 2097176
  38.3 1.3 %copy-done.6 = bf16[1024,1024]{1,0:T(8,128)(2,1)} copy-done((bf16[1024,1024]{1,0:T(8,128)(2,1)}, bf16[1024,1024]{1,0:T(8,128)(2,1)S(1)}, u32[]{:S(2)}) %copy-start.6) | copy-done | bytes 2097176
  39.6 1.4 %copy-done.8 = bf16[1024,1024]{1,0:T(8,128)(2,1)} copy-done((bf16[1024,1024]{1,0:T(8,128)(2,1)}, bf16[1024,1024]{1,0:T(8,128)(2,1)S(1)}, u32[]{:S(2)}) %copy-start.8) | copy-done | bytes 2097176
  41.0 1.4 %copy-done.11 = bf16[1024,1024]{1,0:T(8,128)(2,1)} copy-done((bf16[1024,1024]{1,0:T(8,128)(2,1)}, bf16[1024,1024]{1,0:T(8,128)(2,1)S(1)}, u32[]{:S(2)}) %copy-start.11) | copy-done | bytes 2097176
  42.4 1.4 %copy-done.13 = bf16[1024,1024]{1,0:T(8,128)(2,1)} copy-done((bf16[1024,1024]{1,0:T(8,128)(2,1)}, bf16[1024,1024]{1,0:T(8,128)(2,1)S(1)}, u32[]{:S(2)}) %copy-start.13) | copy-done | bytes 2097176
  43.8 1.3 %copy-done.15 = bf16[1024,1024]{1,0:T(8,128)(2,1)} copy-done((bf16[1024,1024]{1,0:T(8,128)(2,1)}, bf16[1024,1024]{1,0:T(8,128)(2,1)S(1)}, u32[]{:S(2)}) %copy-start.15) | copy-done | bytes 2097176
  45.1 0.8 copy-done.18
  45.9 1.9 %collective-permute-start.2 = (bf16[256,1024]{1,0:T(8,128)(2,1)}, bf16[256,1024]{1,0:T(8,128)(2,1)}, u32[]{:S(2)}, u32[]{:S(2)}) collective-permute-start(bf16[256,1024]{1,0:T(8,128)(2,1)} %get-tuple-element.28.normed), channel_id=1, source_target_pairs={{0,1},{1,2},{2,3},{3,4},{4,5},{5,6},{6,7},{7,8},{8,9},{9,10},{10,1... | collective-permute-start | bytes 1572872 | tf_op jit(solution)/shard_map/ppermute | solution.py:277
  47.8 7.9 %collective-permute-start.3 = (bf16[256,1024]{1,0:T(8,128)(2,1)}, bf16[256,1024]{1,0:T(8,128)(2,1)}, u32[]{:S(2)}, u32[]{:S(2)}) collective-permute-start(bf16[256,1024]{1,0:T(8,128)(2,1)} %get-tuple-element.28.normed), channel_id=1, source_target_pairs={{1,0},{2,1},{3,2},{4,3},{5,4},{6,5},{7,6},{8,7},{9,8},{10,9},{11,1... | collective-permute-start | bytes 1572872 | tf_op jit(solution)/shard_map/ppermute | solution.py:278
  55.7 1.0 pad.8.wout
  56.7 0.1 pad_add_fusion.ends
  56.8 1.6 %copy-done.1 = bf16[1024,1024]{1,0:T(8,128)(2,1)S(1)} copy-done((bf16[1024,1024]{1,0:T(8,128)(2,1)S(1)}, bf16[1024,1024]{1,0:T(8,128)(2,1)}, u32[]{:S(2)}) %copy-start.1) | copy-done | bytes 2097176
  58.4 1.6 %copy-done.12 = bf16[1024,1024]{1,0:T(8,128)(2,1)S(1)} copy-done((bf16[1024,1024]{1,0:T(8,128)(2,1)S(1)}, bf16[1024,1024]{1,0:T(8,128)(2,1)}, u32[]{:S(2)}) %copy-start.12) | copy-done | bytes 2097176
  59.9 1.6 %copy-done.14 = bf16[1024,1024]{1,0:T(8,128)(2,1)S(1)} copy-done((bf16[1024,1024]{1,0:T(8,128)(2,1)S(1)}, bf16[1024,1024]{1,0:T(8,128)(2,1)}, u32[]{:S(2)}) %copy-start.14) | copy-done | bytes 2097176
  61.5 1.6 %copy-done.16 = bf16[1024,1024]{1,0:T(8,128)(2,1)S(1)} copy-done((bf16[1024,1024]{1,0:T(8,128)(2,1)S(1)}, bf16[1024,1024]{1,0:T(8,128)(2,1)}, u32[]{:S(2)}) %copy-start.16) | copy-done | bytes 2097176
  63.1 3.9 %project.1 = (bf16[256,1024]{1,0:T(8,128)(2,1)S(1)}, bf16[256,1024]{1,0:T(8,128)(2,1)S(1)}, bf16[256,1024]{1,0:T(8,128)(2,1)S(1)}, bf16[128,1024]{1,0:T(8,128)(2...) custom-call(bf16[256,1024]{1,0:T(8,128)(2,1)} %get-tuple-element.28.normed, ...), custom_call_target="tpu_custom_call" | custom-call | flops 3000000000 | bytes 12582912 | tf_op jit(solution)/shard_map/project/pallas_call | solution.py:350
  67.0 0.0 collective-permute-done.2.nl
  67.0 0.0 collective-permute-done.3.nr
  67.1 11.5 %window.1.own = bf16[256,1024]{1,0:T(8,128)(2,1)S(1)} custom-call(s32[2]{0:T(128)S(1)} %pad_add_fusion.ends, bf16[256,1024]{1,0:T(8,128)(2,1)S(1)} %get-tuple-element.34.q, bf16[256,1024]{1,0:T(8,128)(2,1)S(1)} %get-tuple-element.35.k, bf16[256,1024]{1,0:T(8,128)(2,1)S(1)} %get-tuple-element.36.v, bf16[256,1024]{1,0:T(8,128)(2,1)} %collective-permute-done.2.nl, ...), custom_call_target="tpu_custom_call" | custom-call | tf_op jit(solution)/shard_map/window/pallas_call | solution.py:360
  78.6 1.9 %collective-permute-start.4 = (bf16[128,1024]{1,0:T(8,128)(2,1)S(1)}, bf16[128,1024]{1,0:T(8,128)(2,1)S(1)}, u32[]{:S(2)}, u32[]{:S(2)}) collective-permute-start(bf16[128,1024]{1,0:T(8,128)(2,1)S(1)} %get-tuple-element.48), channel_id=1, source_target_pairs={{0,1},{1,2},{2,3},{3,4},{4,5},{5,6},{6,7},{7,8},{8,9},{9,10},{10,1... | collective-permute-start | bytes 786440 | tf_op jit(solution)/shard_map/ppermute | solution.py:277
  80.6 8.0 %collective-permute-start.5 = (bf16[128,1024]{1,0:T(8,128)(2,1)S(1)}, bf16[128,1024]{1,0:T(8,128)(2,1)S(1)}, u32[]{:S(2)}, u32[]{:S(2)}) collective-permute-start(bf16[128,1024]{1,0:T(8,128)(2,1)S(1)} %get-tuple-element.47), channel_id=1, source_target_pairs={{1,0},{2,1},{3,2},{4,3},{5,4},{6,5},{7,6},{8,7},{9,8},{10,9},{11,1... | collective-permute-start | bytes 786440 | tf_op jit(solution)/shard_map/ppermute | solution.py:278
  88.6 4.1 %prepare.1 = (f32[16384,128]{1,0:T(8,128)S(1)}, f32[2048,128]{1,0:T(8,128)S(1)}, f32[2048,128]{1,0:T(8,128)S(1)}) custom-call(bf16[256,1024]{1,0:T(8,128)(2,1)S(1)} %window.1.own, bf16[128,2048]{1,0:T(8,128)(2,1)S(1)} %maximum_maximum_fusion.own.state.grid, bf16[128,1024]{1,0:T(8,128)(2,1)S(1)} %get-tuple-element.39.aq, bf16[1024,1024]{1,0:T(8,128)(2,1)S(1)} %copy-done.5, ...), custom_call_target="tpu_custom_call" | custom-call | flops 3000000000 | bytes 12582912 | tf_op jit(solution)/shard_map/prepare/pallas_call | solution.py:376
  92.8 0.0 collective-permute-done.5.right
  92.8 19.0 %decode.1 = bf16[100,2048]{1,0:T(8,128)(2,1)} custom-call(s32[6144]{0:T(1024)S(1)} %mul.29.idx, bf16[128,1024]{1,0:T(8,128)(2,1)S(1)} %collective-permute-done.4.left, bf16[128,1024]{1,0:T(8,128)(2,1)S(1)} %collective-permute-done.5.right, f32[2048,128]{1,0:T(8,128)S(1)} %get-tuple-element.42.ko, f32[2048,128]{1,0:T(8,128)S(1)} %get-tuple-element.43.vo, ...), custom_call_target="tpu_custom_call" | custom-call | tf_op jit(solution)/shard_map/decode/pallas_call | solution.py:389
  (54 shorter events, 0.2 us)
Async XLA Ops:
  0.0 11.3 %copy-start.26 = (bf16[100,1024]{1,0:T(8,128)(2,1)S(1)}, bf16[100,1024]{1,0:T(8,128)(2,1)}, u32[]{:S(2)}) copy-start(bf16[100,1024]{1,0:T(8,128)(2,1)} %param.16) | copy-start | bytes 614404
  0.0 12.0 %copy-start.29 = (f32[3,16]{1,0:T(4,128)S(1)}, f32[3,16]{1,0:T(4,128)}, u32[]{:S(2)}) copy-start(f32[3,16]{1,0:T(4,128)} %param.21) | copy-start | bytes 580
  0.0 12.8 %copy-start.28 = (s32[256,16]{0,1:T(8,128)S(1)}, s32[256,16]{0,1:T(8,128)}, u32[]{:S(2)}) copy-start(s32[256,16]{0,1:T(8,128)} %param.13) | copy-start | bytes 49156
  1.5 17.2 %collective-permute-start = (bf16[128,1024]{1,0:T(8,128)(2,1)S(1)}, bf16[128,1024]{1,0:T(8,128)(2,1)S(1)}, u32[]{:S(2)}, u32[]{:S(2)}) collective-permute-start(bf16[128,1024]{1,0:T(8,128)(2,1)S(1)} %get-tuple-element.50), channel_id=1, source_target_pairs={{0,1},{1,2},{2,3},{3,4},{4,5},{5,6},{6,7},{7,8},{8,9},{9,10},{10,1... | collective-permute-start | bytes 786440 | tf_op jit(solution)/shard_map/ppermute | solution.py:277
  3.4 16.0 %collective-permute-start.1 = (bf16[128,1024]{1,0:T(8,128)(2,1)S(1)}, bf16[128,1024]{1,0:T(8,128)(2,1)S(1)}, u32[]{:S(2)}, u32[]{:S(2)}) collective-permute-start(bf16[128,1024]{1,0:T(8,128)(2,1)S(1)} %get-tuple-element.49), channel_id=1, source_target_pairs={{1,0},{2,1},{3,2},{4,3},{5,4},{6,5},{7,6},{8,7},{9,8},{10,9},{11,1... | collective-permute-start | bytes 786440 | tf_op jit(solution)/shard_map/ppermute | solution.py:278
  12.8 5.6 %copy-start.30 = (s32[256]{0:T(256)S(1)}, s32[256]{0:T(256)}, u32[]{:S(2)}) copy-start(s32[256]{0:T(256)} %param.14) | copy-start | bytes 3076
  12.8 7.4 %copy-start.10 = (bf16[256,1024]{1,0:T(8,128)(2,1)S(1)}, bf16[256,1024]{1,0:T(8,128)(2,1)}, u32[]{:S(2)}) copy-start(bf16[256,1024]{1,0:T(8,128)(2,1)} %lat.3) | copy-start | bytes 1572868
  18.8 0.7 copy-start.20
  19.5 0.7 copy-start.22
  20.2 1.2 %copy-start.17 = (bf16[16,256,128]{2,1,0:T(8,128)(2,1)S(1)}, bf16[16,256,128]{2,1,0:T(8,128)(2,1)}, u32[]{:S(2)}) copy-start(bf16[16,256,128]{2,1,0:T(8,128)(2,1)} %get-tuple-element.26.qt) | copy-start | bytes 3145732
  21.4 0.9 copy-start.21
  22.4 0.9 copy-start.23
  23.3 0.9 copy-start.24
  24.3 31.4 %copy-start.27 = (s32[2048,3]{0,1:T(4,128)S(1)}, s32[2048,3]{0,1:T(4,128)}, u32[]{:S(2)}) copy-start(s32[2048,3]{0,1:T(4,128)} %param.15) | copy-start | bytes 73732
  24.3 32.5 %copy-start.3 = (bf16[128,1024]{1,0:T(8,128)(2,1)S(1)}, bf16[128,1024]{1,0:T(8,128)(2,1)}, u32[]{:S(2)}) copy-start(bf16[128,1024]{1,0:T(8,128)(2,1)} %pad.7.win) | copy-start | bytes 786436
  24.3 32.5 %copy-start.25 = (f32[3,1024]{1,0:T(4,128)S(1)}, f32[3,1024]{1,0:T(4,128)}, u32[]{:S(2)}) copy-start(f32[3,1024]{1,0:T(4,128)} %reshape.23.scale) | copy-start | bytes 36868
  35.5 1.4 %copy-start = (bf16[1024,1024]{1,0:T(8,128)(2,1)}, bf16[1024,1024]{1,0:T(8,128)(2,1)S(1)}, u32[]{:S(2)}) copy-start(bf16[1024,1024]{1,0:T(8,128)(2,1)S(1)} %get-tuple-element.31.wv) | copy-start | bytes 6291460
  36.9 1.4 %copy-start.4 = (bf16[1024,1024]{1,0:T(8,128)(2,1)}, bf16[1024,1024]{1,0:T(8,128)(2,1)S(1)}, u32[]{:S(2)}) copy-start(bf16[1024,1024]{1,0:T(8,128)(2,1)S(1)} %get-tuple-element.40.wk) | copy-start | bytes 6291460
  38.3 1.3 %copy-start.6 = (bf16[1024,1024]{1,0:T(8,128)(2,1)}, bf16[1024,1024]{1,0:T(8,128)(2,1)S(1)}, u32[]{:S(2)}) copy-start(bf16[1024,1024]{1,0:T(8,128)(2,1)S(1)} %get-tuple-element.41.wv) | copy-start | bytes 6291460
  39.6 1.4 %copy-start.8 = (bf16[1024,1024]{1,0:T(8,128)(2,1)}, bf16[1024,1024]{1,0:T(8,128)(2,1)S(1)}, u32[]{:S(2)}) copy-start(bf16[1024,1024]{1,0:T(8,128)(2,1)S(1)} %get-tuple-element.38.wo) | copy-start | bytes 6291460
  41.0 1.4 %copy-start.11 = (bf16[1024,1024]{1,0:T(8,128)(2,1)}, bf16[1024,1024]{1,0:T(8,128)(2,1)S(1)}, u32[]{:S(2)}) copy-start(bf16[1024,1024]{1,0:T(8,128)(2,1)S(1)} %get-tuple-element.29.wq) | copy-start | bytes 6291460
  42.4 1.4 %copy-start.13 = (bf16[1024,1024]{1,0:T(8,128)(2,1)}, bf16[1024,1024]{1,0:T(8,128)(2,1)S(1)}, u32[]{:S(2)}) copy-start(bf16[1024,1024]{1,0:T(8,128)(2,1)S(1)} %get-tuple-element.32.dq) | copy-start | bytes 6291460
  43.8 1.3 %copy-start.15 = (bf16[1024,1024]{1,0:T(8,128)(2,1)}, bf16[1024,1024]{1,0:T(8,128)(2,1)S(1)}, u32[]{:S(2)}) copy-start(bf16[1024,1024]{1,0:T(8,128)(2,1)S(1)} %get-tuple-element.33.do) | copy-start | bytes 6291460
  45.1 0.8 copy-start.18
  45.9 21.1 %collective-permute-start.2 = (bf16[256,1024]{1,0:T(8,128)(2,1)}, bf16[256,1024]{1,0:T(8,128)(2,1)}, u32[]{:S(2)}, u32[]{:S(2)}) collective-permute-start(bf16[256,1024]{1,0:T(8,128)(2,1)} %get-tuple-element.28.normed), channel_id=1, source_target_pairs={{0,1},{1,2},{2,3},{3,4},{4,5},{5,6},{6,7},{7,8},{8,9},{9,10},{10,1... | collective-permute-start | bytes 1572872 | tf_op jit(solution)/shard_map/ppermute | solution.py:277
  47.8 19.2 %collective-permute-start.3 = (bf16[256,1024]{1,0:T(8,128)(2,1)}, bf16[256,1024]{1,0:T(8,128)(2,1)}, u32[]{:S(2)}, u32[]{:S(2)}) collective-permute-start(bf16[256,1024]{1,0:T(8,128)(2,1)} %get-tuple-element.28.normed), channel_id=1, source_target_pairs={{1,0},{2,1},{3,2},{4,3},{5,4},{6,5},{7,6},{8,7},{9,8},{10,9},{11,1... | collective-permute-start | bytes 1572872 | tf_op jit(solution)/shard_map/ppermute | solution.py:278
  56.8 1.6 %copy-start.1 = (bf16[1024,1024]{1,0:T(8,128)(2,1)S(1)}, bf16[1024,1024]{1,0:T(8,128)(2,1)}, u32[]{:S(2)}) copy-start(bf16[1024,1024]{1,0:T(8,128)(2,1)} %copy-done) | copy-start | bytes 6291460
  58.4 1.6 %copy-start.12 = (bf16[1024,1024]{1,0:T(8,128)(2,1)S(1)}, bf16[1024,1024]{1,0:T(8,128)(2,1)}, u32[]{:S(2)}) copy-start(bf16[1024,1024]{1,0:T(8,128)(2,1)} %copy-done.11) | copy-start | bytes 6291460
  59.9 1.6 %copy-start.14 = (bf16[1024,1024]{1,0:T(8,128)(2,1)S(1)}, bf16[1024,1024]{1,0:T(8,128)(2,1)}, u32[]{:S(2)}) copy-start(bf16[1024,1024]{1,0:T(8,128)(2,1)} %copy-done.13) | copy-start | bytes 6291460
  61.5 1.6 %copy-start.16 = (bf16[1024,1024]{1,0:T(8,128)(2,1)S(1)}, bf16[1024,1024]{1,0:T(8,128)(2,1)}, u32[]{:S(2)}) copy-start(bf16[1024,1024]{1,0:T(8,128)(2,1)} %copy-done.15) | copy-start | bytes 6291460
  63.1 3.9 %copy-start.2 = (bf16[1024,1024]{1,0:T(8,128)(2,1)S(1)}, bf16[1024,1024]{1,0:T(8,128)(2,1)}, u32[]{:S(2)}) copy-start(bf16[1024,1024]{1,0:T(8,128)(2,1)} %copy-done) | copy-start | bytes 6291460
  63.1 3.9 %copy-start.9 = (bf16[1024,1024]{1,0:T(8,128)(2,1)S(1)}, bf16[1024,1024]{1,0:T(8,128)(2,1)}, u32[]{:S(2)}) copy-start(bf16[1024,1024]{1,0:T(8,128)(2,1)} %copy-done.8) | copy-start | bytes 6291460
  63.1 3.9 %copy-start.19 = (bf16[256,1024]{1,0:T(8,128)(2,1)S(1)}, bf16[256,1024]{1,0:T(8,128)(2,1)}, u32[]{:S(2)}) copy-start(bf16[256,1024]{1,0:T(8,128)(2,1)} %copy-done.18) | copy-start | bytes 1572868
  67.1 21.5 %copy-start.5 = (bf16[1024,1024]{1,0:T(8,128)(2,1)S(1)}, bf16[1024,1024]{1,0:T(8,128)(2,1)}, u32[]{:S(2)}) copy-start(bf16[1024,1024]{1,0:T(8,128)(2,1)} %copy-done.4) | copy-start | bytes 6291460
  67.1 21.5 %copy-start.7 = (bf16[1024,1024]{1,0:T(8,128)(2,1)S(1)}, bf16[1024,1024]{1,0:T(8,128)(2,1)}, u32[]{:S(2)}) copy-start(bf16[1024,1024]{1,0:T(8,128)(2,1)} %copy-done.6) | copy-start | bytes 6291460
  78.6 14.1 %collective-permute-start.4 = (bf16[128,1024]{1,0:T(8,128)(2,1)S(1)}, bf16[128,1024]{1,0:T(8,128)(2,1)S(1)}, u32[]{:S(2)}, u32[]{:S(2)}) collective-permute-start(bf16[128,1024]{1,0:T(8,128)(2,1)S(1)} %get-tuple-element.48), channel_id=1, source_target_pairs={{0,1},{1,2},{2,3},{3,4},{4,5},{5,6},{6,7},{7,8},{8,9},{9,10},{10,1... | collective-permute-start | bytes 786440 | tf_op jit(solution)/shard_map/ppermute | solution.py:277
  80.6 12.2 %collective-permute-start.5 = (bf16[128,1024]{1,0:T(8,128)(2,1)S(1)}, bf16[128,1024]{1,0:T(8,128)(2,1)S(1)}, u32[]{:S(2)}, u32[]{:S(2)}) collective-permute-start(bf16[128,1024]{1,0:T(8,128)(2,1)S(1)} %get-tuple-element.47), channel_id=1, source_target_pairs={{1,0},{2,1},{3,2},{4,3},{5,4},{6,5},{7,6},{8,7},{9,8},{10,9},{11,1... | collective-permute-start | bytes 786440 | tf_op jit(solution)/shard_map/ppermute | solution.py:278

commit v3 on v2

--- a/solution.py
+++ b/solution.py
@@ -50,7 +50,8 @@
     return copies
 
 
-def fold_kernel(win, enc_w, lat, scale, qt, av, w0, w1, w2, sems):
+def fold_kernel(win, enc_w, lat, scale, *others):
+    qt, av, w0, w1, w2, sems = others[-6:]
     got = fetch(enc_w, (1, 0, 2), (w1, w0, w2), sems)
     got[0].wait()
     ak = dot(win[...], w1[...]).astype(BF)
@@ -147,7 +148,7 @@
 
 
 def window_kernel(
-    ends, q, k, v, nl, nr, latent, wk, wv, wo, out, keys, values, bias, mixed
+    ends, q, k, v, nl, nr, latent, wk, wv, wo, out, head, tail, keys, values, bias, mixed
 ):
     rows = q.shape[0]
     half = rows // 2
@@ -160,10 +161,11 @@
         place = col + side * half
         inside = (col >= row) & (col - row <= WIN) & (place >= ends[0]) & (place < ends[1])
         bias[side] = jnp.where(inside, 0.0, NEG)
-    keys[:rows, :] = dot(nl[...], wk[...]).astype(BF)
-    keys[2 * rows :, :] = dot(nr[...], wk[...]).astype(BF)
-    values[:rows, :] = dot(nl[...], wv[...]).astype(BF)
-    values[2 * rows :, :] = dot(nr[...], wv[...]).astype(BF)
+    halo = jnp.concatenate([nl[...], nr[...]], axis=0)
+    for weight, wide in ((wk, keys), (wv, values)):
+        both = dot(halo, weight[...]).astype(BF)
+        wide[:rows, :] = both[:rows]
+        wide[2 * rows :, :] = both[rows:]
     low = low_half((1, 128))
 
     def one_pair(pair, carry):
@@ -187,8 +189,10 @@
             mixed[these, lanes] = jnp.where(low, part[:half], part[half:]).astype(BF)
         return carry
 
-    lax.fori_loop(0, PAIRS, one_pair, 0)
+    lax.fori_loop(0, PAIRS, one_pair, 0, unroll=True)
     out[...] = (latent[...].astype(F32) + dot(mixed[...], wo[...])).astype(BF)
+    head[...] = out[:BL, :]
+    tail[...] = out[rows - BL :, :]
 
 
 CHUNK = 128
@@ -215,10 +219,13 @@
 ):
     points = grid.shape[1]
     side = left.shape[0]
+    halo = jnp.concatenate([left[...], right[...]], axis=0)
     for weight, tiles, own in ((wk, kf, ko), (wv, vf, vo)):
-        to_tiles(left[...], weight, tiles, 0)
         tiles[side * 8 : side * 8 + own.shape[0], :] = own[...]
-        to_tiles(right[...], weight, tiles, side + own.shape[0] // 8)
+        for block in range(8):
+            both = dot(halo, weight[:, block * 128 : block * 128 + 128])
+            tiles[pl.ds(block, side, stride=8), :] = both[:side]
+            tiles[pl.ds(side * 8 + own.shape[0] + block, side, stride=8), :] = both[side:]
     head_row = lax.broadcasted_iota(jnp.int32, (256, 256), 0) // SIZE
     head_col = lax.broadcasted_iota(jnp.int32, (256, 256), 1) // SIZE
     ones = jnp.where(head_row == head_col, 1.0, 0.0).astype(BF)
@@ -322,13 +329,13 @@
     qt, av = pl.pallas_call(
         fold_kernel,
         out_shape=(shape((HEADS, rows, CPAD)), shape((CPAD, width))),
-        in_specs=[VM, HBM, VM, VM],
+        in_specs=[VM, HBM, VM, VM] + [pl.BlockSpec(memory_space=pl.ANY)] * 5,
         out_specs=(VM, VM),
         scratch_shapes=[weight] * 3 + [dma((3,))],
-        compiler_params=params(56),
+        compiler_params=params(53),
         cost_estimate=pl.CostEstimate(flops=2 * 10**9, bytes_accessed=8 * 2**20, transcendentals=0),
         name="fold",
-    )(win, enc_w, latent_init, scale)
+    )(win, enc_w, latent_init, scale, wout, enc_idx, bias, dec_idx, ends)
     square = shape((width, width))
     latent, normed, pw0, pw1, pw2, pw3, dw0, dw1, dw2, dw3 = pl.pallas_call(
         encode_kernel,
@@ -357,11 +364,11 @@
         cost_estimate=pl.CostEstimate(flops=3 * 10**9, bytes_accessed=12 * 2**20, transcendentals=0),
         name="project",
     )(normed, win, wout, scale, pw0, pw1, pw2, dw0, dw3)
-    latent_out = pl.pallas_call(
+    latent_out, mesh_head, mesh_tail = pl.pallas_call(
         window_kernel,
-        out_shape=shape((rows, width)),
+        out_shape=(shape((rows, width)), shape((BL, width)), shape((BL, width))),
         in_specs=[SM] + [VM] * 9,
-        out_specs=VM,
+        out_specs=(VM,) * 3,
         scratch_shapes=[
             pltpu.VMEM((rows + WIN, width), BF),
             pltpu.VMEM((rows + WIN, width), BF),
@@ -371,7 +378,7 @@
         compiler_params=params(24),
         name="window",
     )(ends, q, k, v, near_left, near_right, latent, pw1, pw2, pw3)
-    mesh_left, mesh_right = neighbours(latent_out[:BL], latent_out[rows - BL :])
+    mesh_left, mesh_right = neighbours(mesh_head, mesh_tail)
     nodes = rows + 2 * BL
     dq, dk, dv = pl.pallas_call(
         prepare_kernel,

time: 114 us -> 95.2 us (0.84)
  local copies, waits for them, and re-layouts: 25.2 us -> 2.62 us
  waiting for transfers between devices: 0.02 us -> 11.8 us
  Pallas kernels: 55.3 us -> 49.7 us
  starting transfers between devices: 29.5 us -> 26.5 us
  other arithmetic: 1.39 us -> 2.85 us
    unnamed x63 -> x11, local copies, waits for them, and re-layouts: 22.2 us -> 1.25 us
    ppermute x3, waiting for transfers between devices: 0.01 us -> 9.89 us  [neighbours(): after = lax.ppermute(tail, axes, [(i, i + 1) for i in range(count - 1)])]
    ppermute x3, starting transfers between devices: 23.8 us -> 20.5 us  [neighbours(): before = lax.ppermute(head, axes, [(i + 1, i) for i in range(count - 1)])]
    pallas_call x1, Pallas kernels: 11.5 us -> 8.51 us  [on_device(): pl.pallas_call(window_kernel, out_shape=(shape((rows, width)), shape((BL,...]
    ppermute x3, waiting for transfers between devices: 0.01 us -> 1.87 us  [neighbours(): before = lax.ppermute(head, axes, [(i + 1, i) for i in range(count - 1)])]
    pallas_call x1, Pallas kernels: 3.87 us -> 2.7 us  [on_device(): pl.pallas_call(project_kernel, out_shape=(shape((rows, width)),) * 3 + (s...]
  transfers between devices with their start and end apart: 6 -> 6, of which waited for: 0 -> 3; matrix products, arithmetic and copies ran while one was open for 3% -> 3% of each run, Pallas kernels for 12% -> 13%
where the time goes in v3:
time: 95.2 us; the launch traced here: 93.6 us
  Pallas kernels  49.7 us (52%)
  starting transfers between devices  26.5 us (28%)
  waiting for transfers between devices  11.8 us (12%)
  other arithmetic  2.85 us (3%)
  local copies, waits for them, and re-layouts  2.62 us (3%)
    ppermute x3, starting transfers between devices, neighbours(): before = lax.ppermute(head, axes, [(i + 1, i) for i in range(count - 1)])  20.5 us
    pallas_call x1, Pallas kernels, on_device(): pl.pallas_call(decode_kernel, out_shape=shape((channels, points)), in_spe...  18.7 us
    pallas_call x1, Pallas kernels, on_device(): pl.pallas_call(encode_kernel, out_shape=(shape((rows, width)),) * 2 + (sq...  10.5 us
    ppermute x3, waiting for transfers between devices, neighbours(): after = lax.ppermute(tail, axes, [(i, i + 1) for i in range(count - 1)])  9.89 us
    pallas_call x1, Pallas kernels, on_device(): pl.pallas_call(window_kernel, out_shape=(shape((rows, width)), shape((BL,...  8.51 us
    ppermute x3, starting transfers between devices, neighbours(): after = lax.ppermute(tail, axes, [(i, i + 1) for i in range(count - 1)])  5.94 us
    pallas_call x1, Pallas kernels, on_device(): pl.pallas_call(fold_kernel, out_shape=(shape((HEADS, rows, CPAD)), shape(...  5.32 us
    pallas_call x1, Pallas kernels, on_device(): pl.pallas_call(prepare_kernel, out_shape=(shape((points * 8, 128), F32),...  4.09 us
  transfers between devices with their start and end apart: 6, of which 3 were waited for; matrix products, arithmetic and copies ran while one was open for 3% of the time, Pallas kernels for 13%

profile of v3, /device:TPU:96, one launch (start us, length us, event | category | flops | bytes accessed | tf_op | source)
XLA Modules:
  0.0 93.6 jit_solution(10567700574993891112)
XLA Ops:
  0.0 0.0 copy-start.4
  0.0 0.0 copy-start.2
  0.0 0.0 copy-start.3
  0.0 0.1 pad.10.clone
  0.1 0.1 pad.11.clone
  0.2 1.3 %maximum_maximum_fusion.own.state.grid = bf16[128,2048]{1,0:T(8,128)(2,1)S(1)} fusion(bf16[100,2048]{1,0:T(8,128)(2,1)} %bitcast.14, bf16[128]{0:T(256)(128)(2,1)S(1)} %pad.11.clone, bf16[128]{0:T(256)(128)(2,1)S(1)} %pad.10.clone), kind=kLoop, calls=%fused_computation | loop fusion | flops 1572864 | bytes 934400 | tf_op jit(solution)/shard_map/concatenate | solution.py:310
  1.5 6.4 %collective-permute-start.1 = (bf16[128,1024]{1,0:T(8,128)(2,1)S(1)}, bf16[128,1024]{1,0:T(8,128)(2,1)S(1)}, u32[]{:S(2)}, u32[]{:S(2)}) collective-permute-start(bf16[128,1024]{1,0:T(8,128)(2,1)S(1)} %get-tuple-element.53), channel_id=1, source_target_pairs={{1,0},{2,1},{3,2},{4,3},{5,4},{6,5},{7,6},{8,7},{9,8},{10,9},{11,1... | collective-permute-start | bytes 786440 | tf_op jit(solution)/shard_map/ppermute | solution.py:285
  7.9 1.9 %collective-permute-start = (bf16[128,1024]{1,0:T(8,128)(2,1)S(1)}, bf16[128,1024]{1,0:T(8,128)(2,1)S(1)}, u32[]{:S(2)}, u32[]{:S(2)}) collective-permute-start(bf16[128,1024]{1,0:T(8,128)(2,1)S(1)} %get-tuple-element.54), channel_id=1, source_target_pairs={{0,1},{1,2},{2,3},{3,4},{4,5},{5,6},{6,7},{7,8},{8,9},{9,10},{10,1... | collective-permute-start | bytes 786440 | tf_op jit(solution)/shard_map/ppermute | solution.py:284
  9.9 0.7 broadcast_multiply_fusion
  10.6 0.8 lt.27
  11.3 0.1 lt.25
  11.4 0.7 clamp_bitcast_fusion
  12.2 0.1 broadcast_in_dim.21
  12.2 0.1 reshape.23.scale
  12.3 0.0 copy-done.4
  12.4 0.1 lt.29
  12.5 0.0 copy-done.2
  12.5 0.0 copy-done.3
  12.6 0.1 pad_add_fusion.others_4_.ends
  12.7 0.0 copy-start
  12.7 5.3 %fold.1 = (bf16[16,256,128]{2,1,0:T(8,128)(2,1)}, bf16[128,1024]{1,0:T(8,128)(2,1)S(1)}) custom-call(bf16[128,1024]{1,0:T(8,128)(2,1)S(1)} %pad.7.win, bf16[4,1024,1024]{2,1,0:T(8,128)(2,1)} %enc_w.3, bf16[256,1024]{1,0:T(8,128)(2,1)} %lat.3, f32[3,1024]{1,0:T(4,128)S(1)} %reshape.23.scale, bf16[128,1024]{1,0:T(8,128)(2,1)S(1)} %pad.8.others_0_.wout, ...), custom_call_target="tpu_custom_call" | custom-call | flops 2000000000 | bytes 8388608 | tf_op jit(solution)/shard_map/fold/pallas_call | solution.py:329
  18.0 0.0 collective-permute-done.1.right
  18.0 1.8 %collective-permute-done.left = bf16[128,1024]{1,0:T(8,128)(2,1)S(1)} collective-permute-done((bf16[128,1024]{1,0:T(8,128)(2,1)S(1)}, bf16[128,1024]{1,0:T(8,128)(2,1)S(1)}, u32[]{:S(2)}, u32[]{:S(2)}) %collective-permute-start) | collective-permute-done | bytes 262176 | tf_op jit(solution)/shard_map/ppermute | solution.py:284
  19.9 0.0 copy-done
  19.9 0.0 copy-start.1
  19.9 1.2 %copy-done.1 = bf16[16,256,128]{2,1,0:T(8,128)(2,1)S(1)} copy-done((bf16[16,256,128]{2,1,0:T(8,128)(2,1)S(1)}, bf16[16,256,128]{2,1,0:T(8,128)(2,1)}, u32[]{:S(2)}) %copy-start.1) | copy-done | bytes 1048600
  21.1 10.5 %encode.1 = (bf16[256,1024]{1,0:T(8,128)(2,1)S(1)}, bf16[256,1024]{1,0:T(8,128)(2,1)S(1)}, bf16[1024,1024]{1,0:T(8,128)(2,1)S(1)}, bf16[1024,1024]{1,0:T(8,128)(...) custom-call(s32[4096]{0:T(1024)S(1)} %bitcast.13, ...), custom_call_target="tpu_custom_call" | custom-call | tf_op jit(solution)/shard_map/encode/pallas_call | solution.py:340
  31.6 6.0 %collective-permute-start.3 = (bf16[256,1024]{1,0:T(8,128)(2,1)S(1)}, bf16[256,1024]{1,0:T(8,128)(2,1)S(1)}, u32[]{:S(2)}, u32[]{:S(2)}) collective-permute-start(bf16[256,1024]{1,0:T(8,128)(2,1)S(1)} %get-tuple-element.31.normed), channel_id=1, source_target_pairs={{1,0},{2,1},{3,2},{4,3},{5,4},{6,5},{7,6},{8,7},{9,8},{10,9},{11,1... | collective-permute-start | bytes 1572872 | tf_op jit(solution)/shard_map/ppermute | solution.py:285
  37.6 2.1 %collective-permute-start.2 = (bf16[256,1024]{1,0:T(8,128)(2,1)S(1)}, bf16[256,1024]{1,0:T(8,128)(2,1)S(1)}, u32[]{:S(2)}, u32[]{:S(2)}) collective-permute-start(bf16[256,1024]{1,0:T(8,128)(2,1)S(1)} %get-tuple-element.31.normed), channel_id=1, source_target_pairs={{0,1},{1,2},{2,3},{3,4},{4,5},{5,6},{6,7},{7,8},{8,9},{9,10},{10,1... | collective-permute-start | bytes 1572872 | tf_op jit(solution)/shard_map/ppermute | solution.py:284
  39.7 2.7 %project.1 = (bf16[256,1024]{1,0:T(8,128)(2,1)S(1)}, bf16[256,1024]{1,0:T(8,128)(2,1)S(1)}, bf16[256,1024]{1,0:T(8,128)(2,1)S(1)}, bf16[128,1024]{1,0:T(8,128)(2...) custom-call(bf16[256,1024]{1,0:T(8,128)(2,1)S(1)} %get-tuple-element.31.normed, ...), custom_call_target="tpu_custom_call" | custom-call | flops 3000000000 | bytes 12582912 | tf_op jit(solution)/shard_map/project/pallas_call | solution.py:357
  42.4 1.9 %collective-permute-done.3.nr = bf16[256,1024]{1,0:T(8,128)(2,1)S(1)} collective-permute-done((bf16[256,1024]{1,0:T(8,128)(2,1)S(1)}, bf16[256,1024]{1,0:T(8,128)(2,1)S(1)}, u32[]{:S(2)}, u32[]{:S(2)}) %collective-permute-start.3) | collective-permute-done | bytes 524320 | tf_op jit(solution)/shard_map/ppermute | solution.py:285
  44.3 8.0 %collective-permute-done.2.nl = bf16[256,1024]{1,0:T(8,128)(2,1)S(1)} collective-permute-done((bf16[256,1024]{1,0:T(8,128)(2,1)S(1)}, bf16[256,1024]{1,0:T(8,128)(2,1)S(1)}, u32[]{:S(2)}, u32[]{:S(2)}) %collective-permute-start.2) | collective-permute-done | bytes 524320 | tf_op jit(solution)/shard_map/ppermute | solution.py:284
  52.3 8.5 %window.1 = (bf16[256,1024]{1,0:T(8,128)(2,1)S(1)}, bf16[128,1024]{1,0:T(8,128)(2,1)S(1)}, bf16[128,1024]{1,0:T(8,128)(2,1)S(1)}) custom-call(s32[2]{0:T(128)S(1)} %pad_add_fusion.others_4_.ends, bf16[256,1024]{1,0:T(8,128)(2,1)S(1)} %get-tuple-element.37.q, bf16[256,1024]{1,0:T(8,128)(2,1)S(1)} %get-tuple-element.38.k, ...), custom_call_target="tpu_custom_call" | custom-call | tf_op jit(solution)/shard_map/window/pallas_call | solution.py:367
  60.8 1.9 %collective-permute-start.4 = (bf16[128,1024]{1,0:T(8,128)(2,1)S(1)}, bf16[128,1024]{1,0:T(8,128)(2,1)S(1)}, u32[]{:S(2)}, u32[]{:S(2)}) collective-permute-start(bf16[128,1024]{1,0:T(8,128)(2,1)S(1)} %get-tuple-element.42), channel_id=1, source_target_pairs={{0,1},{1,2},{2,3},{3,4},{4,5},{5,6},{6,7},{7,8},{8,9},{9,10},{10,1... | collective-permute-start | bytes 786440 | tf_op jit(solution)/shard_map/ppermute | solution.py:284
  62.8 8.1 %collective-permute-start.5 = (bf16[128,1024]{1,0:T(8,128)(2,1)S(1)}, bf16[128,1024]{1,0:T(8,128)(2,1)S(1)}, u32[]{:S(2)}, u32[]{:S(2)}) collective-permute-start(bf16[128,1024]{1,0:T(8,128)(2,1)S(1)} %get-tuple-element.43), channel_id=1, source_target_pairs={{1,0},{2,1},{3,2},{4,3},{5,4},{6,5},{7,6},{8,7},{9,8},{10,9},{11,1... | collective-permute-start | bytes 786440 | tf_op jit(solution)/shard_map/ppermute | solution.py:285
  70.9 4.1 %prepare.1 = (f32[16384,128]{1,0:T(8,128)S(1)}, f32[2048,128]{1,0:T(8,128)S(1)}, f32[2048,128]{1,0:T(8,128)S(1)}) custom-call(bf16[256,1024]{1,0:T(8,128)(2,1)S(1)} %get-tuple-element.44.own, bf16[128,2048]{1,0:T(8,128)(2,1)S(1)} %maximum_maximum_fusion.own.state.grid, bf16[128,1024]{1,0:T(8,128)(2,1)S(1)} %get-tuple-element.45.aq, ...), custom_call_target="tpu_custom_call" | custom-call | flops 3000000000 | bytes 12582912 | tf_op jit(solution)/shard_map/prepare/pallas_call | solution.py:383
  75.0 0.0 collective-permute-done.4.left
  75.0 0.0 collective-permute-done.5.right
  75.0 18.7 %decode.1 = bf16[100,2048]{1,0:T(8,128)(2,1)} custom-call(s32[6144]{0:T(1024)S(1)} %mul.29.others_3_.idx, bf16[128,1024]{1,0:T(8,128)(2,1)S(1)} %collective-permute-done.4.left, bf16[128,1024]{1,0:T(8,128)(2,1)S(1)} %collective-permute-done.5.right, f32[2048,128]{1,0:T(8,128)S(1)} %get-tuple-element.48.ko, f32[2048,128]{1,0:T(8,128)S(1)} %get-tuple-element.49.vo, ...), custom_call_target="tpu_custom_call" | custom-call | tf_op jit(solution)/shard_map/decode/pallas_call | solution.py:396
  (10 shorter events, 0.2 us)
Async XLA Ops:
  0.0 12.3 %copy-start.4 = (s32[2048,3]{0,1:T(4,128)S(1)}, s32[2048,3]{0,1:T(4,128)}, u32[]{:S(2)}) copy-start(s32[2048,3]{0,1:T(4,128)} %param.15) | copy-start | bytes 73732
  0.0 12.5 %copy-start.2 = (bf16[100,1024]{1,0:T(8,128)(2,1)S(1)}, bf16[100,1024]{1,0:T(8,128)(2,1)}, u32[]{:S(2)}) copy-start(bf16[100,1024]{1,0:T(8,128)(2,1)} %param.16) | copy-start | bytes 614404
  0.0 12.5 %copy-start.3 = (bf16[1024,100]{0,1:T(8,128)(2,1)S(1)}, bf16[1024,100]{0,1:T(8,128)(2,1)}, u32[]{:S(2)}) copy-start(bf16[1024,100]{0,1:T(8,128)(2,1)} %param.20) | copy-start | bytes 614404
  1.5 16.5 %collective-permute-start.1 = (bf16[128,1024]{1,0:T(8,128)(2,1)S(1)}, bf16[128,1024]{1,0:T(8,128)(2,1)S(1)}, u32[]{:S(2)}, u32[]{:S(2)}) collective-permute-start(bf16[128,1024]{1,0:T(8,128)(2,1)S(1)} %get-tuple-element.53), channel_id=1, source_target_pairs={{1,0},{2,1},{3,2},{4,3},{5,4},{6,5},{7,6},{8,7},{9,8},{10,9},{11,1... | collective-permute-start | bytes 786440 | tf_op jit(solution)/shard_map/ppermute | solution.py:285
  7.9 11.9 %collective-permute-start = (bf16[128,1024]{1,0:T(8,128)(2,1)S(1)}, bf16[128,1024]{1,0:T(8,128)(2,1)S(1)}, u32[]{:S(2)}, u32[]{:S(2)}) collective-permute-start(bf16[128,1024]{1,0:T(8,128)(2,1)S(1)} %get-tuple-element.54), channel_id=1, source_target_pairs={{0,1},{1,2},{2,3},{3,4},{4,5},{5,6},{6,7},{7,8},{8,9},{9,10},{10,1... | collective-permute-start | bytes 786440 | tf_op jit(solution)/shard_map/ppermute | solution.py:284
  12.7 7.2 %copy-start = (bf16[256,1024]{1,0:T(8,128)(2,1)S(1)}, bf16[256,1024]{1,0:T(8,128)(2,1)}, u32[]{:S(2)}) copy-start(bf16[256,1024]{1,0:T(8,128)(2,1)} %lat.3) | copy-start | bytes 1572868
  19.9 1.2 %copy-start.1 = (bf16[16,256,128]{2,1,0:T(8,128)(2,1)S(1)}, bf16[16,256,128]{2,1,0:T(8,128)(2,1)}, u32[]{:S(2)}) copy-start(bf16[16,256,128]{2,1,0:T(8,128)(2,1)} %get-tuple-element.29.qt) | copy-start | bytes 3145732
  31.6 12.7 %collective-permute-start.3 = (bf16[256,1024]{1,0:T(8,128)(2,1)S(1)}, bf16[256,1024]{1,0:T(8,128)(2,1)S(1)}, u32[]{:S(2)}, u32[]{:S(2)}) collective-permute-start(bf16[256,1024]{1,0:T(8,128)(2,1)S(1)} %get-tuple-element.31.normed), channel_id=1, source_target_pairs={{1,0},{2,1},{3,2},{4,3},{5,4},{6,5},{7,6},{8,7},{9,8},{10,9},{11,1... | collective-permute-start | bytes 1572872 | tf_op jit(solution)/shard_map/ppermute | solution.py:285
  37.6 14.7 %collective-permute-start.2 = (bf16[256,1024]{1,0:T(8,128)(2,1)S(1)}, bf16[256,1024]{1,0:T(8,128)(2,1)S(1)}, u32[]{:S(2)}, u32[]{:S(2)}) collective-permute-start(bf16[256,1024]{1,0:T(8,128)(2,1)S(1)} %get-tuple-element.31.normed), channel_id=1, source_target_pairs={{0,1},{1,2},{2,3},{3,4},{4,5},{5,6},{6,7},{7,8},{8,9},{9,10},{10,1... | collective-permute-start | bytes 1572872 | tf_op jit(solution)/shard_map/ppermute | solution.py:284
  60.8 14.1 %collective-permute-start.4 = (bf16[128,1024]{1,0:T(8,128)(2,1)S(1)}, bf16[128,1024]{1,0:T(8,128)(2,1)S(1)}, u32[]{:S(2)}, u32[]{:S(2)}) collective-permute-start(bf16[128,1024]{1,0:T(8,128)(2,1)S(1)} %get-tuple-element.42), channel_id=1, source_target_pairs={{0,1},{1,2},{2,3},{3,4},{4,5},{5,6},{6,7},{7,8},{8,9},{9,10},{10,1... | collective-permute-start | bytes 786440 | tf_op jit(solution)/shard_map/ppermute | solution.py:284
  62.8 12.2 %collective-permute-start.5 = (bf16[128,1024]{1,0:T(8,128)(2,1)S(1)}, bf16[128,1024]{1,0:T(8,128)(2,1)S(1)}, u32[]{:S(2)}, u32[]{:S(2)}) collective-permute-start(bf16[128,1024]{1,0:T(8,128)(2,1)S(1)} %get-tuple-element.43), channel_id=1, source_target_pairs={{1,0},{2,1},{3,2},{4,3},{5,4},{6,5},{7,6},{8,7},{9,8},{10,9},{11,1... | collective-permute-start | bytes 786440 | tf_op jit(solution)/shard_map/ppermute | solution.py:285

commit v4 on v3

--- a/solution.py
+++ b/solution.py
@@ -34,6 +34,10 @@
 
 def low_half(shape):
     return lax.broadcasted_iota(jnp.int32, shape, len(shape) - 1) < SIZE
+
+
+def sides(core, near, far):
+    return jnp.where(core == 0, far, near), jnp.where(core == 0, near, far)
 
 
 def params(mib):
@@ -70,7 +74,7 @@
 
 
 def encode_kernel(
-    idx, left, own, right, qt, bias, av, lat, enc_w, proc_w, dec_w,
+    ends, idx, near, own, far, qt, bias, av, lat, enc_w, proc_w, dec_w,
     latent, normed, pw0, pw1, pw2, pw3, dw0, dw1, dw2, dw3,
     grid, ge0, ge1, z, w3, sems,
 ):
@@ -80,7 +84,8 @@
     rows = lat.shape[0]
     groups = rows // 16
     at = 0
-    for piece in (left, own, right):
+    left, right = sides(ends[2], near[...], far[...])
+    for piece in (left, own[...], right):
         for begin in range(0, piece.shape[1], 512):
             grid[at : at + 512, :] = piece[:, begin : begin + 512].astype(F32).T
             at += 512
@@ -148,7 +153,7 @@
 
 
 def window_kernel(
-    ends, q, k, v, nl, nr, latent, wk, wv, wo, out, head, tail, keys, values, bias, mixed
+    ends, q, k, v, near, far, latent, wk, wv, wo, out, inner, outer, keys, values, bias, mixed
 ):
     rows = q.shape[0]
     half = rows // 2
@@ -161,7 +166,7 @@
         place = col + side * half
         inside = (col >= row) & (col - row <= WIN) & (place >= ends[0]) & (place < ends[1])
         bias[side] = jnp.where(inside, 0.0, NEG)
-    halo = jnp.concatenate([nl[...], nr[...]], axis=0)
+    halo = jnp.concatenate(sides(ends[2], near[...], far[...]), axis=0)
     for weight, wide in ((wk, keys), (wv, values)):
         both = dot(halo, weight[...]).astype(BF)
         wide[:rows, :] = both[:rows]
@@ -172,14 +177,14 @@
         lanes = pl.ds(pl.multiple_of(pair * 128, 128), 128)
         for side in range(2):
             these = slice(side * half, side * half + half)
-            near = slice(side * half, side * half + span)
+            band = slice(side * half, side * half + span)
             both = q[these, lanes]
             zero = jnp.zeros_like(both)
             stacked = jnp.concatenate(
                 [jnp.where(low, both, zero), jnp.where(low, zero, both)], axis=0
             )
-            near_values = values[near, lanes]
-            score = dot_t(stacked, keys[near, lanes]).reshape(2, half, span) + bias[side][None]
+            near_values = values[band, lanes]
+            score = dot_t(stacked, keys[band, lanes]).reshape(2, half, span) + bias[side][None]
             score = score.reshape(2 * half, span)
             expo = jnp.exp2(score - jnp.max(score, axis=1, keepdims=True)).astype(BF)
             total = dot(
@@ -191,8 +196,7 @@
 
     lax.fori_loop(0, PAIRS, one_pair, 0, unroll=True)
     out[...] = (latent[...].astype(F32) + dot(mixed[...], wo[...])).astype(BF)
-    head[...] = out[:BL, :]
-    tail[...] = out[rows - BL :, :]
+    inner[...], outer[...] = sides(ends[2], out[:BL, :], out[rows - BL :, :])
 
 
 CHUNK = 128
@@ -215,11 +219,11 @@
 
 
 def decode_kernel(
-    idx, left, right, ko, vo, q, grid, bo, co, wk, wv, out, kf, vf, prod, wts, dec
+    ends, idx, near, far, ko, vo, q, grid, bo, co, wk, wv, out, kf, vf, prod, wts, dec
 ):
     points = grid.shape[1]
-    side = left.shape[0]
-    halo = jnp.concatenate([left[...], right[...]], axis=0)
+    side = near.shape[0]
+    halo = jnp.concatenate(sides(ends[2], near[...], far[...]), axis=0)
     for weight, tiles, own in ((wk, kf, ko), (wv, vf, vo)):
         tiles[side * 8 : side * 8 + own.shape[0], :] = own[...]
         for block in range(8):
@@ -278,12 +282,15 @@
     return jax.ShapeDtypeStruct(dims, kind)
 
 
-def neighbours(head, tail):
+def swap(inner, outer):
     axes = ("wide", "narrow")
     count = lax.axis_size(axes)
-    after = lax.ppermute(tail, axes, [(i, i + 1) for i in range(count - 1)])
-    before = lax.ppermute(head, axes, [(i + 1, i) for i in range(count - 1)])
-    return after, before
+    pairs = []
+    for i in range(1, count - 1, 2):
+        pairs += [(i, i + 1), (i + 1, i)]
+    far = lax.ppermute(outer, axes, pairs)
+    near = lax.ppermute(inner, "narrow", [(0, 1), (1, 0)])
+    return near, far
 
 
 def on_device(
@@ -315,7 +322,11 @@
         ],
         axis=0,
     )
-    grid_left, grid_right = neighbours(grid[:, :BG], grid[:, points - BG :])
+    core = lax.axis_index("narrow")
+    grid_near, grid_far = swap(
+        lax.dynamic_slice_in_dim(grid, (1 - core) * (points - BG), BG, 1),
+        lax.dynamic_slice_in_dim(grid, core * (points - BG), BG, 1),
+    )
     win = jnp.pad(w_in, ((0, CPAD - channels), (0, 0)))
     wout = jnp.pad(w_out.T, ((0, CPAD - channels), (0, 0)))
     scale = jnp.repeat(logit_scale * (LOG2E / math.sqrt(SIZE)), SIZE, axis=1)
@@ -324,7 +335,7 @@
     bias = jnp.where(live, 0.0, NEG).astype(F32)
     bias = bias.reshape(slots, rows // 16, 16).transpose(1, 0, 2).reshape(rows // 16, slots * 16)
     dec_idx = jnp.clip(dec_src.T - (place * rows - BL), 0, rows + 2 * BL - 1).reshape(-1) * 8
-    ends = jnp.stack([WIN // 2 - place * rows, total + WIN // 2 - place * rows])
+    ends = jnp.stack([WIN // 2 - place * rows, total + WIN // 2 - place * rows, core])
 
     qt, av = pl.pallas_call(
         fold_kernel,
@@ -340,7 +351,7 @@
     latent, normed, pw0, pw1, pw2, pw3, dw0, dw1, dw2, dw3 = pl.pallas_call(
         encode_kernel,
         out_shape=(shape((rows, width)),) * 2 + (square,) * 8,
-        in_specs=[SM] + [VM] * 7 + [HBM] * 3,
+        in_specs=[SM] * 2 + [VM] * 7 + [HBM] * 3,
         out_specs=(VM,) * 10,
         scratch_shapes=[
             pltpu.VMEM((points + 2 * BG, CPAD), F32),
@@ -352,8 +363,8 @@
         ],
         compiler_params=params(28),
         name="encode",
-    )(enc_idx, grid_left, grid, grid_right, qt, bias, av, latent_init, enc_w, proc_w, dec_w)
-    near_left, near_right = neighbours(normed, normed)
+    )(ends, enc_idx, grid_near, grid, grid_far, qt, bias, av, latent_init, enc_w, proc_w, dec_w)
+    normed_near, normed_far = swap(normed, normed)
     q, k, v, aq, bo, co = pl.pallas_call(
         project_kernel,
         out_shape=(shape((rows, width)),) * 3
@@ -364,7 +375,7 @@
         cost_estimate=pl.CostEstimate(flops=3 * 10**9, bytes_accessed=12 * 2**20, transcendentals=0),
         name="project",
     )(normed, win, wout, scale, pw0, pw1, pw2, dw0, dw3)
-    latent_out, mesh_head, mesh_tail = pl.pallas_call(
+    latent_out, mesh_inner, mesh_outer = pl.pallas_call(
         window_kernel,
         out_shape=(shape((rows, width)), shape((BL, width)), shape((BL, width))),
         in_specs=[SM] + [VM] * 9,
@@ -377,8 +388,8 @@
         ],
         compiler_params=params(24),
         name="window",
-    )(ends, q, k, v, near_left, near_right, latent, pw1, pw2, pw3)
-    mesh_left, mesh_right = neighbours(mesh_head, mesh_tail)
+    )(ends, q, k, v, normed_near, normed_far, latent, pw1, pw2, pw3)
+    mesh_near, mesh_far = swap(mesh_inner, mesh_outer)
     nodes = rows + 2 * BL
     dq, dk, dv = pl.pallas_call(
         prepare_kernel,
@@ -396,7 +407,7 @@
     out = pl.pallas_call(
         decode_kernel,
         out_shape=shape((channels, points)),
-        in_specs=[SM] + [VM] * 10,
+        in_specs=[SM] * 2 + [VM] * 10,
         out_specs=VM,
         scratch_shapes=[
             pltpu.VMEM((nodes * 8, 128), F32),
@@ -407,7 +418,7 @@
         ],
         compiler_params=params(32),
         name="decode",
-    )(dec_idx, mesh_left, mesh_right, dk, dv, dq, grid, bo, co, dw1, dw2)
+    )(ends, dec_idx, mesh_near, mesh_far, dk, dv, dq, grid, bo, co, dw1, dw2)
     return out.T
 
 

time: 95.2 us -> 81.5 us (0.86); the launches traced: 93.6 us -> 81.2 us
  starting transfers between devices: 26.5 us -> 15.8 us
  waiting for transfers between devices: 11.8 us -> 10.6 us
    ppermute x6, starting transfers between devices: 26.5 us -> 15.8 us  [the longest x3 15.3 us: swap(): far = lax.ppermute(outer, axes, pairs)]
    ppermute x6, waiting for transfers between devices: 11.8 us -> 10.6 us  [the longest x3 10.6 us: swap(): far = lax.ppermute(outer, axes, pairs)]
  transfers between devices with their start and end apart: 6 -> 6, of which waited for: 3 -> 2; matrix products, arithmetic and copies ran while one was open for 3% -> 2% of each run, Pallas kernels for 13% -> 15%
where the time goes in v4:
time: 81.5 us; the launch traced here: 81.2 us
  Pallas kernels  49.9 us (61%)
  starting transfers between devices  15.8 us (19%)
  waiting for transfers between devices  10.6 us (13%)
  local copies, waits for them, and re-layouts  2.62 us (3%)
  other arithmetic  2.12 us (3%)
    pallas_call x1, Pallas kernels, on_device(): pl.pallas_call(decode_kernel, out_shape=shape((channels, points)), in_spe...  18.7 us
    ppermute x3, starting transfers between devices, swap(): far = lax.ppermute(outer, axes, pairs)  15.3 us
    ppermute x3, waiting for transfers between devices, swap(): far = lax.ppermute(outer, axes, pairs)  10.6 us
    pallas_call x1, Pallas kernels, on_device(): pl.pallas_call(encode_kernel, out_shape=(shape((rows, width)),) * 2 + (sq...  10.5 us
    pallas_call x1, Pallas kernels, on_device(): pl.pallas_call(window_kernel, out_shape=(shape((rows, width)), shape((BL,...  8.58 us
    pallas_call x1, Pallas kernels, on_device(): pl.pallas_call(fold_kernel, out_shape=(shape((HEADS, rows, CPAD)), shape(...  5.34 us
    pallas_call x1, Pallas kernels, on_device(): pl.pallas_call(prepare_kernel, out_shape=(shape((points * 8, 128), F32),...  4.11 us
    pallas_call x1, Pallas kernels, on_device(): pl.pallas_call(project_kernel, out_shape=(shape((rows, width)),) * 3 + (s...  2.71 us
  transfers between devices with their start and end apart: 6, of which 2 were waited for; matrix products, arithmetic and copies ran while one was open for 2% of the time, Pallas kernels for 15%

profile of v4, /device:TPU:96, one launch (start us, length us, event | category | flops | bytes accessed | tf_op | source)
XLA Modules:
  0.0 81.2 jit_solution(10054791588971147883)
XLA Ops:
  0.0 0.0 copy-start.5
  0.0 0.0 copy-start.4
  0.0 0.0 copy-start.2
  0.0 0.0 copy-start.3
  0.0 0.1 pad.10.clone
  0.1 0.1 pad.11.clone
  0.2 1.3 %maximum_maximum_fusion.own.state.grid = bf16[128,2048]{1,0:T(8,128)(2,1)S(1)} fusion(bf16[100,2048]{1,0:T(8,128)(2,1)} %bitcast.15, bf16[128]{0:T(256)(128)(2,1)S(1)} %pad.11.clone, bf16[128]{0:T(256)(128)(2,1)S(1)} %pad.10.clone), kind=kLoop, calls=%fused_computation | loop fusion | flops 1572864 | bytes 934400 | tf_op jit(solution)/shard_map/concatenate | solution.py:317
  1.6 6.4 %collective-permute-start.1 = (bf16[128,1024]{1,0:T(8,128)(2,1)S(1)}, bf16[128,1024]{1,0:T(8,128)(2,1)S(1)}, u32[]{:S(2)}, u32[]{:S(2)}) collective-permute-start(bf16[128,1024]{1,0:T(8,128)(2,1)S(1)} %get-tuple-element.53), channel_id=1, source_target_pairs={{1,2},{2,1},{3,4},{4,3},{5,6},{6,5},{7,8},{8,7},{9,10},{10,9},{11,... | collective-permute-start | bytes 786440 | tf_op jit(solution)/shard_map/ppermute | solution.py:291
  8.0 0.1 collective-permute-start
  8.1 0.7 broadcast_multiply_fusion
  8.8 0.8 lt.35
  9.5 0.1 lt.33
  9.6 0.0 copy-done.5
  9.6 0.1 broadcast_in_dim.21
  9.7 0.1 reshape.23.scale
  9.8 0.0 copy-done.4
  9.9 0.1 lt.37
  10.0 0.0 copy-done.2
  10.0 0.0 copy-done.3
  10.1 0.1 pad_add_fusion.others_4_.ends
  10.2 0.0 copy-start
  10.2 5.3 %fold.1 = (bf16[16,256,128]{2,1,0:T(8,128)(2,1)}, bf16[128,1024]{1,0:T(8,128)(2,1)S(1)}) custom-call(bf16[128,1024]{1,0:T(8,128)(2,1)S(1)} %pad.7.win, bf16[4,1024,1024]{2,1,0:T(8,128)(2,1)} %enc_w.3, bf16[256,1024]{1,0:T(8,128)(2,1)} %lat.3, f32[3,1024]{1,0:T(4,128)S(1)} %reshape.23.scale, bf16[128,1024]{1,0:T(8,128)(2,1)S(1)} %pad.8.others_0_.wout, ...), custom_call_target="tpu_custom_call" | custom-call | flops 2000000000 | bytes 8388608 | tf_op jit(solution)/shard_map/fold/pallas_call | solution.py:340
  15.5 0.0 collective-permute-done.1.far
  15.5 0.0 collective-permute-done.near
  15.5 0.0 copy-done
  15.5 0.0 copy-start.1
  15.5 1.2 %copy-done.1 = bf16[16,256,128]{2,1,0:T(8,128)(2,1)S(1)} copy-done((bf16[16,256,128]{2,1,0:T(8,128)(2,1)S(1)}, bf16[16,256,128]{2,1,0:T(8,128)(2,1)}, u32[]{:S(2)}) %copy-start.1) | copy-done | bytes 1048600
  16.8 10.5 %encode.1 = (bf16[256,1024]{1,0:T(8,128)(2,1)S(1)}, bf16[256,1024]{1,0:T(8,128)(2,1)S(1)}, bf16[1024,1024]{1,0:T(8,128)(2,1)S(1)}, bf16[1024,1024]{1,0:T(8,128)(...) custom-call(s32[3]{0:T(128)S(1)} %pad_add_fusion.others_4_.ends, ...), custom_call_target="tpu_custom_call" | custom-call | tf_op jit(solution)/shard_map/encode/pallas_call | solution.py:351
  27.2 4.4 %collective-permute-start.3 = (bf16[256,1024]{1,0:T(8,128)(2,1)S(1)}, bf16[256,1024]{1,0:T(8,128)(2,1)S(1)}, u32[]{:S(2)}, u32[]{:S(2)}) collective-permute-start(bf16[256,1024]{1,0:T(8,128)(2,1)S(1)} %get-tuple-element.31.normed), channel_id=1, source_target_pairs={{1,2},{2,1},{3,4},{4,3},{5,6},{6,5},{7,8},{8,7},{9,10},{10,9},{11,... | collective-permute-start | bytes 1572872 | tf_op jit(solution)/shard_map/ppermute | solution.py:291
  31.6 0.3 collective-permute-start.2
  31.9 2.7 %project.1 = (bf16[256,1024]{1,0:T(8,128)(2,1)S(1)}, bf16[256,1024]{1,0:T(8,128)(2,1)S(1)}, bf16[256,1024]{1,0:T(8,128)(2,1)S(1)}, bf16[128,1024]{1,0:T(8,128)(2...) custom-call(bf16[256,1024]{1,0:T(8,128)(2,1)S(1)} %get-tuple-element.31.normed, ...), custom_call_target="tpu_custom_call" | custom-call | flops 3000000000 | bytes 12582912 | tf_op jit(solution)/shard_map/project/pallas_call | solution.py:368
  34.6 7.4 %collective-permute-done.3.far = bf16[256,1024]{1,0:T(8,128)(2,1)S(1)} collective-permute-done((bf16[256,1024]{1,0:T(8,128)(2,1)S(1)}, bf16[256,1024]{1,0:T(8,128)(2,1)S(1)}, u32[]{:S(2)}, u32[]{:S(2)}) %collective-permute-start.3) | collective-permute-done | bytes 524320 | tf_op jit(solution)/shard_map/ppermute | solution.py:291
  42.0 0.0 collective-permute-done.2.near
  42.0 8.6 %window.1 = (bf16[256,1024]{1,0:T(8,128)(2,1)S(1)}, bf16[128,1024]{1,0:T(8,128)(2,1)S(1)}, bf16[128,1024]{1,0:T(8,128)(2,1)S(1)}) custom-call(s32[3]{0:T(128)S(1)} %pad_add_fusion.others_4_.ends, bf16[256,1024]{1,0:T(8,128)(2,1)S(1)} %get-tuple-element.37.q, bf16[256,1024]{1,0:T(8,128)(2,1)S(1)} %get-tuple-element.38.k, ...), custom_call_target="tpu_custom_call" | custom-call | tf_op jit(solution)/shard_map/window/pallas_call | solution.py:378
  50.5 0.1 collective-permute-start.4
  50.6 4.6 %collective-permute-start.5 = (bf16[128,1024]{1,0:T(8,128)(2,1)S(1)}, bf16[128,1024]{1,0:T(8,128)(2,1)S(1)}, u32[]{:S(2)}, u32[]{:S(2)}) collective-permute-start(bf16[128,1024]{1,0:T(8,128)(2,1)S(1)} %get-tuple-element.43), channel_id=1, source_target_pairs={{1,2},{2,1},{3,4},{4,3},{5,6},{6,5},{7,8},{8,7},{9,10},{10,9},{11,... | collective-permute-start | bytes 786440 | tf_op jit(solution)/shard_map/ppermute | solution.py:291
  55.2 4.1 %prepare.1 = (f32[16384,128]{1,0:T(8,128)S(1)}, f32[2048,128]{1,0:T(8,128)S(1)}, f32[2048,128]{1,0:T(8,128)S(1)}) custom-call(bf16[256,1024]{1,0:T(8,128)(2,1)S(1)} %get-tuple-element.44.own, bf16[128,2048]{1,0:T(8,128)(2,1)S(1)} %maximum_maximum_fusion.own.state.grid, bf16[128,1024]{1,0:T(8,128)(2,1)S(1)} %get-tuple-element.45.aq, ...), custom_call_target="tpu_custom_call" | custom-call | flops 3000000000 | bytes 12582912 | tf_op jit(solution)/shard_map/prepare/pallas_call | solution.py:394
  59.3 0.0 collective-permute-done.4.near
  59.3 3.2 %collective-permute-done.5.far = bf16[128,1024]{1,0:T(8,128)(2,1)S(1)} collective-permute-done((bf16[128,1024]{1,0:T(8,128)(2,1)S(1)}, bf16[128,1024]{1,0:T(8,128)(2,1)S(1)}, u32[]{:S(2)}, u32[]{:S(2)}) %collective-permute-start.5) | collective-permute-done | bytes 262176 | tf_op jit(solution)/shard_map/ppermute | solution.py:291
  62.5 18.7 %decode.1 = bf16[100,2048]{1,0:T(8,128)(2,1)} custom-call(s32[3]{0:T(128)S(1)} %pad_add_fusion.others_4_.ends, s32[6144]{0:T(1024)S(1)} %mul.35.others_3_.idx, bf16[128,1024]{1,0:T(8,128)(2,1)S(1)} %collective-permute-done.4.near, bf16[128,1024]{1,0:T(8,128)(2,1)S(1)} %collective-permute-done.5.far, f32[2048,128]{1,0:T(8,128)S(1)} %get-tuple-element.48.ko, ...), custom_call_target="tpu_custom_call" | custom-call | tf_op jit(solution)/shard_map/decode/pallas_call | solution.py:407
  (11 shorter events, 0.2 us)
Async XLA Ops:
  0.0 9.6 %copy-start.5 = (s32[256,16]{0,1:T(8,128)S(1)}, s32[256,16]{0,1:T(8,128)}, u32[]{:S(2)}) copy-start(s32[256,16]{0,1:T(8,128)} %param.13) | copy-start | bytes 49156
  0.0 9.8 %copy-start.4 = (s32[2048,3]{0,1:T(4,128)S(1)}, s32[2048,3]{0,1:T(4,128)}, u32[]{:S(2)}) copy-start(s32[2048,3]{0,1:T(4,128)} %param.15) | copy-start | bytes 73732
  0.0 10.0 %copy-start.2 = (bf16[100,1024]{1,0:T(8,128)(2,1)S(1)}, bf16[100,1024]{1,0:T(8,128)(2,1)}, u32[]{:S(2)}) copy-start(bf16[100,1024]{1,0:T(8,128)(2,1)} %param.16) | copy-start | bytes 614404
  0.0 10.0 %copy-start.3 = (bf16[1024,100]{0,1:T(8,128)(2,1)S(1)}, bf16[1024,100]{0,1:T(8,128)(2,1)}, u32[]{:S(2)}) copy-start(bf16[1024,100]{0,1:T(8,128)(2,1)} %param.20) | copy-start | bytes 614404
  1.6 13.9 %collective-permute-start.1 = (bf16[128,1024]{1,0:T(8,128)(2,1)S(1)}, bf16[128,1024]{1,0:T(8,128)(2,1)S(1)}, u32[]{:S(2)}, u32[]{:S(2)}) collective-permute-start(bf16[128,1024]{1,0:T(8,128)(2,1)S(1)} %get-tuple-element.53), channel_id=1, source_target_pairs={{1,2},{2,1},{3,4},{4,3},{5,6},{6,5},{7,8},{8,7},{9,10},{10,9},{11,... | collective-permute-start | bytes 786440 | tf_op jit(solution)/shard_map/ppermute | solution.py:291
  8.0 7.5 %collective-permute-start = (bf16[128,1024]{1,0:T(8,128)(2,1)S(1)}, bf16[128,1024]{1,0:T(8,128)(2,1)S(1)}, u32[]{:S(2)}, u32[]{:S(2)}) collective-permute-start(bf16[128,1024]{1,0:T(8,128)(2,1)S(1)} %get-tuple-element.54), channel_id=1, source_target_pairs={{0,1},{1,0},{2,3},{3,2},{4,5},{5,4},{6,7},{7,6},{8,9},{9,8},{10,11... | collective-permute-start | bytes 786440 | tf_op jit(solution)/shard_map/ppermute | solution.py:292
  10.2 5.4 %copy-start = (bf16[256,1024]{1,0:T(8,128)(2,1)S(1)}, bf16[256,1024]{1,0:T(8,128)(2,1)}, u32[]{:S(2)}) copy-start(bf16[256,1024]{1,0:T(8,128)(2,1)} %lat.3) | copy-start | bytes 1572868
  15.5 1.2 %copy-start.1 = (bf16[16,256,128]{2,1,0:T(8,128)(2,1)S(1)}, bf16[16,256,128]{2,1,0:T(8,128)(2,1)}, u32[]{:S(2)}) copy-start(bf16[16,256,128]{2,1,0:T(8,128)(2,1)} %get-tuple-element.29.qt) | copy-start | bytes 3145732
  27.2 14.7 %collective-permute-start.3 = (bf16[256,1024]{1,0:T(8,128)(2,1)S(1)}, bf16[256,1024]{1,0:T(8,128)(2,1)S(1)}, u32[]{:S(2)}, u32[]{:S(2)}) collective-permute-start(bf16[256,1024]{1,0:T(8,128)(2,1)S(1)} %get-tuple-element.31.normed), channel_id=1, source_target_pairs={{1,2},{2,1},{3,4},{4,3},{5,6},{6,5},{7,8},{8,7},{9,10},{10,9},{11,... | collective-permute-start | bytes 1572872 | tf_op jit(solution)/shard_map/ppermute | solution.py:291
  31.6 10.4 %collective-permute-start.2 = (bf16[256,1024]{1,0:T(8,128)(2,1)S(1)}, bf16[256,1024]{1,0:T(8,128)(2,1)S(1)}, u32[]{:S(2)}, u32[]{:S(2)}) collective-permute-start(bf16[256,1024]{1,0:T(8,128)(2,1)S(1)} %get-tuple-element.31.normed), channel_id=1, source_target_pairs={{0,1},{1,0},{2,3},{3,2},{4,5},{5,4},{6,7},{7,6},{8,9},{9,8},{10,11... | collective-permute-start | bytes 1572872 | tf_op jit(solution)/shard_map/ppermute | solution.py:292
  50.5 8.8 %collective-permute-start.4 = (bf16[128,1024]{1,0:T(8,128)(2,1)S(1)}, bf16[128,1024]{1,0:T(8,128)(2,1)S(1)}, u32[]{:S(2)}, u32[]{:S(2)}) collective-permute-start(bf16[128,1024]{1,0:T(8,128)(2,1)S(1)} %get-tuple-element.42), channel_id=1, source_target_pairs={{0,1},{1,0},{2,3},{3,2},{4,5},{5,4},{6,7},{7,6},{8,9},{9,8},{10,11... | collective-permute-start | bytes 786440 | tf_op jit(solution)/shard_map/ppermute | solution.py:292
  50.6 11.9 %collective-permute-start.5 = (bf16[128,1024]{1,0:T(8,128)(2,1)S(1)}, bf16[128,1024]{1,0:T(8,128)(2,1)S(1)}, u32[]{:S(2)}, u32[]{:S(2)}) collective-permute-start(bf16[128,1024]{1,0:T(8,128)(2,1)S(1)} %get-tuple-element.43), channel_id=1, source_target_pairs={{1,2},{2,1},{3,4},{4,3},{5,6},{6,5},{7,8},{8,7},{9,10},{10,9},{11,... | collective-permute-start | bytes 786440 | tf_op jit(solution)/shard_map/ppermute | solution.py:291

commit v5 on v4

--- a/solution.py
+++ b/solution.py
@@ -14,6 +14,7 @@
 SIZE = 64
 PAIRS = HEADS // 2
 CPAD = 128
+CSENT = 112
 LOG2E = math.log2(math.e)
 NEG = -1e30
 BF = jnp.bfloat16
@@ -55,8 +56,8 @@
 
 
 def fold_kernel(win, enc_w, lat, scale, *others):
-    qt, av, w0, w1, w2, sems = others[-6:]
-    got = fetch(enc_w, (1, 0, 2), (w1, w0, w2), sems)
+    qt, w0, w1, sems = others[-4:]
+    got = fetch(enc_w, (1, 0), (w1, w0), sems)
     got[0].wait()
     ak = dot(win[...], w1[...]).astype(BF)
     got[1].wait()
@@ -69,25 +70,25 @@
         zero = jnp.zeros_like(both)
         qt[2 * pair] = dot_t(jnp.where(low, both, zero), keys).astype(BF)
         qt[2 * pair + 1] = dot_t(jnp.where(low, zero, both), keys).astype(BF)
-    got[2].wait()
-    av[...] = dot(win[...], w2[...]).astype(BF)
 
 
 def encode_kernel(
-    ends, idx, near, own, far, qt, bias, av, lat, enc_w, proc_w, dec_w,
+    ends, idx, near, own, far, qt, bias, win, lat, enc_w, proc_w, dec_w,
     latent, normed, pw0, pw1, pw2, pw3, dw0, dw1, dw2, dw3,
-    grid, ge0, ge1, z, w3, sems,
+    grid, ge0, ge1, ge2, ge3, z, w2, w3, sems,
 ):
-    got = fetch(enc_w, (3,), (w3,), sems.at[pl.ds(0, 1)])
-    later = fetch(proc_w, (0, 1, 2, 3), (pw0, pw1, pw2, pw3), sems.at[pl.ds(1, 4)])
-    later += fetch(dec_w, (0, 3, 1, 2), (dw0, dw3, dw1, dw2), sems.at[pl.ds(5, 4)])
+    got = fetch(enc_w, (2, 3), (w2, w3), sems.at[pl.ds(8, 2)])
+    later = fetch(proc_w, (0, 1, 2, 3), (pw0, pw1, pw2, pw3), sems.at[pl.ds(0, 4)])
+    later += fetch(dec_w, (0, 3, 1, 2), (dw0, dw3, dw1, dw2), sems.at[pl.ds(4, 4)])
     rows = lat.shape[0]
     groups = rows // 16
     at = 0
     left, right = sides(ends[2], near[...], far[...])
-    for piece in (left, own[...], right):
+    empty = jnp.zeros((CPAD - CSENT, 512), BF)
+    for piece in (left, own[:CSENT, :], right):
         for begin in range(0, piece.shape[1], 512):
-            grid[at : at + 512, :] = piece[:, begin : begin + 512].astype(F32).T
+            part = jnp.concatenate([piece[:, begin : begin + 512], empty], axis=0)
+            grid[at : at + 512, :] = part.astype(F32).T
             at += 512
     row = lax.broadcasted_iota(jnp.int32, (256, 256), 0)
     col = lax.broadcasted_iota(jnp.int32, (256, 256), 1)
@@ -100,27 +101,30 @@
                 edge = slot * 16 + node
                 ge[pl.ds(edge, 1), :] = grid[pl.ds(idx[base + (slot * rows + node)], 1), :]
 
-    def attend(number, ge):
-        points = ge[...].astype(BF)
-        base = pl.multiple_of(number * 16, 16)
-        queries = qt[:, pl.ds(base, 16), :].reshape(256, CPAD)
-        score = dot_t(queries, points) + (diag + bias[pl.ds(number, 1), :])
-        expo = jnp.exp2(score - jnp.max(score, axis=1, keepdims=True)).astype(BF)
-        mixed = dot(expo, points)
-        mixed = mixed / mixed[:, 100:101]
-        z[:, pl.ds(base, 16), :] = mixed.reshape(16, 16, CPAD).astype(BF)
-
-    collect(0, ge0)
-
-    def two_groups(step, carry):
-        number = step * 2
-        attend(number, ge0)
-        collect(number + 1, ge1)
-        attend(number + 1, ge1)
-        collect(jnp.minimum(number + 2, groups - 1), ge0)
-        return carry
-
-    lax.fori_loop(0, groups // 2, two_groups, 0)
+    def attend(numbers, buffers):
+        points = [ge[...].astype(BF) for ge in buffers]
+        score = [
+            dot_t(qt[:, number * 16 : number * 16 + 16, :].reshape(256, CPAD), rows_of)
+            + (diag + bias[number : number + 1, :])
+            for number, rows_of in zip(numbers, points)
+        ]
+        expo = [
+            jnp.exp2(part - jnp.max(part, axis=1, keepdims=True)).astype(BF) for part in score
+        ]
+        for number, part, rows_of in zip(numbers, expo, points):
+            mixed = dot(part, rows_of)
+            mixed = mixed * (1.0 / mixed[:, 100:101])
+            z[:, number * 16 : number * 16 + 16, :] = mixed.reshape(16, 16, CPAD).astype(BF)
+
+    buffers = ((ge0, ge1), (ge2, ge3))
+    for number in range(0, groups + 2, 2):
+        if number < groups:
+            for at in range(2):
+                collect(number + at, buffers[number // 2 % 2][at])
+        if number:
+            attend((number - 2, number - 1), buffers[(number // 2 + 1) % 2])
+    got[0].wait()
+    av = dot(win[...], w2[...]).astype(BF)
     low = low_half((1, 128))
     parts = []
     for pair in range(PAIRS):
@@ -131,7 +135,7 @@
             + dot(z[2 * pair + 1], jnp.where(low, zero, values))
         )
     encoded = jnp.concatenate(parts, axis=1).astype(BF)
-    got[0].wait()
+    got[1].wait()
     rounded = (lat[...].astype(F32) + dot(encoded, w3[...])).astype(BF)
     latent[...] = rounded
     wide = rounded.astype(F32)
@@ -173,28 +177,32 @@
         wide[2 * rows :, :] = both[rows:]
     low = low_half((1, 128))
 
-    def one_pair(pair, carry):
-        lanes = pl.ds(pl.multiple_of(pair * 128, 128), 128)
+    for pair in range(PAIRS):
+        lanes = slice(pair * 128, pair * 128 + 128)
+        bands = [slice(side * half, side * half + span) for side in range(2)]
+        score = []
         for side in range(2):
-            these = slice(side * half, side * half + half)
-            band = slice(side * half, side * half + span)
-            both = q[these, lanes]
+            both = q[side * half : side * half + half, lanes]
             zero = jnp.zeros_like(both)
             stacked = jnp.concatenate(
                 [jnp.where(low, both, zero), jnp.where(low, zero, both)], axis=0
             )
-            near_values = values[band, lanes]
-            score = dot_t(stacked, keys[band, lanes]).reshape(2, half, span) + bias[side][None]
-            score = score.reshape(2 * half, span)
-            expo = jnp.exp2(score - jnp.max(score, axis=1, keepdims=True)).astype(BF)
+            part = dot_t(stacked, keys[bands[side], lanes])
+            score.append(
+                (part.reshape(2, half, span) + bias[side][None]).reshape(2 * half, span)
+            )
+        expo = [
+            jnp.exp2(part - jnp.max(part, axis=1, keepdims=True)).astype(BF) for part in score
+        ]
+        for side in range(2):
+            near_values = values[bands[side], lanes]
             total = dot(
-                expo, jnp.concatenate([near_values, jnp.ones_like(near_values)], axis=1)
+                expo[side], jnp.concatenate([near_values, jnp.ones_like(near_values)], axis=1)
             )
-            part = total[:, :128] / total[:, 128:]
-            mixed[these, lanes] = jnp.where(low, part[:half], part[half:]).astype(BF)
-        return carry
-
-    lax.fori_loop(0, PAIRS, one_pair, 0, unroll=True)
+            part = total[:, :128] * (1.0 / total[:, 128:])
+            mixed[side * half : side * half + half, lanes] = jnp.where(
+                low, part[:half], part[half:]
+            ).astype(BF)
     out[...] = (latent[...].astype(F32) + dot(mixed[...], wo[...])).astype(BF)
     inner[...], outer[...] = sides(ends[2], out[:BL, :], out[rows - BL :, :])
 
@@ -205,7 +213,7 @@
 def to_tiles(rows, weight, tiles, begin):
     count = rows.shape[0]
     for block in range(8):
-        tiles[pl.ds(begin * 8 + block, count, stride=8), :] = dot(
+        tiles[begin : begin + count, block, :] = dot(
             rows, weight[:, block * 128 : block * 128 + 128]
         )
 
@@ -225,11 +233,11 @@
     side = near.shape[0]
     halo = jnp.concatenate(sides(ends[2], near[...], far[...]), axis=0)
     for weight, tiles, own in ((wk, kf, ko), (wv, vf, vo)):
-        tiles[side * 8 : side * 8 + own.shape[0], :] = own[...]
+        tiles[side : side + own.shape[0]] = own[...]
         for block in range(8):
             both = dot(halo, weight[:, block * 128 : block * 128 + 128])
-            tiles[pl.ds(block, side, stride=8), :] = both[:side]
-            tiles[pl.ds(side * 8 + own.shape[0] + block, side, stride=8), :] = both[side:]
+            tiles[:side, block, :] = both[:side]
+            tiles[side + own.shape[0] :, block, :] = both[side:]
     head_row = lax.broadcasted_iota(jnp.int32, (256, 256), 0) // SIZE
     head_col = lax.broadcasted_iota(jnp.int32, (256, 256), 1) // SIZE
     ones = jnp.where(head_row == head_col, 1.0, 0.0).astype(BF)
@@ -239,11 +247,11 @@
         first = pl.multiple_of(number * CHUNK, CHUNK)
 
         def tile_of(tiles, edge, at):
-            return tiles[pl.ds(pl.multiple_of(idx[edge * points + first + at], 8), 8), :]
+            return tiles[idx[edge * points + first + at]]
 
         for quad in range(0, CHUNK, 4):
             mine = [
-                q[pl.ds(pl.multiple_of((first + quad + at) * 8, 8), 8), :] for at in range(4)
+                q[first + quad + at] for at in range(4)
             ]
             for edge in range(3):
                 terms = [mine[at] * tile_of(kf, edge, quad + at) for at in range(4)]
@@ -265,14 +273,14 @@
             for edge in range(3):
                 term = wts[edge, top : top + 8, lane : lane + 128] * tile_of(vf, edge, at)
                 total = term if total is None else total + term
-            dec[pl.ds(pl.multiple_of((first + at) * 8, 8), 8), :] = total
+            dec[first + at] = total
         return carry
 
     lax.fori_loop(0, points // CHUNK, one_chunk, 0)
     block = 256
     for first in range(0, points, block):
         wide = jnp.concatenate(
-            [dec[pl.ds(first * 8 + part, block, stride=8), :] for part in range(8)], axis=1
+            [dec[first : first + block, part, :] for part in range(8)], axis=1
         ).astype(BF)
         result = dot(wide, bo[...]).T + dot(co[...], grid[:, first : first + block])
         out[:, first : first + block] = result[: out.shape[0], :].astype(BF)
@@ -324,8 +332,8 @@
     )
     core = lax.axis_index("narrow")
     grid_near, grid_far = swap(
-        lax.dynamic_slice_in_dim(grid, (1 - core) * (points - BG), BG, 1),
-        lax.dynamic_slice_in_dim(grid, core * (points - BG), BG, 1),
+        lax.dynamic_slice_in_dim(grid[:CSENT], (1 - core) * (points - BG), BG, 1),
+        lax.dynamic_slice_in_dim(grid[:CSENT], core * (points - BG), BG, 1),
     )
     win = jnp.pad(w_in, ((0, CPAD - channels), (0, 0)))
     wout = jnp.pad(w_out.T, ((0, CPAD - channels), (0, 0)))
@@ -334,15 +342,15 @@
     live = jnp.arange(slots, dtype=jnp.int32)[:, None] < enc_count[None, :]
     bias = jnp.where(live, 0.0, NEG).astype(F32)
     bias = bias.reshape(slots, rows // 16, 16).transpose(1, 0, 2).reshape(rows // 16, slots * 16)
-    dec_idx = jnp.clip(dec_src.T - (place * rows - BL), 0, rows + 2 * BL - 1).reshape(-1) * 8
+    dec_idx = jnp.clip(dec_src.T - (place * rows - BL), 0, rows + 2 * BL - 1).reshape(-1)
     ends = jnp.stack([WIN // 2 - place * rows, total + WIN // 2 - place * rows, core])
 
-    qt, av = pl.pallas_call(
+    qt = pl.pallas_call(
         fold_kernel,
-        out_shape=(shape((HEADS, rows, CPAD)), shape((CPAD, width))),
+        out_shape=shape((HEADS, rows, CPAD)),
         in_specs=[VM, HBM, VM, VM] + [pl.BlockSpec(memory_space=pl.ANY)] * 5,
-        out_specs=(VM, VM),
-        scratch_shapes=[weight] * 3 + [dma((3,))],
+        out_specs=VM,
+        scratch_shapes=[weight] * 2 + [dma((2,))],
         compiler_params=params(53),
         cost_estimate=pl.CostEstimate(flops=2 * 10**9, bytes_accessed=8 * 2**20, transcendentals=0),
         name="fold",
@@ -357,13 +365,16 @@
             pltpu.VMEM((points + 2 * BG, CPAD), F32),
             pltpu.VMEM((slots * 16, CPAD), F32),
             pltpu.VMEM((slots * 16, CPAD), F32),
+            pltpu.VMEM((slots * 16, CPAD), F32),
+            pltpu.VMEM((slots * 16, CPAD), F32),
             pltpu.VMEM((HEADS, rows, CPAD), BF),
             weight,
-            dma((9,)),
+            weight,
+            dma((10,)),
         ],
         compiler_params=params(28),
         name="encode",
-    )(ends, enc_idx, grid_near, grid, grid_far, qt, bias, av, latent_init, enc_w, proc_w, dec_w)
+    )(ends, enc_idx, grid_near, grid, grid_far, qt, bias, win, latent_init, enc_w, proc_w, dec_w)
     normed_near, normed_far = swap(normed, normed)
     q, k, v, aq, bo, co = pl.pallas_call(
         project_kernel,
@@ -394,9 +405,9 @@
     dq, dk, dv = pl.pallas_call(
         prepare_kernel,
         out_shape=(
-            shape((points * 8, 128), F32),
-            shape((rows * 8, 128), F32),
-            shape((rows * 8, 128), F32),
+            shape((points, 8, 128), F32),
+            shape((rows, 8, 128), F32),
+            shape((rows, 8, 128), F32),
         ),
         in_specs=[VM] * 5,
         out_specs=(VM,) * 3,
@@ -410,11 +421,11 @@
         in_specs=[SM] * 2 + [VM] * 10,
         out_specs=VM,
         scratch_shapes=[
-            pltpu.VMEM((nodes * 8, 128), F32),
-            pltpu.VMEM((nodes * 8, 128), F32),
+            pltpu.VMEM((nodes, 8, 128), F32),
+            pltpu.VMEM((nodes, 8, 128), F32),
             pltpu.VMEM((3, CHUNK * 4, 256), BF),
             pltpu.VMEM((3, CHUNK * 4, 256), F32),
-            pltpu.VMEM((points * 8, 128), F32),
+            pltpu.VMEM((points, 8, 128), F32),
         ],
         compiler_params=params(32),
         name="decode",

time: 81.5 us -> 89.8 us (1.10)
  Pallas kernels: 49.9 us -> 61.7 us
  waiting for transfers between devices: 10.6 us -> 6.37 us
  starting transfers between devices: 15.8 us -> 17.8 us
    pallas_call x1, Pallas kernels: 18.7 us -> 25.5 us  [on_device(): pl.pallas_call(decode_kernel, out_shape=shape((channels, points)), in_spe...]
    ppermute x3, waiting for transfers between devices: 10.6 us -> 6.36 us  [swap(): far = lax.ppermute(outer, axes, pairs)]
    pallas_call x2, Pallas kernels: 9.44 us -> 13.3 us  [the longest x1 8.03 us: on_device(): pl.pallas_call(prepare_kernel, out_shape=(shape((points, 8, 128), F32), s...]
    ppermute x3, starting transfers between devices: 15.3 us -> 17.4 us  [swap(): far = lax.ppermute(outer, axes, pairs)]
    pallas_call x1, Pallas kernels: 10.5 us -> 11.6 us  [on_device(): pl.pallas_call(encode_kernel, out_shape=(shape((rows, width)),) * 2 + (sq...]
  transfers between devices with their start and end apart: 6 -> 6, of which waited for: 2 -> 1; matrix products, arithmetic and copies ran while one was open for 2% -> 1% of each run, Pallas kernels for 15% -> 18%
where the time goes in v5:
time: 89.8 us; the launch traced here: 89.6 us
  Pallas kernels  61.7 us (69%)
  starting transfers between devices  17.8 us (20%)
  waiting for transfers between devices  6.37 us (7%)
  local copies, waits for them, and re-layouts  1.98 us (2%)
  other arithmetic  1.45 us (2%)
    pallas_call x1, Pallas kernels, on_device(): pl.pallas_call(decode_kernel, out_shape=shape((channels, points)), in_spe...  25.5 us
    ppermute x3, starting transfers between devices, swap(): far = lax.ppermute(outer, axes, pairs)  17.4 us
    pallas_call x1, Pallas kernels, on_device(): pl.pallas_call(encode_kernel, out_shape=(shape((rows, width)),) * 2 + (sq...  11.6 us
    pallas_call x1, Pallas kernels, on_device(): pl.pallas_call(window_kernel, out_shape=(shape((rows, width)), shape((BL,...  8.49 us
    pallas_call x1, Pallas kernels, on_device(): pl.pallas_call(prepare_kernel, out_shape=(shape((points, 8, 128), F32), s...  8.03 us
    ppermute x3, waiting for transfers between devices, swap(): far = lax.ppermute(outer, axes, pairs)  6.36 us
    pallas_call x1, Pallas kernels, on_device(): pl.pallas_call(fold_kernel, out_shape=shape((HEADS, rows, CPAD)), in_spec...  5.31 us
    pallas_call x1, Pallas kernels, on_device(): pl.pallas_call(project_kernel, out_shape=(shape((rows, width)),) * 3 + (s...  2.71 us
  transfers between devices with their start and end apart: 6, of which 1 were waited for; matrix products, arithmetic and copies ran while one was open for 1% of the time, Pallas kernels for 18%

profile of v5, /device:TPU:96, one launch (start us, length us, event | category | flops | bytes accessed | tf_op | source)
XLA Modules:
  0.0 89.6 jit_solution(1543007457075574460)
XLA Ops:
  0.0 0.0 copy-start.6
  0.0 0.0 copy-start.7
  0.0 0.0 copy-start.5
  0.0 0.0 copy-start.4
  0.0 0.0 copy-start.2
  0.0 0.0 copy-start.3
  0.0 0.1 pad.10.clone
  0.1 0.1 pad.11.clone
  0.2 1.3 %maximum_maximum_fusion.own.state.grid = bf16[128,2048]{1,0:T(8,128)(2,1)S(1)} fusion(bf16[100,2048]{1,0:T(8,128)(2,1)} %bitcast.15, bf16[128]{0:T(256)(128)(2,1)S(1)} %pad.11.clone, bf16[128]{0:T(256)(128)(2,1)S(1)} %pad.10.clone), kind=kLoop, calls=%fused_computation | loop fusion | flops 1572864 | bytes 934400 | tf_op jit(solution)/shard_map/concatenate | solution.py:325
  1.6 6.4 %collective-permute-start.1 = (bf16[112,1024]{1,0:T(8,128)(2,1)S(1)}, bf16[112,1024]{1,0:T(8,128)(2,1)S(1)}, u32[]{:S(2)}, u32[]{:S(2)}) collective-permute-start(bf16[112,1024]{1,0:T(8,128)(2,1)S(1)} %get-tuple-element.49), channel_id=1, source_target_pairs={{1,2},{2,1},{3,4},{4,3},{5,6},{6,5},{7,8},{8,7},{9,10},{10,9},{11,... | collective-permute-start | bytes 688136 | tf_op jit(solution)/shard_map/ppermute | solution.py:299
  8.0 0.1 collective-permute-start
  8.1 0.0 copy-done.6
  8.2 0.0 copy-done.7
  8.2 0.1 lt.35
  8.3 0.1 lt.33
  8.3 0.0 copy-done.5
  8.4 0.1 lt.37
  8.5 0.0 copy-done.4
  8.5 0.1 pad_add_fusion.others_4_.ends
  8.6 0.1 broadcast_in_dim.21
  8.7 0.1 reshape.24.scale
  8.8 0.0 copy-done.2
  8.8 0.0 copy-done.3
  8.9 0.0 copy-start.1
  8.9 5.3 %fold.1.qt = bf16[16,256,128]{2,1,0:T(8,128)(2,1)} custom-call(bf16[128,1024]{1,0:T(8,128)(2,1)S(1)} %pad.7.win, bf16[4,1024,1024]{2,1,0:T(8,128)(2,1)} %enc_w.3, bf16[256,1024]{1,0:T(8,128)(2,1)} %lat.3, f32[3,1024]{1,0:T(4,128)S(1)} %reshape.24.scale, bf16[128,1024]{1,0:T(8,128)(2,1)S(1)} %pad.8.others_0_.wout, s32[4096]{0:T(1024)S(1)} %bitcast.13, ...), custom_call_target="tpu_custom_call" | custom-call | flops 2000000000 | bytes 8388608 | tf_op jit(solution)/shard_map/fold/pallas_call | solution.py:348
  14.2 0.0 collective-permute-done.1.far
  14.2 0.0 collective-permute-done.near
  14.2 0.0 copy-done.1
  14.2 0.0 copy-start
  14.3 1.2 %copy-done = bf16[16,256,128]{2,1,0:T(8,128)(2,1)S(1)} copy-done((bf16[16,256,128]{2,1,0:T(8,128)(2,1)S(1)}, bf16[16,256,128]{2,1,0:T(8,128)(2,1)}, u32[]{:S(2)}) %copy-start) | copy-done | bytes 1048600
  15.5 11.6 %encode.1 = (bf16[256,1024]{1,0:T(8,128)(2,1)S(1)}, bf16[256,1024]{1,0:T(8,128)(2,1)S(1)}, bf16[1024,1024]{1,0:T(8,128)(2,1)S(1)}, bf16[1024,1024]{1,0:T(8,128)(...) custom-call(s32[3]{0:T(128)S(1)} %pad_add_fusion.others_4_.ends, ...), custom_call_target="tpu_custom_call" | custom-call | tf_op jit(solution)/shard_map/encode/pallas_call | solution.py:359
  27.1 5.4 %collective-permute-start.3 = (bf16[256,1024]{1,0:T(8,128)(2,1)S(1)}, bf16[256,1024]{1,0:T(8,128)(2,1)S(1)}, u32[]{:S(2)}, u32[]{:S(2)}) collective-permute-start(bf16[256,1024]{1,0:T(8,128)(2,1)S(1)} %get-tuple-element.27.normed), channel_id=1, source_target_pairs={{1,2},{2,1},{3,4},{4,3},{5,6},{6,5},{7,8},{8,7},{9,10},{10,9},{11,... | collective-permute-start | bytes 1572872 | tf_op jit(solution)/shard_map/ppermute | solution.py:299
  32.5 0.3 collective-permute-start.2
  32.7 2.7 %project.1 = (bf16[256,1024]{1,0:T(8,128)(2,1)S(1)}, bf16[256,1024]{1,0:T(8,128)(2,1)S(1)}, bf16[256,1024]{1,0:T(8,128)(2,1)S(1)}, bf16[128,1024]{1,0:T(8,128)(2...) custom-call(bf16[256,1024]{1,0:T(8,128)(2,1)S(1)} %get-tuple-element.27.normed, ...), custom_call_target="tpu_custom_call" | custom-call | flops 3000000000 | bytes 12582912 | tf_op jit(solution)/shard_map/project/pallas_call | solution.py:379
  35.4 6.4 %collective-permute-done.3.far = bf16[256,1024]{1,0:T(8,128)(2,1)S(1)} collective-permute-done((bf16[256,1024]{1,0:T(8,128)(2,1)S(1)}, bf16[256,1024]{1,0:T(8,128)(2,1)S(1)}, u32[]{:S(2)}, u32[]{:S(2)}) %collective-permute-start.3) | collective-permute-done | bytes 524320 | tf_op jit(solution)/shard_map/ppermute | solution.py:299
  41.8 0.0 collective-permute-done.2.near
  41.8 8.5 %window.1 = (bf16[256,1024]{1,0:T(8,128)(2,1)S(1)}, bf16[128,1024]{1,0:T(8,128)(2,1)S(1)}, bf16[128,1024]{1,0:T(8,128)(2,1)S(1)}) custom-call(s32[3]{0:T(128)S(1)} %pad_add_fusion.others_4_.ends, bf16[256,1024]{1,0:T(8,128)(2,1)S(1)} %get-tuple-element.33.q, bf16[256,1024]{1,0:T(8,128)(2,1)S(1)} %get-tuple-element.34.k, ...), custom_call_target="tpu_custom_call" | custom-call | tf_op jit(solution)/shard_map/window/pallas_call | solution.py:389
  50.3 0.1 collective-permute-start.4
  50.4 5.6 %collective-permute-start.5 = (bf16[128,1024]{1,0:T(8,128)(2,1)S(1)}, bf16[128,1024]{1,0:T(8,128)(2,1)S(1)}, u32[]{:S(2)}, u32[]{:S(2)}) collective-permute-start(bf16[128,1024]{1,0:T(8,128)(2,1)S(1)} %get-tuple-element.39), channel_id=1, source_target_pairs={{1,2},{2,1},{3,4},{4,3},{5,6},{6,5},{7,8},{8,7},{9,10},{10,9},{11,... | collective-permute-start | bytes 786440 | tf_op jit(solution)/shard_map/ppermute | solution.py:299
  56.0 8.0 %prepare.1 = (f32[2048,8,128]{2,1,0:T(8,128)S(1)}, f32[256,8,128]{2,1,0:T(8,128)S(1)}, f32[256,8,128]{2,1,0:T(8,128)S(1)}) custom-call(bf16[256,1024]{1,0:T(8,128)(2,1)S(1)} %get-tuple-element.40.own, bf16[128,2048]{1,0:T(8,128)(2,1)S(1)} %maximum_maximum_fusion.own.state.grid, bf16[128,1024]{1,0:T(8,128)(2,1)S(1)} %get-tuple-element.41.aq, ...), custom_call_target="tpu_custom_call" | custom-call | flops 3000000000 | bytes 12582912 | tf_op jit(solution)/shard_map/prepare/pallas_call | solution.py:405
  64.0 0.0 collective-permute-done.4.near
  64.0 0.0 collective-permute-done.5.far
  64.0 25.5 %decode.1 = bf16[100,2048]{1,0:T(8,128)(2,1)} custom-call(s32[3]{0:T(128)S(1)} %pad_add_fusion.others_4_.ends, s32[6144]{0:T(1024)S(1)} %reshape.22.others_3_.idx, bf16[128,1024]{1,0:T(8,128)(2,1)S(1)} %collective-permute-done.4.near, bf16[128,1024]{1,0:T(8,128)(2,1)S(1)} %collective-permute-done.5.far, f32[256,8,128]{2,1,0:T(8,128)S(1)} %get-tuple-element.44.ko, ...), custom_call_target="tpu_custom_call" | custom-call | tf_op jit(solution)/shard_map/decode/pallas_call | solution.py:418
  (13 shorter events, 0.2 us)
Async XLA Ops:
  0.0 8.1 %copy-start.6 = (f32[3,16]{1,0:T(4,128)S(1)}, f32[3,16]{1,0:T(4,128)}, u32[]{:S(2)}) copy-start(f32[3,16]{1,0:T(4,128)} %param.21) | copy-start | bytes 580
  0.0 8.2 %copy-start.7 = (s32[256]{0:T(256)S(1)}, s32[256]{0:T(256)}, u32[]{:S(2)}) copy-start(s32[256]{0:T(256)} %param.14) | copy-start | bytes 3076
  0.0 8.3 %copy-start.5 = (s32[256,16]{0,1:T(8,128)S(1)}, s32[256,16]{0,1:T(8,128)}, u32[]{:S(2)}) copy-start(s32[256,16]{0,1:T(8,128)} %param.13) | copy-start | bytes 49156
  0.0 8.5 %copy-start.4 = (s32[2048,3]{0,1:T(4,128)S(1)}, s32[2048,3]{0,1:T(4,128)}, u32[]{:S(2)}) copy-start(s32[2048,3]{0,1:T(4,128)} %param.15) | copy-start | bytes 73732
  0.0 8.8 %copy-start.2 = (bf16[100,1024]{1,0:T(8,128)(2,1)S(1)}, bf16[100,1024]{1,0:T(8,128)(2,1)}, u32[]{:S(2)}) copy-start(bf16[100,1024]{1,0:T(8,128)(2,1)} %param.16) | copy-start | bytes 614404
  0.0 8.8 %copy-start.3 = (bf16[1024,100]{0,1:T(8,128)(2,1)S(1)}, bf16[1024,100]{0,1:T(8,128)(2,1)}, u32[]{:S(2)}) copy-start(bf16[1024,100]{0,1:T(8,128)(2,1)} %param.20) | copy-start | bytes 614404
  1.6 12.6 %collective-permute-start.1 = (bf16[112,1024]{1,0:T(8,128)(2,1)S(1)}, bf16[112,1024]{1,0:T(8,128)(2,1)S(1)}, u32[]{:S(2)}, u32[]{:S(2)}) collective-permute-start(bf16[112,1024]{1,0:T(8,128)(2,1)S(1)} %get-tuple-element.49), channel_id=1, source_target_pairs={{1,2},{2,1},{3,4},{4,3},{5,6},{6,5},{7,8},{8,7},{9,10},{10,9},{11,... | collective-permute-start | bytes 688136 | tf_op jit(solution)/shard_map/ppermute | solution.py:299
  8.0 6.2 %collective-permute-start = (bf16[112,1024]{1,0:T(8,128)(2,1)S(1)}, bf16[112,1024]{1,0:T(8,128)(2,1)S(1)}, u32[]{:S(2)}, u32[]{:S(2)}) collective-permute-start(bf16[112,1024]{1,0:T(8,128)(2,1)S(1)} %get-tuple-element.50), channel_id=1, source_target_pairs={{0,1},{1,0},{2,3},{3,2},{4,5},{5,4},{6,7},{7,6},{8,9},{9,8},{10,11... | collective-permute-start | bytes 688136 | tf_op jit(solution)/shard_map/ppermute | solution.py:300
  8.9 5.4 %copy-start.1 = (bf16[256,1024]{1,0:T(8,128)(2,1)S(1)}, bf16[256,1024]{1,0:T(8,128)(2,1)}, u32[]{:S(2)}) copy-start(bf16[256,1024]{1,0:T(8,128)(2,1)} %lat.3) | copy-start | bytes 1572868
  14.2 1.2 %copy-start = (bf16[16,256,128]{2,1,0:T(8,128)(2,1)S(1)}, bf16[16,256,128]{2,1,0:T(8,128)(2,1)}, u32[]{:S(2)}) copy-start(bf16[16,256,128]{2,1,0:T(8,128)(2,1)} %fold.1.qt) | copy-start | bytes 3145732
  27.1 14.7 %collective-permute-start.3 = (bf16[256,1024]{1,0:T(8,128)(2,1)S(1)}, bf16[256,1024]{1,0:T(8,128)(2,1)S(1)}, u32[]{:S(2)}, u32[]{:S(2)}) collective-permute-start(bf16[256,1024]{1,0:T(8,128)(2,1)S(1)} %get-tuple-element.27.normed), channel_id=1, source_target_pairs={{1,2},{2,1},{3,4},{4,3},{5,6},{6,5},{7,8},{8,7},{9,10},{10,9},{11,... | collective-permute-start | bytes 1572872 | tf_op jit(solution)/shard_map/ppermute | solution.py:299
  32.5 9.3 %collective-permute-start.2 = (bf16[256,1024]{1,0:T(8,128)(2,1)S(1)}, bf16[256,1024]{1,0:T(8,128)(2,1)S(1)}, u32[]{:S(2)}, u32[]{:S(2)}) collective-permute-start(bf16[256,1024]{1,0:T(8,128)(2,1)S(1)} %get-tuple-element.27.normed), channel_id=1, source_target_pairs={{0,1},{1,0},{2,3},{3,2},{4,5},{5,4},{6,7},{7,6},{8,9},{9,8},{10,11... | collective-permute-start | bytes 1572872 | tf_op jit(solution)/shard_map/ppermute | solution.py:300
  50.3 13.7 %collective-permute-start.4 = (bf16[128,1024]{1,0:T(8,128)(2,1)S(1)}, bf16[128,1024]{1,0:T(8,128)(2,1)S(1)}, u32[]{:S(2)}, u32[]{:S(2)}) collective-permute-start(bf16[128,1024]{1,0:T(8,128)(2,1)S(1)} %get-tuple-element.38), channel_id=1, source_target_pairs={{0,1},{1,0},{2,3},{3,2},{4,5},{5,4},{6,7},{7,6},{8,9},{9,8},{10,11... | collective-permute-start | bytes 786440 | tf_op jit(solution)/shard_map/ppermute | solution.py:300
  50.4 13.6 %collective-permute-start.5 = (bf16[128,1024]{1,0:T(8,128)(2,1)S(1)}, bf16[128,1024]{1,0:T(8,128)(2,1)S(1)}, u32[]{:S(2)}, u32[]{:S(2)}) collective-permute-start(bf16[128,1024]{1,0:T(8,128)(2,1)S(1)} %get-tuple-element.39), channel_id=1, source_target_pairs={{1,2},{2,1},{3,4},{4,3},{5,6},{6,5},{7,8},{8,7},{9,10},{10,9},{11,... | collective-permute-start | bytes 786440 | tf_op jit(solution)/shard_map/ppermute | solution.py:299

commit v6 on v4

--- a/solution.py
+++ b/solution.py
@@ -102,25 +102,20 @@
 
     def attend(number, ge):
         points = ge[...].astype(BF)
-        base = pl.multiple_of(number * 16, 16)
-        queries = qt[:, pl.ds(base, 16), :].reshape(256, CPAD)
-        score = dot_t(queries, points) + (diag + bias[pl.ds(number, 1), :])
+        these = slice(number * 16, number * 16 + 16)
+        queries = qt[:, these, :].reshape(256, CPAD)
+        score = dot_t(queries, points) + (diag + bias[number : number + 1, :])
         expo = jnp.exp2(score - jnp.max(score, axis=1, keepdims=True)).astype(BF)
-        mixed = dot(expo, points)
-        mixed = mixed / mixed[:, 100:101]
-        z[:, pl.ds(base, 16), :] = mixed.reshape(16, 16, CPAD).astype(BF)
-
+        mixed = dot(expo, jnp.concatenate([points, jnp.ones_like(points)], axis=1))
+        mixed = mixed[:, :CPAD] * (1.0 / mixed[:, CPAD:])
+        z[:, these, :] = mixed.reshape(16, 16, CPAD).astype(BF)
+
+    buffers = (ge0, ge1)
     collect(0, ge0)
-
-    def two_groups(step, carry):
-        number = step * 2
-        attend(number, ge0)
-        collect(number + 1, ge1)
-        attend(number + 1, ge1)
-        collect(jnp.minimum(number + 2, groups - 1), ge0)
-        return carry
-
-    lax.fori_loop(0, groups // 2, two_groups, 0)
+    for number in range(groups):
+        attend(number, buffers[number % 2])
+        if number + 1 < groups:
+            collect(number + 1, buffers[(number + 1) % 2])
     low = low_half((1, 128))
     parts = []
     for pair in range(PAIRS):
@@ -173,28 +168,32 @@
         wide[2 * rows :, :] = both[rows:]
     low = low_half((1, 128))
 
-    def one_pair(pair, carry):
-        lanes = pl.ds(pl.multiple_of(pair * 128, 128), 128)
+    for pair in range(PAIRS):
+        lanes = slice(pair * 128, pair * 128 + 128)
+        bands = [slice(side * half, side * half + span) for side in range(2)]
+        score = []
         for side in range(2):
-            these = slice(side * half, side * half + half)
-            band = slice(side * half, side * half + span)
-            both = q[these, lanes]
+            both = q[side * half : side * half + half, lanes]
             zero = jnp.zeros_like(both)
             stacked = jnp.concatenate(
                 [jnp.where(low, both, zero), jnp.where(low, zero, both)], axis=0
             )
-            near_values = values[band, lanes]
-            score = dot_t(stacked, keys[band, lanes]).reshape(2, half, span) + bias[side][None]
-            score = score.reshape(2 * half, span)
-            expo = jnp.exp2(score - jnp.max(score, axis=1, keepdims=True)).astype(BF)
+            part = dot_t(stacked, keys[bands[side], lanes])
+            score.append(
+                (part.reshape(2, half, span) + bias[side][None]).reshape(2 * half, span)
+            )
+        expo = [
+            jnp.exp2(part - jnp.max(part, axis=1, keepdims=True)).astype(BF) for part in score
+        ]
+        for side in range(2):
+            near_values = values[bands[side], lanes]
             total = dot(
-                expo, jnp.concatenate([near_values, jnp.ones_like(near_values)], axis=1)
+                expo[side], jnp.concatenate([near_values, jnp.ones_like(near_values)], axis=1)
             )
-            part = total[:, :128] / total[:, 128:]
-            mixed[these, lanes] = jnp.where(low, part[:half], part[half:]).astype(BF)
-        return carry
-
-    lax.fori_loop(0, PAIRS, one_pair, 0, unroll=True)
+            part = total[:, :128] * (1.0 / total[:, 128:])
+            mixed[side * half : side * half + half, lanes] = jnp.where(
+                low, part[:half], part[half:]
+            ).astype(BF)
     out[...] = (latent[...].astype(F32) + dot(mixed[...], wo[...])).astype(BF)
     inner[...], outer[...] = sides(ends[2], out[:BL, :], out[rows - BL :, :])
 
@@ -204,10 +203,12 @@
 
 def to_tiles(rows, weight, tiles, begin):
     count = rows.shape[0]
-    for block in range(8):
-        tiles[pl.ds(begin * 8 + block, count, stride=8), :] = dot(
-            rows, weight[:, block * 128 : block * 128 + 128]
-        )
+    for two in range(4):
+        wide = dot(rows, weight[:, two * 256 : two * 256 + 256])
+        for block in (2 * two, 2 * two + 1):
+            tiles[pl.ds(begin * 8 + block, count, stride=8), :] = wide[
+                :, block % 2 * 128 : block % 2 * 128 + 128
+            ]
 
 
 def prepare_kernel(own, state, aq, wk, wv, q, k, v):
@@ -226,10 +227,12 @@
     halo = jnp.concatenate(sides(ends[2], near[...], far[...]), axis=0)
     for weight, tiles, own in ((wk, kf, ko), (wv, vf, vo)):
         tiles[side * 8 : side * 8 + own.shape[0], :] = own[...]
-        for block in range(8):
-            both = dot(halo, weight[:, block * 128 : block * 128 + 128])
-            tiles[pl.ds(block, side, stride=8), :] = both[:side]
-            tiles[pl.ds(side * 8 + own.shape[0] + block, side, stride=8), :] = both[side:]
+        for two in range(4):
+            wide = dot(halo, weight[:, two * 256 : two * 256 + 256])
+            for block in (2 * two, 2 * two + 1):
+                both = wide[:, block % 2 * 128 : block % 2 * 128 + 128]
+                tiles[pl.ds(block, side, stride=8), :] = both[:side]
+                tiles[pl.ds(side * 8 + own.shape[0] + block, side, stride=8), :] = both[side:]
     head_row = lax.broadcasted_iota(jnp.int32, (256, 256), 0) // SIZE
     head_col = lax.broadcasted_iota(jnp.int32, (256, 256), 1) // SIZE
     ones = jnp.where(head_row == head_col, 1.0, 0.0).astype(BF)

time: 81.5 us -> 80.7 us (level)
  Pallas kernels: 49.9 us -> 47.8 us
  waiting for transfers between devices: 10.6 us -> 11.9 us
    pallas_call x1, Pallas kernels: 18.7 us -> 17.3 us  [on_device(): pl.pallas_call(decode_kernel, out_shape=shape((channels, points)), in_spe...]
    pallas_call x1, Pallas kernels: 4.11 us -> 2.8 us  [on_device(): pl.pallas_call(prepare_kernel, out_shape=(shape((points * 8, 128), F32),...]
    ppermute x3, waiting for transfers between devices: 10.6 us -> 11.9 us  [swap(): far = lax.ppermute(outer, axes, pairs)]
  transfers between devices with their start and end apart: 6 -> 6, of which waited for: 2 -> 2; matrix products, arithmetic and copies ran while one was open for 2% -> 2% of each run, Pallas kernels for 15% -> 13%
where the time goes in v6:
time: 80.7 us; the launch traced here: 80.4 us
  Pallas kernels  47.8 us (59%)
  starting transfers between devices  15.8 us (20%)
  waiting for transfers between devices  11.9 us (15%)
  local copies, waits for them, and re-layouts  2.62 us (3%)
  other arithmetic  2.12 us (3%)
    pallas_call x1, Pallas kernels, on_device(): pl.pallas_call(decode_kernel, out_shape=shape((channels, points)), in_spe...  17.3 us
    ppermute x3, starting transfers between devices, swap(): far = lax.ppermute(outer, axes, pairs)  15.3 us
    ppermute x3, waiting for transfers between devices, swap(): far = lax.ppermute(outer, axes, pairs)  11.9 us
    pallas_call x1, Pallas kernels, on_device(): pl.pallas_call(encode_kernel, out_shape=(shape((rows, width)),) * 2 + (sq...  11.1 us
    pallas_call x1, Pallas kernels, on_device(): pl.pallas_call(window_kernel, out_shape=(shape((rows, width)), shape((BL,...  8.48 us
    pallas_call x1, Pallas kernels, on_device(): pl.pallas_call(fold_kernel, out_shape=(shape((HEADS, rows, CPAD)), shape(...  5.34 us
    pallas_call x1, Pallas kernels, on_device(): pl.pallas_call(prepare_kernel, out_shape=(shape((points * 8, 128), F32),...  2.8 us
    pallas_call x1, Pallas kernels, on_device(): pl.pallas_call(project_kernel, out_shape=(shape((rows, width)),) * 3 + (s...  2.71 us
  transfers between devices with their start and end apart: 6, of which 2 were waited for; matrix products, arithmetic and copies ran while one was open for 2% of the time, Pallas kernels for 13%

profile of v6, /device:TPU:96, one launch (start us, length us, event | category | flops | bytes accessed | tf_op | source)
XLA Modules:
  0.0 80.4 jit_solution(8844610291038237642)
XLA Ops:
  0.0 0.0 copy-start.5
  0.0 0.0 copy-start.4
  0.0 0.0 copy-start.2
  0.0 0.0 copy-start.3
  0.0 0.1 pad.10.clone
  0.1 0.1 pad.11.clone
  0.2 1.3 %maximum_maximum_fusion.own.state.grid = bf16[128,2048]{1,0:T(8,128)(2,1)S(1)} fusion(bf16[100,2048]{1,0:T(8,128)(2,1)} %bitcast.15, bf16[128]{0:T(256)(128)(2,1)S(1)} %pad.11.clone, bf16[128]{0:T(256)(128)(2,1)S(1)} %pad.10.clone), kind=kLoop, calls=%fused_computation | loop fusion | flops 1572864 | bytes 934400 | tf_op jit(solution)/shard_map/concatenate | solution.py:320
  1.6 6.4 %collective-permute-start.1 = (bf16[128,1024]{1,0:T(8,128)(2,1)S(1)}, bf16[128,1024]{1,0:T(8,128)(2,1)S(1)}, u32[]{:S(2)}, u32[]{:S(2)}) collective-permute-start(bf16[128,1024]{1,0:T(8,128)(2,1)S(1)} %get-tuple-element.53), channel_id=1, source_target_pairs={{1,2},{2,1},{3,4},{4,3},{5,6},{6,5},{7,8},{8,7},{9,10},{10,9},{11,... | collective-permute-start | bytes 786440 | tf_op jit(solution)/shard_map/ppermute | solution.py:294
  8.0 0.1 collective-permute-start
  8.1 0.7 broadcast_multiply_fusion
  8.8 0.8 lt.35
  9.5 0.1 lt.33
  9.6 0.0 copy-done.5
  9.6 0.1 broadcast_in_dim.21
  9.7 0.1 reshape.23.scale
  9.8 0.0 copy-done.4
  9.9 0.1 lt.37
  10.0 0.0 copy-done.2
  10.0 0.0 copy-done.3
  10.1 0.1 pad_add_fusion.others_4_.ends
  10.2 0.0 copy-start
  10.2 5.3 %fold.1 = (bf16[16,256,128]{2,1,0:T(8,128)(2,1)}, bf16[128,1024]{1,0:T(8,128)(2,1)S(1)}) custom-call(bf16[128,1024]{1,0:T(8,128)(2,1)S(1)} %pad.7.win, bf16[4,1024,1024]{2,1,0:T(8,128)(2,1)} %enc_w.3, bf16[256,1024]{1,0:T(8,128)(2,1)} %lat.3, f32[3,1024]{1,0:T(4,128)S(1)} %reshape.23.scale, bf16[128,1024]{1,0:T(8,128)(2,1)S(1)} %pad.8.others_0_.wout, ...), custom_call_target="tpu_custom_call" | custom-call | flops 2000000000 | bytes 8388608 | tf_op jit(solution)/shard_map/fold/pallas_call | solution.py:343
  15.5 0.0 collective-permute-done.1.far
  15.5 0.0 collective-permute-done.near
  15.5 0.0 copy-done
  15.5 0.0 copy-start.1
  15.5 1.2 %copy-done.1 = bf16[16,256,128]{2,1,0:T(8,128)(2,1)S(1)} copy-done((bf16[16,256,128]{2,1,0:T(8,128)(2,1)S(1)}, bf16[16,256,128]{2,1,0:T(8,128)(2,1)}, u32[]{:S(2)}) %copy-start.1) | copy-done | bytes 1048600
  16.8 11.1 %encode.1 = (bf16[256,1024]{1,0:T(8,128)(2,1)S(1)}, bf16[256,1024]{1,0:T(8,128)(2,1)S(1)}, bf16[1024,1024]{1,0:T(8,128)(2,1)S(1)}, bf16[1024,1024]{1,0:T(8,128)(...) custom-call(s32[3]{0:T(128)S(1)} %pad_add_fusion.others_4_.ends, ...), custom_call_target="tpu_custom_call" | custom-call | tf_op jit(solution)/shard_map/encode/pallas_call | solution.py:354
  27.8 4.4 %collective-permute-start.3 = (bf16[256,1024]{1,0:T(8,128)(2,1)S(1)}, bf16[256,1024]{1,0:T(8,128)(2,1)S(1)}, u32[]{:S(2)}, u32[]{:S(2)}) collective-permute-start(bf16[256,1024]{1,0:T(8,128)(2,1)S(1)} %get-tuple-element.31.normed), channel_id=1, source_target_pairs={{1,2},{2,1},{3,4},{4,3},{5,6},{6,5},{7,8},{8,7},{9,10},{10,9},{11,... | collective-permute-start | bytes 1572872 | tf_op jit(solution)/shard_map/ppermute | solution.py:294
  32.2 0.3 collective-permute-start.2
  32.5 2.7 %project.1 = (bf16[256,1024]{1,0:T(8,128)(2,1)S(1)}, bf16[256,1024]{1,0:T(8,128)(2,1)S(1)}, bf16[256,1024]{1,0:T(8,128)(2,1)S(1)}, bf16[128,1024]{1,0:T(8,128)(2...) custom-call(bf16[256,1024]{1,0:T(8,128)(2,1)S(1)} %get-tuple-element.31.normed, ...), custom_call_target="tpu_custom_call" | custom-call | flops 3000000000 | bytes 12582912 | tf_op jit(solution)/shard_map/project/pallas_call | solution.py:371
  35.2 7.4 %collective-permute-done.3.far = bf16[256,1024]{1,0:T(8,128)(2,1)S(1)} collective-permute-done((bf16[256,1024]{1,0:T(8,128)(2,1)S(1)}, bf16[256,1024]{1,0:T(8,128)(2,1)S(1)}, u32[]{:S(2)}, u32[]{:S(2)}) %collective-permute-start.3) | collective-permute-done | bytes 524320 | tf_op jit(solution)/shard_map/ppermute | solution.py:294
  42.6 0.0 collective-permute-done.2.near
  42.6 8.5 %window.1 = (bf16[256,1024]{1,0:T(8,128)(2,1)S(1)}, bf16[128,1024]{1,0:T(8,128)(2,1)S(1)}, bf16[128,1024]{1,0:T(8,128)(2,1)S(1)}) custom-call(s32[3]{0:T(128)S(1)} %pad_add_fusion.others_4_.ends, bf16[256,1024]{1,0:T(8,128)(2,1)S(1)} %get-tuple-element.37.q, bf16[256,1024]{1,0:T(8,128)(2,1)S(1)} %get-tuple-element.38.k, ...), custom_call_target="tpu_custom_call" | custom-call | tf_op jit(solution)/shard_map/window/pallas_call | solution.py:381
  51.1 0.1 collective-permute-start.4
  51.1 4.6 %collective-permute-start.5 = (bf16[128,1024]{1,0:T(8,128)(2,1)S(1)}, bf16[128,1024]{1,0:T(8,128)(2,1)S(1)}, u32[]{:S(2)}, u32[]{:S(2)}) collective-permute-start(bf16[128,1024]{1,0:T(8,128)(2,1)S(1)} %get-tuple-element.43), channel_id=1, source_target_pairs={{1,2},{2,1},{3,4},{4,3},{5,6},{6,5},{7,8},{8,7},{9,10},{10,9},{11,... | collective-permute-start | bytes 786440 | tf_op jit(solution)/shard_map/ppermute | solution.py:294
  55.7 2.8 %prepare.1 = (f32[16384,128]{1,0:T(8,128)S(1)}, f32[2048,128]{1,0:T(8,128)S(1)}, f32[2048,128]{1,0:T(8,128)S(1)}) custom-call(bf16[256,1024]{1,0:T(8,128)(2,1)S(1)} %get-tuple-element.44.own, bf16[128,2048]{1,0:T(8,128)(2,1)S(1)} %maximum_maximum_fusion.own.state.grid, bf16[128,1024]{1,0:T(8,128)(2,1)S(1)} %get-tuple-element.45.aq, ...), custom_call_target="tpu_custom_call" | custom-call | flops 3000000000 | bytes 12582912 | tf_op jit(solution)/shard_map/prepare/pallas_call | solution.py:397
  58.5 0.0 collective-permute-done.4.near
  58.6 4.5 %collective-permute-done.5.far = bf16[128,1024]{1,0:T(8,128)(2,1)S(1)} collective-permute-done((bf16[128,1024]{1,0:T(8,128)(2,1)S(1)}, bf16[128,1024]{1,0:T(8,128)(2,1)S(1)}, u32[]{:S(2)}, u32[]{:S(2)}) %collective-permute-start.5) | collective-permute-done | bytes 262176 | tf_op jit(solution)/shard_map/ppermute | solution.py:294
  63.1 17.3 %decode.1 = bf16[100,2048]{1,0:T(8,128)(2,1)} custom-call(s32[3]{0:T(128)S(1)} %pad_add_fusion.others_4_.ends, s32[6144]{0:T(1024)S(1)} %mul.35.others_3_.idx, bf16[128,1024]{1,0:T(8,128)(2,1)S(1)} %collective-permute-done.4.near, bf16[128,1024]{1,0:T(8,128)(2,1)S(1)} %collective-permute-done.5.far, f32[2048,128]{1,0:T(8,128)S(1)} %get-tuple-element.48.ko, ...), custom_call_target="tpu_custom_call" | custom-call | tf_op jit(solution)/shard_map/decode/pallas_call | solution.py:410
  (11 shorter events, 0.2 us)
Async XLA Ops:
  0.0 9.6 %copy-start.5 = (s32[256,16]{0,1:T(8,128)S(1)}, s32[256,16]{0,1:T(8,128)}, u32[]{:S(2)}) copy-start(s32[256,16]{0,1:T(8,128)} %param.13) | copy-start | bytes 49156
  0.0 9.8 %copy-start.4 = (s32[2048,3]{0,1:T(4,128)S(1)}, s32[2048,3]{0,1:T(4,128)}, u32[]{:S(2)}) copy-start(s32[2048,3]{0,1:T(4,128)} %param.15) | copy-start | bytes 73732
  0.0 10.0 %copy-start.2 = (bf16[100,1024]{1,0:T(8,128)(2,1)S(1)}, bf16[100,1024]{1,0:T(8,128)(2,1)}, u32[]{:S(2)}) copy-start(bf16[100,1024]{1,0:T(8,128)(2,1)} %param.16) | copy-start | bytes 614404
  0.0 10.0 %copy-start.3 = (bf16[1024,100]{0,1:T(8,128)(2,1)S(1)}, bf16[1024,100]{0,1:T(8,128)(2,1)}, u32[]{:S(2)}) copy-start(bf16[1024,100]{0,1:T(8,128)(2,1)} %param.20) | copy-start | bytes 614404
  1.6 13.9 %collective-permute-start.1 = (bf16[128,1024]{1,0:T(8,128)(2,1)S(1)}, bf16[128,1024]{1,0:T(8,128)(2,1)S(1)}, u32[]{:S(2)}, u32[]{:S(2)}) collective-permute-start(bf16[128,1024]{1,0:T(8,128)(2,1)S(1)} %get-tuple-element.53), channel_id=1, source_target_pairs={{1,2},{2,1},{3,4},{4,3},{5,6},{6,5},{7,8},{8,7},{9,10},{10,9},{11,... | collective-permute-start | bytes 786440 | tf_op jit(solution)/shard_map/ppermute | solution.py:294
  8.0 7.5 %collective-permute-start = (bf16[128,1024]{1,0:T(8,128)(2,1)S(1)}, bf16[128,1024]{1,0:T(8,128)(2,1)S(1)}, u32[]{:S(2)}, u32[]{:S(2)}) collective-permute-start(bf16[128,1024]{1,0:T(8,128)(2,1)S(1)} %get-tuple-element.54), channel_id=1, source_target_pairs={{0,1},{1,0},{2,3},{3,2},{4,5},{5,4},{6,7},{7,6},{8,9},{9,8},{10,11... | collective-permute-start | bytes 786440 | tf_op jit(solution)/shard_map/ppermute | solution.py:295
  10.2 5.4 %copy-start = (bf16[256,1024]{1,0:T(8,128)(2,1)S(1)}, bf16[256,1024]{1,0:T(8,128)(2,1)}, u32[]{:S(2)}) copy-start(bf16[256,1024]{1,0:T(8,128)(2,1)} %lat.3) | copy-start | bytes 1572868
  15.5 1.2 %copy-start.1 = (bf16[16,256,128]{2,1,0:T(8,128)(2,1)S(1)}, bf16[16,256,128]{2,1,0:T(8,128)(2,1)}, u32[]{:S(2)}) copy-start(bf16[16,256,128]{2,1,0:T(8,128)(2,1)} %get-tuple-element.29.qt) | copy-start | bytes 3145732
  27.8 14.7 %collective-permute-start.3 = (bf16[256,1024]{1,0:T(8,128)(2,1)S(1)}, bf16[256,1024]{1,0:T(8,128)(2,1)S(1)}, u32[]{:S(2)}, u32[]{:S(2)}) collective-permute-start(bf16[256,1024]{1,0:T(8,128)(2,1)S(1)} %get-tuple-element.31.normed), channel_id=1, source_target_pairs={{1,2},{2,1},{3,4},{4,3},{5,6},{6,5},{7,8},{8,7},{9,10},{10,9},{11,... | collective-permute-start | bytes 1572872 | tf_op jit(solution)/shard_map/ppermute | solution.py:294
  32.2 10.4 %collective-permute-start.2 = (bf16[256,1024]{1,0:T(8,128)(2,1)S(1)}, bf16[256,1024]{1,0:T(8,128)(2,1)S(1)}, u32[]{:S(2)}, u32[]{:S(2)}) collective-permute-start(bf16[256,1024]{1,0:T(8,128)(2,1)S(1)} %get-tuple-element.31.normed), channel_id=1, source_target_pairs={{0,1},{1,0},{2,3},{3,2},{4,5},{5,4},{6,7},{7,6},{8,9},{9,8},{10,11... | collective-permute-start | bytes 1572872 | tf_op jit(solution)/shard_map/ppermute | solution.py:295
  51.1 7.5 %collective-permute-start.4 = (bf16[128,1024]{1,0:T(8,128)(2,1)S(1)}, bf16[128,1024]{1,0:T(8,128)(2,1)S(1)}, u32[]{:S(2)}, u32[]{:S(2)}) collective-permute-start(bf16[128,1024]{1,0:T(8,128)(2,1)S(1)} %get-tuple-element.42), channel_id=1, source_target_pairs={{0,1},{1,0},{2,3},{3,2},{4,5},{5,4},{6,7},{7,6},{8,9},{9,8},{10,11... | collective-permute-start | bytes 786440 | tf_op jit(solution)/shard_map/ppermute | solution.py:295
  51.1 11.9 %collective-permute-start.5 = (bf16[128,1024]{1,0:T(8,128)(2,1)S(1)}, bf16[128,1024]{1,0:T(8,128)(2,1)S(1)}, u32[]{:S(2)}, u32[]{:S(2)}) collective-permute-start(bf16[128,1024]{1,0:T(8,128)(2,1)S(1)} %get-tuple-element.43), channel_id=1, source_target_pairs={{1,2},{2,1},{3,4},{4,3},{5,6},{6,5},{7,8},{8,7},{9,10},{10,9},{11,... | collective-permute-start | bytes 786440 | tf_op jit(solution)/shard_map/ppermute | solution.py:294

commit v7 on v6

--- a/solution.py
+++ b/solution.py
@@ -74,13 +74,12 @@
 
 
 def encode_kernel(
-    ends, idx, near, own, far, qt, bias, av, lat, enc_w, proc_w, dec_w,
-    latent, normed, pw0, pw1, pw2, pw3, dw0, dw1, dw2, dw3,
+    ends, idx, near, own, far, qt, bias, av, lat, enc_w, proc_w,
+    latent, normed, pw0, pw1, pw2,
     grid, ge0, ge1, z, w3, sems,
 ):
     got = fetch(enc_w, (3,), (w3,), sems.at[pl.ds(0, 1)])
-    later = fetch(proc_w, (0, 1, 2, 3), (pw0, pw1, pw2, pw3), sems.at[pl.ds(1, 4)])
-    later += fetch(dec_w, (0, 3, 1, 2), (dw0, dw3, dw1, dw2), sems.at[pl.ds(5, 4)])
+    later = fetch(proc_w, (0, 1, 2), (pw0, pw1, pw2), sems.at[pl.ds(1, 3)])
     rows = lat.shape[0]
     groups = rows // 16
     at = 0
@@ -137,65 +136,79 @@
         copy.wait()
 
 
-def project_kernel(normed, win, wout, scale, wq, wk, wv, dq, do, q, k, v, aq, bo, co):
+def project_kernel(
+    normed, win, wout, scale, wq, wk, wv, proc_w, dec_w,
+    q, k, v, aq, bo, co, pw3, dw1, dw2, dw0, dw3, sems,
+):
+    got = fetch(dec_w, (0, 3), (dw0, dw3), sems.at[pl.ds(0, 2)])
+    later = fetch(proc_w, (3,), (pw3,), sems.at[pl.ds(2, 1)])
+    later += fetch(dec_w, (1, 2), (dw1, dw2), sems.at[pl.ds(3, 2)])
     rows = normed[...]
     q[...] = (dot(rows, wq[...]) * scale[1:2, :]).astype(BF)
     k[...] = dot(rows, wk[...]).astype(BF)
     v[...] = dot(rows, wv[...]).astype(BF)
     co[...] = dot_t(wout[...], win[...]).astype(BF)
-    aq[...] = (dot(win[...], dq[...]) * scale[2:3, :]).astype(BF)
-    bo[...] = dot_t(do[...], wout[...]).astype(BF)
-
-
-def window_kernel(
-    ends, q, k, v, near, far, latent, wk, wv, wo, out, inner, outer, keys, values, bias, mixed
+    got[0].wait()
+    aq[...] = (dot(win[...], dw0[...]) * scale[2:3, :]).astype(BF)
+    got[1].wait()
+    bo[...] = dot_t(dw3[...], wout[...]).astype(BF)
+    for copy in later:
+        copy.wait()
+
+
+def window_half(side, ends, q, keys, values, latent, wo, bias, mixed, out):
+    half, span = bias.shape
+    row = lax.broadcasted_iota(jnp.int32, (half, span), 0)
+    col = lax.broadcasted_iota(jnp.int32, (half, span), 1)
+    begin = pl.multiple_of(side * half, half)
+    place = col + begin
+    inside = (col >= row) & (col - row <= WIN) & (place >= ends[0]) & (place < ends[1])
+    bias[...] = jnp.where(inside, 0.0, NEG)
+    these = pl.ds(begin, half)
+    band = pl.ds(begin, span)
+    low = low_half((1, 128))
+    for first in range(0, PAIRS, 2):
+        lanes = [slice(pair * 128, pair * 128 + 128) for pair in (first, first + 1)]
+        score = []
+        for at in lanes:
+            both = q[these, at]
+            zero = jnp.zeros_like(both)
+            stacked = jnp.concatenate(
+                [jnp.where(low, both, zero), jnp.where(low, zero, both)], axis=0
+            )
+            part = dot_t(stacked, keys[band, at])
+            score.append(
+                (part.reshape(2, half, span) + bias[...][None]).reshape(2 * half, span)
+            )
+        expo = [
+            jnp.exp2(part - jnp.max(part, axis=1, keepdims=True)).astype(BF) for part in score
+        ]
+        for at, weights in zip(lanes, expo):
+            near_values = values[band, at]
+            total = dot(
+                weights, jnp.concatenate([near_values, jnp.ones_like(near_values)], axis=1)
+            )
+            part = total[:, :128] * (1.0 / total[:, 128:])
+            mixed[:, at] = jnp.where(low, part[:half], part[half:]).astype(BF)
+    out[...] = (latent[these, :].astype(F32) + dot(mixed[...], wo[...])).astype(BF)
+
+
+def window_outer_kernel(
+    ends, q, k, v, near, far, latent, wk, wv, wo, outer, keys, values, bias, mixed
 ):
     rows = q.shape[0]
-    half = rows // 2
-    span = half + WIN
     keys[rows : 2 * rows, :] = k[...]
     values[rows : 2 * rows, :] = v[...]
-    row = lax.broadcasted_iota(jnp.int32, (half, span), 0)
-    col = lax.broadcasted_iota(jnp.int32, (half, span), 1)
-    for side in range(2):
-        place = col + side * half
-        inside = (col >= row) & (col - row <= WIN) & (place >= ends[0]) & (place < ends[1])
-        bias[side] = jnp.where(inside, 0.0, NEG)
     halo = jnp.concatenate(sides(ends[2], near[...], far[...]), axis=0)
     for weight, wide in ((wk, keys), (wv, values)):
         both = dot(halo, weight[...]).astype(BF)
         wide[:rows, :] = both[:rows]
         wide[2 * rows :, :] = both[rows:]
-    low = low_half((1, 128))
-
-    for pair in range(PAIRS):
-        lanes = slice(pair * 128, pair * 128 + 128)
-        bands = [slice(side * half, side * half + span) for side in range(2)]
-        score = []
-        for side in range(2):
-            both = q[side * half : side * half + half, lanes]
-            zero = jnp.zeros_like(both)
-            stacked = jnp.concatenate(
-                [jnp.where(low, both, zero), jnp.where(low, zero, both)], axis=0
-            )
-            part = dot_t(stacked, keys[bands[side], lanes])
-            score.append(
-                (part.reshape(2, half, span) + bias[side][None]).reshape(2 * half, span)
-            )
-        expo = [
-            jnp.exp2(part - jnp.max(part, axis=1, keepdims=True)).astype(BF) for part in score
-        ]
-        for side in range(2):
-            near_values = values[bands[side], lanes]
-            total = dot(
-                expo[side], jnp.concatenate([near_values, jnp.ones_like(near_values)], axis=1)
-            )
-            part = total[:, :128] * (1.0 / total[:, 128:])
-            mixed[side * half : side * half + half, lanes] = jnp.where(
-                low, part[:half], part[half:]
-            ).astype(BF)
-    out[...] = (latent[...].astype(F32) + dot(mixed[...], wo[...])).astype(BF)
-    inner[...], outer[...] = sides(ends[2], out[:BL, :], out[rows - BL :, :])
+    window_half(ends[2], ends, q, keys, values, latent, wo, bias, mixed, outer)
+
+
+def window_inner_kernel(ends, q, keys, values, latent, wo, inner, bias, mixed):
+    window_half(1 - ends[2], ends, q, keys, values, latent, wo, bias, mixed, inner)
 
 
 CHUNK = 128
@@ -211,16 +224,17 @@
             ]
 
 
-def prepare_kernel(own, state, aq, wk, wv, q, k, v):
-    to_tiles(own[...], wk, k, 0)
-    to_tiles(own[...], wv, v, 0)
+def prepare_kernel(ends, inner, outer, state, aq, wk, wv, q, k, v):
+    own = jnp.concatenate(sides(ends[2], inner[...], outer[...]), axis=0)
+    to_tiles(own, wk, k, 0)
+    to_tiles(own, wv, v, 0)
     points = state.shape[1]
     for first in range(0, points, 512):
         to_tiles(state[:, first : first + 512].astype(F32).T.astype(BF), aq, q, first)
 
 
 def decode_kernel(
-    ends, idx, near, far, ko, vo, q, grid, bo, co, wk, wv, out, kf, vf, prod, wts, dec
+    ends, idx, far, near, ko, vo, q, grid, bo, co, wk, wv, out, kf, vf, prod, wts, dec
 ):
     points = grid.shape[1]
     side = near.shape[0]
@@ -281,19 +295,24 @@
         out[:, first : first + block] = result[: out.shape[0], :].astype(BF)
 
 
+def pass_kernel(given, same):
+    pass
+
+
 def shape(dims, kind=BF):
     return jax.ShapeDtypeStruct(dims, kind)
 
 
-def swap(inner, outer):
+def swap_near(inner):
+    return lax.ppermute(inner, "narrow", [(0, 1), (1, 0)])
+
+
+def swap_far(outer):
     axes = ("wide", "narrow")
-    count = lax.axis_size(axes)
     pairs = []
-    for i in range(1, count - 1, 2):
+    for i in range(1, lax.axis_size(axes) - 1, 2):
         pairs += [(i, i + 1), (i + 1, i)]
-    far = lax.ppermute(outer, axes, pairs)
-    near = lax.ppermute(inner, "narrow", [(0, 1), (1, 0)])
-    return near, far
+    return lax.ppermute(outer, axes, pairs)
 
 
 def on_device(
@@ -326,10 +345,8 @@
         axis=0,
     )
     core = lax.axis_index("narrow")
-    grid_near, grid_far = swap(
-        lax.dynamic_slice_in_dim(grid, (1 - core) * (points - BG), BG, 1),
-        lax.dynamic_slice_in_dim(grid, core * (points - BG), BG, 1),
-    )
+    grid_far = swap_far(lax.dynamic_slice_in_dim(grid, core * (points - BG), BG, 1))
+    grid_near = swap_near(lax.dynamic_slice_in_dim(grid, (1 - core) * (points - BG), BG, 1))
     win = jnp.pad(w_in, ((0, CPAD - channels), (0, 0)))
     wout = jnp.pad(w_out.T, ((0, CPAD - channels), (0, 0)))
     scale = jnp.repeat(logit_scale * (LOG2E / math.sqrt(SIZE)), SIZE, axis=1)
@@ -351,48 +368,71 @@
         name="fold",
     )(win, enc_w, latent_init, scale, wout, enc_idx, bias, dec_idx, ends)
     square = shape((width, width))
-    latent, normed, pw0, pw1, pw2, pw3, dw0, dw1, dw2, dw3 = pl.pallas_call(
+    latent, normed, pw0, pw1, pw2 = pl.pallas_call(
         encode_kernel,
-        out_shape=(shape((rows, width)),) * 2 + (square,) * 8,
-        in_specs=[SM] * 2 + [VM] * 7 + [HBM] * 3,
-        out_specs=(VM,) * 10,
+        out_shape=(shape((rows, width)),) * 2 + (square,) * 3,
+        in_specs=[SM] * 2 + [VM] * 7 + [HBM] * 2,
+        out_specs=(VM,) * 5,
         scratch_shapes=[
             pltpu.VMEM((points + 2 * BG, CPAD), F32),
             pltpu.VMEM((slots * 16, CPAD), F32),
             pltpu.VMEM((slots * 16, CPAD), F32),
             pltpu.VMEM((HEADS, rows, CPAD), BF),
             weight,
-            dma((9,)),
+            dma((4,)),
         ],
-        compiler_params=params(28),
+        compiler_params=params(48),
         name="encode",
-    )(ends, enc_idx, grid_near, grid, grid_far, qt, bias, av, latent_init, enc_w, proc_w, dec_w)
-    normed_near, normed_far = swap(normed, normed)
-    q, k, v, aq, bo, co = pl.pallas_call(
+    )(ends, enc_idx, grid_near, grid, grid_far, qt, bias, av, latent_init, enc_w, proc_w)
+    normed_far = swap_far(normed)
+    normed_near = swap_near(normed)
+    q, k, v, aq, bo, co, pw3, dw1, dw2 = pl.pallas_call(
         project_kernel,
         out_shape=(shape((rows, width)),) * 3
-        + (shape((CPAD, width)), shape((width, CPAD)), shape((CPAD, CPAD))),
-        in_specs=[VM] * 9,
-        out_specs=(VM,) * 6,
+        + (shape((CPAD, width)), shape((width, CPAD)), shape((CPAD, CPAD)))
+        + (square,) * 3,
+        in_specs=[VM] * 7 + [HBM] * 2,
+        out_specs=(VM,) * 9,
+        scratch_shapes=[weight] * 2 + [dma((5,))],
+        compiler_params=params(40),
+        cost_estimate=pl.CostEstimate(flops=3 * 10**9, bytes_accessed=12 * 2**20, transcendentals=0),
+        name="project",
+    )(normed, win, wout, scale, pw0, pw1, pw2, proc_w, dec_w)
+    half_scratch = [
+        pltpu.VMEM((rows // 2, rows // 2 + WIN), F32),
+        pltpu.VMEM((rows // 2, width), BF),
+    ]
+    wide = shape((rows + WIN, width))
+    mesh_outer, keys, values = pl.pallas_call(
+        window_outer_kernel,
+        out_shape=(shape((BL, width)), wide, wide),
+        in_specs=[SM] + [VM] * 9,
+        out_specs=(VM,) * 3,
+        scratch_shapes=half_scratch,
+        compiler_params=params(24),
+        name="window_outer",
+    )(ends, q, k, v, normed_near, normed_far, latent, pw1, pw2, pw3)
+    mesh_far = swap_far(mesh_outer)
+    mesh_inner = pl.pallas_call(
+        window_inner_kernel,
+        out_shape=shape((BL, width)),
+        in_specs=[SM] + [VM] * 5,
+        out_specs=VM,
+        scratch_shapes=half_scratch,
         compiler_params=params(24),
         cost_estimate=pl.CostEstimate(flops=3 * 10**9, bytes_accessed=12 * 2**20, transcendentals=0),
-        name="project",
-    )(normed, win, wout, scale, pw0, pw1, pw2, dw0, dw3)
-    latent_out, mesh_inner, mesh_outer = pl.pallas_call(
-        window_kernel,
-        out_shape=(shape((rows, width)), shape((BL, width)), shape((BL, width))),
-        in_specs=[SM] + [VM] * 9,
-        out_specs=(VM,) * 3,
-        scratch_shapes=[
-            pltpu.VMEM((rows + WIN, width), BF),
-            pltpu.VMEM((rows + WIN, width), BF),
-            pltpu.VMEM((2, rows // 2, rows // 2 + WIN), F32),
-            pltpu.VMEM((rows, width), BF),
-        ],
-        compiler_params=params(24),
-        name="window",
-    )(ends, q, k, v, normed_near, normed_far, latent, pw1, pw2, pw3)
-    mesh_near, mesh_far = swap(mesh_inner, mesh_outer)
+        name="window_inner",
+    )(ends, q, keys, values, latent, pw3)
+    mesh_near = swap_near(mesh_inner)
+    mesh_far = pl.pallas_call(
+        pass_kernel,
+        out_shape=shape((BL, width)),
+        in_specs=[pl.BlockSpec(memory_space=pl.ANY)],
+        out_specs=pl.BlockSpec(memory_space=pl.ANY),
+        input_output_aliases={0: 0},
+        compiler_params=params(16),
+        name="pass",
+    )(mesh_far)
     nodes = rows + 2 * BL
     dq, dk, dv = pl.pallas_call(
         prepare_kernel,
@@ -401,12 +441,12 @@
             shape((rows * 8, 128), F32),
             shape((rows * 8, 128), F32),
         ),
-        in_specs=[VM] * 5,
+        in_specs=[SM] + [VM] * 6,
         out_specs=(VM,) * 3,
         compiler_params=params(24),
-        cost_estimate=pl.CostEstimate(flops=3 * 10**9, bytes_accessed=12 * 2**20, transcendentals=0),
+        cost_estimate=pl.CostEstimate(flops=10**6, bytes_accessed=2**16, transcendentals=0),
         name="prepare",
-    )(latent_out, grid, aq, dw1, dw2)
+    )(ends, mesh_inner, mesh_outer, grid, aq, dw1, dw2)
     out = pl.pallas_call(
         decode_kernel,
         out_shape=shape((channels, points)),
@@ -421,7 +461,7 @@
         ],
         compiler_params=params(32),
         name="decode",
-    )(ends, dec_idx, mesh_near, mesh_far, dk, dv, dq, grid, bo, co, dw1, dw2)
+    )(ends, dec_idx, mesh_far, mesh_near, dk, dv, dq, grid, bo, co, dw1, dw2)
     return out.T
 
 

time: 80.7 us -> 77.5 us (0.960)
  waiting for transfers between devices: 11.9 us -> 1.93 us
  Pallas kernels: 47.8 us -> 52.2 us
  local copies, waits for them, and re-layouts: 2.62 us -> 4.21 us
    ppermute x6, waiting for transfers between devices: 11.9 us -> 1.93 us  [the longest x3 1.92 us: swap_far(): return lax.ppermute(outer, axes, pairs)]
    pallas_call x1, Pallas kernels: 2.71 us -> 6.56 us  [on_device(): pl.pallas_call(project_kernel, out_shape=(shape((rows, width)),) * 3 + (s...]
    unnamed x13 -> x17, local copies, waits for them, and re-layouts: 1.25 us -> 2.83 us
    pallas_call x1, Pallas kernels: 11.1 us -> 10 us  [on_device(): pl.pallas_call(encode_kernel, out_shape=(shape((rows, width)),) * 2 + (sq...]
    pallas_call x1, Pallas kernels: 2.8 us -> 3.68 us  [on_device(): pl.pallas_call(prepare_kernel, out_shape=(shape((points * 8, 128), F32),...]
    pallas_call x1 -> x3, Pallas kernels: 8.48 us -> 9.26 us  [the longest x1 5.73 us: on_device(): pl.pallas_call(window_outer_kernel, out_shape=(shape((BL, width)), wide,...]
  transfers between devices with their start and end apart: 6 -> 6, of which waited for: 2 -> 1; matrix products, arithmetic and copies ran while one was open for 2% -> 3% of each run, Pallas kernels for 13% -> 25%
where the time goes in v7:
time: 77.5 us; the launch traced here: 76.5 us
  Pallas kernels  52.2 us (67%)
  starting transfers between devices  15.8 us (20%)
  local copies, waits for them, and re-layouts  4.21 us (5%)
  other arithmetic  2.12 us (3%)
  waiting for transfers between devices  1.93 us (2%)
    pallas_call x1, Pallas kernels, on_device(): pl.pallas_call(decode_kernel, out_shape=shape((channels, points)), in_spe...  17.3 us
    ppermute x3, starting transfers between devices, swap_far(): return lax.ppermute(outer, axes, pairs)  15.1 us
    pallas_call x1, Pallas kernels, on_device(): pl.pallas_call(encode_kernel, out_shape=(shape((rows, width)),) * 2 + (sq...  10 us
    pallas_call x1, Pallas kernels, on_device(): pl.pallas_call(project_kernel, out_shape=(shape((rows, width)),) * 3 + (s...  6.56 us
    pallas_call x1, Pallas kernels, on_device(): pl.pallas_call(window_outer_kernel, out_shape=(shape((BL, width)), wide,...  5.73 us
    pallas_call x1, Pallas kernels, on_device(): pl.pallas_call(fold_kernel, out_shape=(shape((HEADS, rows, CPAD)), shape(...  5.33 us
    pallas_call x1, Pallas kernels, on_device(): pl.pallas_call(prepare_kernel, out_shape=(shape((points * 8, 128), F32),...  3.68 us
    pallas_call x1, Pallas kernels, on_device(): pl.pallas_call(window_inner_kernel, out_shape=shape((BL, width)), in_spec...  3.53 us
  transfers between devices with their start and end apart: 6, of which 1 were waited for; matrix products, arithmetic and copies ran while one was open for 3% of the time, Pallas kernels for 25%

profile of v7, /device:TPU:96, one launch (start us, length us, event | category | flops | bytes accessed | tf_op | source)
XLA Modules:
  0.0 76.5 jit_solution(4560310247300466745)
XLA Ops:
  0.0 0.0 copy-start.7
  0.0 0.0 copy-start.6
  0.0 0.0 copy-start.4
  0.0 0.0 copy-start.5
  0.0 0.1 pad.10.clone
  0.1 0.1 pad.11.clone
  0.2 1.3 %maximum_maximum_fusion.own.state.grid = bf16[128,2048]{1,0:T(8,128)(2,1)S(1)} fusion(bf16[100,2048]{1,0:T(8,128)(2,1)} %bitcast.15, bf16[128]{0:T(256)(128)(2,1)S(1)} %pad.11.clone, bf16[128]{0:T(256)(128)(2,1)S(1)} %pad.10.clone), kind=kLoop, calls=%fused_computation | loop fusion | flops 1572864 | bytes 934400 | tf_op jit(solution)/shard_map/concatenate | solution.py:339
  1.6 6.4 %collective-permute-start.1 = (bf16[128,1024]{1,0:T(8,128)(2,1)S(1)}, bf16[128,1024]{1,0:T(8,128)(2,1)S(1)}, u32[]{:S(2)}, u32[]{:S(2)}) collective-permute-start(bf16[128,1024]{1,0:T(8,128)(2,1)S(1)} %get-tuple-element.49), channel_id=1, source_target_pairs={{1,2},{2,1},{3,4},{4,3},{5,6},{6,5},{7,8},{8,7},{9,10},{10,9},{11,... | collective-permute-start | bytes 786440 | tf_op jit(solution)/shard_map/ppermute | solution.py:315
  8.0 0.1 collective-permute-start
  8.1 0.7 broadcast_multiply_fusion
  8.8 0.8 lt.35
  9.5 0.1 lt.33
  9.6 0.0 copy-done.7
  9.6 0.1 broadcast_in_dim.21
  9.7 0.1 reshape.23.scale
  9.8 0.0 copy-done.6
  9.9 0.1 lt.37
  10.0 0.0 copy-done.4
  10.0 0.0 copy-done.5
  10.1 0.1 pad_add_fusion.others_4_.ends
  10.2 0.0 copy-start.2
  10.2 5.3 %fold.1 = (bf16[16,256,128]{2,1,0:T(8,128)(2,1)}, bf16[128,1024]{1,0:T(8,128)(2,1)S(1)}) custom-call(bf16[128,1024]{1,0:T(8,128)(2,1)S(1)} %pad.7.win, bf16[4,1024,1024]{2,1,0:T(8,128)(2,1)} %enc_w.3, bf16[256,1024]{1,0:T(8,128)(2,1)} %lat.3, f32[3,1024]{1,0:T(4,128)S(1)} %reshape.23.scale, bf16[128,1024]{1,0:T(8,128)(2,1)S(1)} %pad.8.others_0_.wout, ...), custom_call_target="tpu_custom_call" | custom-call | flops 2000000000 | bytes 8388608 | tf_op jit(solution)/shard_map/fold/pallas_call | solution.py:360
  15.5 0.0 collective-permute-done.1.far
  15.5 0.0 collective-permute-done.near
  15.5 0.0 copy-done.2
  15.5 0.0 copy-start.3
  15.5 1.2 %copy-done.3 = bf16[16,256,128]{2,1,0:T(8,128)(2,1)S(1)} copy-done((bf16[16,256,128]{2,1,0:T(8,128)(2,1)S(1)}, bf16[16,256,128]{2,1,0:T(8,128)(2,1)}, u32[]{:S(2)}) %copy-start.3) | copy-done | bytes 1048600
  16.7 10.0 %encode.1 = (bf16[256,1024]{1,0:T(8,128)(2,1)S(1)}, bf16[256,1024]{1,0:T(8,128)(2,1)S(1)}, bf16[1024,1024]{1,0:T(8,128)(2,1)S(1)}, bf16[1024,1024]{1,0:T(8,128)(2,1)}, bf16[1024,1024]{1,0:T(8,128)(2,1)}) custom-call(s32[3]{0:T(128)S(1)} %pad_add_fusion.others_4_.ends, s32[4096]{0:T(1024)S(1)} %bitcast.14, bf16[128,1024]{1,0:T(8,128)(2,1)S(1)} %collective-permute-done.near, ...), custom_call_target="tpu_custom_call" | custom-call | tf_op jit(solution)/shard_map/encode/pallas_call | solution.py:371
  26.8 4.4 %collective-permute-start.3 = (bf16[256,1024]{1,0:T(8,128)(2,1)S(1)}, bf16[256,1024]{1,0:T(8,128)(2,1)S(1)}, u32[]{:S(2)}, u32[]{:S(2)}) collective-permute-start(bf16[256,1024]{1,0:T(8,128)(2,1)S(1)} %get-tuple-element.29.normed), channel_id=1, source_target_pairs={{1,2},{2,1},{3,4},{4,3},{5,6},{6,5},{7,8},{8,7},{9,10},{10,9},{11,... | collective-permute-start | bytes 1572872 | tf_op jit(solution)/shard_map/ppermute | solution.py:315
  31.2 0.3 collective-permute-start.2
  31.4 0.0 copy-start
  31.4 1.6 %copy-done = bf16[1024,1024]{1,0:T(8,128)(2,1)S(1)} copy-done((bf16[1024,1024]{1,0:T(8,128)(2,1)S(1)}, bf16[1024,1024]{1,0:T(8,128)(2,1)}, u32[]{:S(2)}) %copy-start) | copy-done | bytes 2097176
  33.0 0.0 copy-start.1
  33.0 6.6 %project.1 = (bf16[256,1024]{1,0:T(8,128)(2,1)S(1)}, bf16[256,1024]{1,0:T(8,128)(2,1)S(1)}, bf16[256,1024]{1,0:T(8,128)(2,1)S(1)}, bf16[128,1024]{1,0:T(8,128)(2...) custom-call(bf16[256,1024]{1,0:T(8,128)(2,1)S(1)} %get-tuple-element, ...), custom_call_target="tpu_custom_call" | custom-call | flops 3000000000 | bytes 12582912 | tf_op jit(solution)/shard_map/project/pallas_call | solution.py:389
  39.6 1.9 %collective-permute-done.3.far = bf16[256,1024]{1,0:T(8,128)(2,1)S(1)} collective-permute-done((bf16[256,1024]{1,0:T(8,128)(2,1)S(1)}, bf16[256,1024]{1,0:T(8,128)(2,1)S(1)}, u32[]{:S(2)}, u32[]{:S(2)}) %collective-permute-start.3) | collective-permute-done | bytes 524320 | tf_op jit(solution)/shard_map/ppermute | solution.py:315
  41.5 0.0 collective-permute-done.2.near
  41.5 0.0 copy-done.1
  41.5 5.7 %window_outer.1 = (bf16[128,1024]{1,0:T(8,128)(2,1)S(1)}, bf16[768,1024]{1,0:T(8,128)(2,1)S(1)}, bf16[768,1024]{1,0:T(8,128)(2,1)S(1)}) custom-call(s32[3]{0:T(128)S(1)} %pad_add_fusion.others_4_.ends, bf16[256,1024]{1,0:T(8,128)(2,1)S(1)} %get-tuple-element.33.q, bf16[256,1024]{1,0:T(8,128)(2,1)S(1)} %get-tuple-element.34.k, ...), custom_call_target="tpu_custom_call" | custom-call | tf_op jit(solution)/shard_map/window_outer/pallas_call | solution.py:406
  47.2 4.4 %collective-permute-start.4 = (bf16[128,1024]{1,0:T(8,128)(2,1)S(1)}, bf16[128,1024]{1,0:T(8,128)(2,1)S(1)}, u32[]{:S(2)}, u32[]{:S(2)}) collective-permute-start(bf16[128,1024]{1,0:T(8,128)(2,1)S(1)} %get-tuple-element.38.outer), channel_id=1, source_target_pairs={{1,2},{2,1},{3,4},{4,3},{5,6},{6,5},{7,8},{8,7},{9,10},{10,9},{11,... | collective-permute-start | bytes 786440 | tf_op jit(solution)/shard_map/ppermute | solution.py:315
  51.6 3.5 %window_inner.1.inner = bf16[128,1024]{1,0:T(8,128)(2,1)S(1)} custom-call(s32[3]{0:T(128)S(1)} %pad_add_fusion.others_4_.ends, bf16[256,1024]{1,0:T(8,128)(2,1)S(1)} %get-tuple-element.33.q, bf16[768,1024]{1,0:T(8,128)(2,1)S(1)} %get-tuple-element.39.keys, bf16[768,1024]{1,0:T(8,128)(2,1)S(1)} %get-tuple-element.40.values, ...), custom_call_target="tpu_custom_call" | custom-call | flops 3000000000 | bytes 12582912 | tf_op jit(solution)/shard_map/window_inner/pallas_call | solution.py:416
  55.1 0.3 collective-permute-start.5
  55.5 3.7 %prepare.1 = (f32[16384,128]{1,0:T(8,128)S(1)}, f32[2048,128]{1,0:T(8,128)S(1)}, f32[2048,128]{1,0:T(8,128)S(1)}) custom-call(s32[3]{0:T(128)S(1)} %pad_add_fusion.others_4_.ends, bf16[128,1024]{1,0:T(8,128)(2,1)S(1)} %window_inner.1.inner, bf16[128,1024]{1,0:T(8,128)(2,1)S(1)} %get-tuple-element.38.outer, ...), custom_call_target="tpu_custom_call" | custom-call | flops 1000000 | bytes 65536 | tf_op jit(solution)/shard_map/prepare/pallas_call | solution.py:437
  59.1 0.0 collective-permute-done.4.given
  59.2 0.0 collective-permute-done.5.near
  59.2 17.3 %decode.1 = bf16[100,2048]{1,0:T(8,128)(2,1)} custom-call(s32[3]{0:T(128)S(1)} %pad_add_fusion.others_4_.ends, s32[6144]{0:T(1024)S(1)} %mul.35.others_3_.idx, bf16[128,1024]{1,0:T(8,128)(2,1)S(1)} %pass.1.far, bf16[128,1024]{1,0:T(8,128)(2,1)S(1)} %collective-permute-done.5.near, f32[2048,128]{1,0:T(8,128)S(1)} %get-tuple-element.44.ko, ...), custom_call_target="tpu_custom_call" | custom-call | tf_op jit(solution)/shard_map/decode/pallas_call | solution.py:450
  (12 shorter events, 0.2 us)
Async XLA Ops:
  0.0 9.6 %copy-start.7 = (s32[256,16]{0,1:T(8,128)S(1)}, s32[256,16]{0,1:T(8,128)}, u32[]{:S(2)}) copy-start(s32[256,16]{0,1:T(8,128)} %param.13) | copy-start | bytes 49156
  0.0 9.8 %copy-start.6 = (s32[2048,3]{0,1:T(4,128)S(1)}, s32[2048,3]{0,1:T(4,128)}, u32[]{:S(2)}) copy-start(s32[2048,3]{0,1:T(4,128)} %param.15) | copy-start | bytes 73732
  0.0 10.0 %copy-start.4 = (bf16[100,1024]{1,0:T(8,128)(2,1)S(1)}, bf16[100,1024]{1,0:T(8,128)(2,1)}, u32[]{:S(2)}) copy-start(bf16[100,1024]{1,0:T(8,128)(2,1)} %param.16) | copy-start | bytes 614404
  0.0 10.0 %copy-start.5 = (bf16[1024,100]{0,1:T(8,128)(2,1)S(1)}, bf16[1024,100]{0,1:T(8,128)(2,1)}, u32[]{:S(2)}) copy-start(bf16[1024,100]{0,1:T(8,128)(2,1)} %param.20) | copy-start | bytes 614404
  1.6 13.9 %collective-permute-start.1 = (bf16[128,1024]{1,0:T(8,128)(2,1)S(1)}, bf16[128,1024]{1,0:T(8,128)(2,1)S(1)}, u32[]{:S(2)}, u32[]{:S(2)}) collective-permute-start(bf16[128,1024]{1,0:T(8,128)(2,1)S(1)} %get-tuple-element.49), channel_id=1, source_target_pairs={{1,2},{2,1},{3,4},{4,3},{5,6},{6,5},{7,8},{8,7},{9,10},{10,9},{11,... | collective-permute-start | bytes 786440 | tf_op jit(solution)/shard_map/ppermute | solution.py:315
  8.0 7.5 %collective-permute-start = (bf16[128,1024]{1,0:T(8,128)(2,1)S(1)}, bf16[128,1024]{1,0:T(8,128)(2,1)S(1)}, u32[]{:S(2)}, u32[]{:S(2)}) collective-permute-start(bf16[128,1024]{1,0:T(8,128)(2,1)S(1)} %get-tuple-element.50), channel_id=1, source_target_pairs={{0,1},{1,0},{2,3},{3,2},{4,5},{5,4},{6,7},{7,6},{8,9},{9,8},{10,11... | collective-permute-start | bytes 786440 | tf_op jit(solution)/shard_map/ppermute | solution.py:307
  10.2 5.4 %copy-start.2 = (bf16[256,1024]{1,0:T(8,128)(2,1)S(1)}, bf16[256,1024]{1,0:T(8,128)(2,1)}, u32[]{:S(2)}) copy-start(bf16[256,1024]{1,0:T(8,128)(2,1)} %lat.3) | copy-start | bytes 1572868
  15.5 1.2 %copy-start.3 = (bf16[16,256,128]{2,1,0:T(8,128)(2,1)S(1)}, bf16[16,256,128]{2,1,0:T(8,128)(2,1)}, u32[]{:S(2)}) copy-start(bf16[16,256,128]{2,1,0:T(8,128)(2,1)} %get-tuple-element.27.qt) | copy-start | bytes 3145732
  26.8 14.7 %collective-permute-start.3 = (bf16[256,1024]{1,0:T(8,128)(2,1)S(1)}, bf16[256,1024]{1,0:T(8,128)(2,1)S(1)}, u32[]{:S(2)}, u32[]{:S(2)}) collective-permute-start(bf16[256,1024]{1,0:T(8,128)(2,1)S(1)} %get-tuple-element.29.normed), channel_id=1, source_target_pairs={{1,2},{2,1},{3,4},{4,3},{5,6},{6,5},{7,8},{8,7},{9,10},{10,9},{11,... | collective-permute-start | bytes 1572872 | tf_op jit(solution)/shard_map/ppermute | solution.py:315
  31.2 10.4 %collective-permute-start.2 = (bf16[256,1024]{1,0:T(8,128)(2,1)S(1)}, bf16[256,1024]{1,0:T(8,128)(2,1)S(1)}, u32[]{:S(2)}, u32[]{:S(2)}) collective-permute-start(bf16[256,1024]{1,0:T(8,128)(2,1)S(1)} %get-tuple-element.29.normed), channel_id=1, source_target_pairs={{0,1},{1,0},{2,3},{3,2},{4,5},{5,4},{6,7},{7,6},{8,9},{9,8},{10,11... | collective-permute-start | bytes 1572872 | tf_op jit(solution)/shard_map/ppermute | solution.py:307
  31.4 1.6 %copy-start = (bf16[1024,1024]{1,0:T(8,128)(2,1)S(1)}, bf16[1024,1024]{1,0:T(8,128)(2,1)}, u32[]{:S(2)}) copy-start(bf16[1024,1024]{1,0:T(8,128)(2,1)} %get-tuple-element.31.wk) | copy-start | bytes 6291460
  33.0 8.5 %copy-start.1 = (bf16[1024,1024]{1,0:T(8,128)(2,1)S(1)}, bf16[1024,1024]{1,0:T(8,128)(2,1)}, u32[]{:S(2)}) copy-start(bf16[1024,1024]{1,0:T(8,128)(2,1)} %get-tuple-element.32.wv) | copy-start | bytes 6291460
  47.2 11.9 %collective-permute-start.4 = (bf16[128,1024]{1,0:T(8,128)(2,1)S(1)}, bf16[128,1024]{1,0:T(8,128)(2,1)S(1)}, u32[]{:S(2)}, u32[]{:S(2)}) collective-permute-start(bf16[128,1024]{1,0:T(8,128)(2,1)S(1)} %get-tuple-element.38.outer), channel_id=1, source_target_pairs={{1,2},{2,1},{3,4},{4,3},{5,6},{6,5},{7,8},{8,7},{9,10},{10,9},{11,... | collective-permute-start | bytes 786440 | tf_op jit(solution)/shard_map/ppermute | solution.py:315
  55.1 4.0 %collective-permute-start.5 = (bf16[128,1024]{1,0:T(8,128)(2,1)S(1)}, bf16[128,1024]{1,0:T(8,128)(2,1)S(1)}, u32[]{:S(2)}, u32[]{:S(2)}) collective-permute-start(bf16[128,1024]{1,0:T(8,128)(2,1)S(1)} %window_inner.1.inner), channel_id=1, source_target_pairs={{0,1},{1,0},{2,3},{3,2},{4,5},{5,4},{6,7},{7,6},{8,9},{9,8},{10,11... | collective-permute-start | bytes 786440 | tf_op jit(solution)/shard_map/ppermute | solution.py:307

commit v8 on v7

--- a/solution.py
+++ b/solution.py
@@ -363,7 +363,7 @@
         in_specs=[VM, HBM, VM, VM] + [pl.BlockSpec(memory_space=pl.ANY)] * 5,
         out_specs=(VM, VM),
         scratch_shapes=[weight] * 3 + [dma((3,))],
-        compiler_params=params(53),
+        compiler_params=params(50),
         cost_estimate=pl.CostEstimate(flops=2 * 10**9, bytes_accessed=8 * 2**20, transcendentals=0),
         name="fold",
     )(win, enc_w, latent_init, scale, wout, enc_idx, bias, dec_idx, ends)
@@ -381,7 +381,7 @@
             weight,
             dma((4,)),
         ],
-        compiler_params=params(48),
+        compiler_params=params(44),
         name="encode",
     )(ends, enc_idx, grid_near, grid, grid_far, qt, bias, av, latent_init, enc_w, proc_w)
     normed_far = swap_far(normed)
@@ -394,7 +394,7 @@
         in_specs=[VM] * 7 + [HBM] * 2,
         out_specs=(VM,) * 9,
         scratch_shapes=[weight] * 2 + [dma((5,))],
-        compiler_params=params(40),
+        compiler_params=params(36),
         cost_estimate=pl.CostEstimate(flops=3 * 10**9, bytes_accessed=12 * 2**20, transcendentals=0),
         name="project",
     )(normed, win, wout, scale, pw0, pw1, pw2, proc_w, dec_w)

time: 77.5 us -> 74.4 us (0.960)
  Pallas kernels: 52.2 us -> 47.9 us
  starting transfers between devices: 15.8 us -> 19 us
  local copies, waits for them, and re-layouts: 4.21 us -> 1.41 us
  waiting for transfers between devices: 1.93 us -> 2.73 us
    ppermute x3, starting transfers between devices: 15.1 us -> 18.4 us  [swap_far(): return lax.ppermute(outer, axes, pairs)]
    unnamed x17 -> x11, local copies, waits for them, and re-layouts: 2.83 us -> 0.03 us
    pallas_call x1, Pallas kernels: 10 us -> 8.07 us  [on_device(): pl.pallas_call(encode_kernel, out_shape=(shape((rows, width)),) * 2 + (sq...]
    pallas_call x1, Pallas kernels: 5.33 us -> 3.69 us  [on_device(): pl.pallas_call(fold_kernel, out_shape=(shape((HEADS, rows, CPAD)), shape(...]
    pallas_call x1, Pallas kernels: 6.56 us -> 5.71 us  [on_device(): pl.pallas_call(project_kernel, out_shape=(shape((rows, width)),) * 3 + (s...]
    ppermute x3, waiting for transfers between devices: 1.92 us -> 2.72 us  [swap_far(): return lax.ppermute(outer, axes, pairs)]
  transfers between devices with their start and end apart: 6 -> 6, of which waited for: 1 -> 1; matrix products, arithmetic and copies ran while one was open for 3% -> 3% of each run, Pallas kernels for 25% -> 23%
where the time goes in v8:
time: 74.4 us; the launch traced here: 73.6 us
  Pallas kernels  47.9 us (64%)
  starting transfers between devices  19 us (26%)
  waiting for transfers between devices  2.73 us (4%)
  other arithmetic  2.26 us (3%)
  local copies, waits for them, and re-layouts  1.41 us (2%)
    ppermute x3, starting transfers between devices, swap_far(): return lax.ppermute(outer, axes, pairs)  18.4 us
    pallas_call x1, Pallas kernels, on_device(): pl.pallas_call(decode_kernel, out_shape=shape((channels, points)), in_spe...  17.4 us
    pallas_call x1, Pallas kernels, on_device(): pl.pallas_call(encode_kernel, out_shape=(shape((rows, width)),) * 2 + (sq...  8.07 us
    pallas_call x1, Pallas kernels, on_device(): pl.pallas_call(window_outer_kernel, out_shape=(shape((BL, width)), wide,...  5.76 us
    pallas_call x1, Pallas kernels, on_device(): pl.pallas_call(project_kernel, out_shape=(shape((rows, width)),) * 3 + (s...  5.71 us
    pallas_call x1, Pallas kernels, on_device(): pl.pallas_call(fold_kernel, out_shape=(shape((HEADS, rows, CPAD)), shape(...  3.69 us
    pallas_call x1, Pallas kernels, on_device(): pl.pallas_call(prepare_kernel, out_shape=(shape((points * 8, 128), F32),...  3.67 us
    pallas_call x1, Pallas kernels, on_device(): pl.pallas_call(window_inner_kernel, out_shape=shape((BL, width)), in_spec...  3.58 us
  transfers between devices with their start and end apart: 6, of which 1 were waited for; matrix products, arithmetic and copies ran while one was open for 3% of the time, Pallas kernels for 23%

profile of v8, /device:TPU:96, one launch (start us, length us, event | category | flops | bytes accessed | tf_op | source)
XLA Modules:
  0.0 73.6 jit_solution(2615274834772000987)
XLA Ops:
  0.0 0.0 copy-start.4
  0.0 0.0 copy-start.3
  0.0 0.0 copy-start.1
  0.0 0.0 copy-start.2
  0.0 0.0 copy-start
  0.0 0.1 pad.10.clone
  0.1 0.1 pad.11.clone
  0.2 1.5 %maximum_maximum_fusion.own.state.grid = bf16[128,2048]{1,0:T(8,128)(2,1)S(1)} fusion(bf16[100,2048]{1,0:T(8,128)(2,1)} %bitcast.15, bf16[128]{0:T(256)(128)(2,1)S(1)} %pad.11.clone, bf16[128]{0:T(256)(128)(2,1)S(1)} %pad.10.clone), kind=kLoop, calls=%fused_computation | loop fusion | flops 1572864 | bytes 934400 | tf_op jit(solution)/shard_map/concatenate | solution.py:339
  1.7 6.4 %collective-permute-start.1 = (bf16[128,1024]{1,0:T(8,128)(2,1)S(1)}, bf16[128,1024]{1,0:T(8,128)(2,1)S(1)}, u32[]{:S(2)}, u32[]{:S(2)}) collective-permute-start(bf16[128,1024]{1,0:T(8,128)(2,1)S(1)} %get-tuple-element.49), channel_id=1, source_target_pairs={{1,2},{2,1},{3,4},{4,3},{5,6},{6,5},{7,8},{8,7},{9,10},{10,9},{11,... | collective-permute-start | bytes 786440 | tf_op jit(solution)/shard_map/ppermute | solution.py:315
  8.1 0.1 collective-permute-start
  8.2 0.7 broadcast_multiply_fusion
  8.9 0.8 %lt.35 = s32[16,16]{1,0:T(8,128)S(1)} reshape(s32[256]{0:T(256)} %param.14) | data formatting | bytes 2048 | tf_op jit(solution)/shard_map/lt | solution.py:354
  9.7 0.1 lt.33
  9.8 0.0 copy-done.4
  9.8 0.1 broadcast_in_dim.21
  9.9 0.1 reshape.23.scale
  9.9 0.0 copy-done.3
  10.0 0.1 lt.37
  10.1 0.0 copy-done.1
  10.2 0.0 copy-done.2
  10.2 0.1 pad_add_fusion.others_4_.ends
  10.3 0.0 copy-done
  10.3 3.7 %fold.1 = (bf16[16,256,128]{2,1,0:T(8,128)(2,1)S(1)}, bf16[128,1024]{1,0:T(8,128)(2,1)S(1)}) custom-call(bf16[128,1024]{1,0:T(8,128)(2,1)S(1)} %pad.7.win, bf16[4,1024,1024]{2,1,0:T(8,128)(2,1)} %enc_w.3, bf16[256,1024]{1,0:T(8,128)(2,1)S(1)} %copy-done, f32[3,1024]{1,0:T(4,128)S(1)} %reshape.23.scale, bf16[128,1024]{1,0:T(8,128)(2,1)S(1)} %pad.8.others_0_.wout, ...), custom_call_target="tpu_custom_call" | custom-call | flops 2000000000 | bytes 8388608 | tf_op jit(solution)/shard_map/fold/pallas_call | solution.py:360
  14.0 0.0 collective-permute-done.1.far
  14.0 0.0 collective-permute-done.near
  14.0 8.1 %encode.1 = (bf16[256,1024]{1,0:T(8,128)(2,1)S(1)}, bf16[256,1024]{1,0:T(8,128)(2,1)S(1)}, bf16[1024,1024]{1,0:T(8,128)(2,1)S(1)}, bf16[1024,1024]{1,0:T(8,128)(2,1)S(1)}, bf16[1024,1024]{1,0:T(8,128)(2,1)S(1)}) custom-call(s32[3]{0:T(128)S(1)} %pad_add_fusion.others_4_.ends, s32[4096]{0:T(1024)S(1)} %bitcast.14, ...), custom_call_target="tpu_custom_call" | custom-call | tf_op jit(solution)/shard_map/encode/pallas_call | solution.py:371
  22.1 6.0 %collective-permute-start.3 = (bf16[256,1024]{1,0:T(8,128)(2,1)S(1)}, bf16[256,1024]{1,0:T(8,128)(2,1)S(1)}, u32[]{:S(2)}, u32[]{:S(2)}) collective-permute-start(bf16[256,1024]{1,0:T(8,128)(2,1)S(1)} %get-tuple-element.29.normed), channel_id=1, source_target_pairs={{1,2},{2,1},{3,4},{4,3},{5,6},{6,5},{7,8},{8,7},{9,10},{10,9},{11,... | collective-permute-start | bytes 1572872 | tf_op jit(solution)/shard_map/ppermute | solution.py:315
  28.1 0.3 collective-permute-start.2
  28.4 5.7 %project.1 = (bf16[256,1024]{1,0:T(8,128)(2,1)S(1)}, bf16[256,1024]{1,0:T(8,128)(2,1)S(1)}, bf16[256,1024]{1,0:T(8,128)(2,1)S(1)}, bf16[128,1024]{1,0:T(8,128)(2...) custom-call(bf16[256,1024]{1,0:T(8,128)(2,1)S(1)} %get-tuple-element, ...), custom_call_target="tpu_custom_call" | custom-call | flops 3000000000 | bytes 12582912 | tf_op jit(solution)/shard_map/project/pallas_call | solution.py:389
  34.1 2.7 %collective-permute-done.3.far = bf16[256,1024]{1,0:T(8,128)(2,1)S(1)} collective-permute-done((bf16[256,1024]{1,0:T(8,128)(2,1)S(1)}, bf16[256,1024]{1,0:T(8,128)(2,1)S(1)}, u32[]{:S(2)}, u32[]{:S(2)}) %collective-permute-start.3) | collective-permute-done | bytes 524320 | tf_op jit(solution)/shard_map/ppermute | solution.py:315
  36.8 0.0 collective-permute-done.2.near
  36.8 5.8 %window_outer.1 = (bf16[128,1024]{1,0:T(8,128)(2,1)S(1)}, bf16[768,1024]{1,0:T(8,128)(2,1)S(1)}, bf16[768,1024]{1,0:T(8,128)(2,1)S(1)}) custom-call(s32[3]{0:T(128)S(1)} %pad_add_fusion.others_4_.ends, bf16[256,1024]{1,0:T(8,128)(2,1)S(1)} %get-tuple-element.33.q, bf16[256,1024]{1,0:T(8,128)(2,1)S(1)} %get-tuple-element.34.k, ...), custom_call_target="tpu_custom_call" | custom-call | tf_op jit(solution)/shard_map/window_outer/pallas_call | solution.py:406
  42.6 6.0 %collective-permute-start.4 = (bf16[128,1024]{1,0:T(8,128)(2,1)S(1)}, bf16[128,1024]{1,0:T(8,128)(2,1)S(1)}, u32[]{:S(2)}, u32[]{:S(2)}) collective-permute-start(bf16[128,1024]{1,0:T(8,128)(2,1)S(1)} %get-tuple-element.38.outer), channel_id=1, source_target_pairs={{1,2},{2,1},{3,4},{4,3},{5,6},{6,5},{7,8},{8,7},{9,10},{10,9},{11,... | collective-permute-start | bytes 786440 | tf_op jit(solution)/shard_map/ppermute | solution.py:315
  48.6 3.6 %window_inner.1.inner = bf16[128,1024]{1,0:T(8,128)(2,1)S(1)} custom-call(s32[3]{0:T(128)S(1)} %pad_add_fusion.others_4_.ends, bf16[256,1024]{1,0:T(8,128)(2,1)S(1)} %get-tuple-element.33.q, bf16[768,1024]{1,0:T(8,128)(2,1)S(1)} %get-tuple-element.39.keys, bf16[768,1024]{1,0:T(8,128)(2,1)S(1)} %get-tuple-element.40.values, ...), custom_call_target="tpu_custom_call" | custom-call | flops 3000000000 | bytes 12582912 | tf_op jit(solution)/shard_map/window_inner/pallas_call | solution.py:416
  52.2 0.3 collective-permute-start.5
  52.5 3.7 %prepare.1 = (f32[16384,128]{1,0:T(8,128)S(1)}, f32[2048,128]{1,0:T(8,128)S(1)}, f32[2048,128]{1,0:T(8,128)S(1)}) custom-call(s32[3]{0:T(128)S(1)} %pad_add_fusion.others_4_.ends, bf16[128,1024]{1,0:T(8,128)(2,1)S(1)} %window_inner.1.inner, bf16[128,1024]{1,0:T(8,128)(2,1)S(1)} %get-tuple-element.38.outer, ...), custom_call_target="tpu_custom_call" | custom-call | flops 1000000 | bytes 65536 | tf_op jit(solution)/shard_map/prepare/pallas_call | solution.py:437
  56.2 0.0 collective-permute-done.4.given
  56.2 0.0 collective-permute-done.5.near
  56.2 17.4 %decode.1 = bf16[100,2048]{1,0:T(8,128)(2,1)} custom-call(s32[3]{0:T(128)S(1)} %pad_add_fusion.others_4_.ends, s32[6144]{0:T(1024)S(1)} %mul.35.others_3_.idx, bf16[128,1024]{1,0:T(8,128)(2,1)S(1)} %pass.1.far, bf16[128,1024]{1,0:T(8,128)(2,1)S(1)} %collective-permute-done.5.near, f32[2048,128]{1,0:T(8,128)S(1)} %get-tuple-element.44.ko, ...), custom_call_target="tpu_custom_call" | custom-call | tf_op jit(solution)/shard_map/decode/pallas_call | solution.py:450
  (12 shorter events, 0.2 us)
Async XLA Ops:
  0.0 9.8 %copy-start.4 = (s32[256,16]{0,1:T(8,128)S(1)}, s32[256,16]{0,1:T(8,128)}, u32[]{:S(2)}) copy-start(s32[256,16]{0,1:T(8,128)} %param.13) | copy-start | bytes 49156
  0.0 9.9 %copy-start.3 = (s32[2048,3]{0,1:T(4,128)S(1)}, s32[2048,3]{0,1:T(4,128)}, u32[]{:S(2)}) copy-start(s32[2048,3]{0,1:T(4,128)} %param.15) | copy-start | bytes 73732
  0.0 10.1 %copy-start.1 = (bf16[100,1024]{1,0:T(8,128)(2,1)S(1)}, bf16[100,1024]{1,0:T(8,128)(2,1)}, u32[]{:S(2)}) copy-start(bf16[100,1024]{1,0:T(8,128)(2,1)} %param.16) | copy-start | bytes 614404
  0.0 10.2 %copy-start.2 = (bf16[1024,100]{0,1:T(8,128)(2,1)S(1)}, bf16[1024,100]{0,1:T(8,128)(2,1)}, u32[]{:S(2)}) copy-start(bf16[1024,100]{0,1:T(8,128)(2,1)} %param.20) | copy-start | bytes 614404
  0.0 10.3 %copy-start = (bf16[256,1024]{1,0:T(8,128)(2,1)S(1)}, bf16[256,1024]{1,0:T(8,128)(2,1)}, u32[]{:S(2)}) copy-start(bf16[256,1024]{1,0:T(8,128)(2,1)} %lat.3) | copy-start | bytes 1572868
  1.7 12.3 %collective-permute-start.1 = (bf16[128,1024]{1,0:T(8,128)(2,1)S(1)}, bf16[128,1024]{1,0:T(8,128)(2,1)S(1)}, u32[]{:S(2)}, u32[]{:S(2)}) collective-permute-start(bf16[128,1024]{1,0:T(8,128)(2,1)S(1)} %get-tuple-element.49), channel_id=1, source_target_pairs={{1,2},{2,1},{3,4},{4,3},{5,6},{6,5},{7,8},{8,7},{9,10},{10,9},{11,... | collective-permute-start | bytes 786440 | tf_op jit(solution)/shard_map/ppermute | solution.py:315
  8.1 5.9 %collective-permute-start = (bf16[128,1024]{1,0:T(8,128)(2,1)S(1)}, bf16[128,1024]{1,0:T(8,128)(2,1)S(1)}, u32[]{:S(2)}, u32[]{:S(2)}) collective-permute-start(bf16[128,1024]{1,0:T(8,128)(2,1)S(1)} %get-tuple-element.50), channel_id=1, source_target_pairs={{0,1},{1,0},{2,3},{3,2},{4,5},{5,4},{6,7},{7,6},{8,9},{9,8},{10,11... | collective-permute-start | bytes 786440 | tf_op jit(solution)/shard_map/ppermute | solution.py:307
  22.1 14.7 %collective-permute-start.3 = (bf16[256,1024]{1,0:T(8,128)(2,1)S(1)}, bf16[256,1024]{1,0:T(8,128)(2,1)S(1)}, u32[]{:S(2)}, u32[]{:S(2)}) collective-permute-start(bf16[256,1024]{1,0:T(8,128)(2,1)S(1)} %get-tuple-element.29.normed), channel_id=1, source_target_pairs={{1,2},{2,1},{3,4},{4,3},{5,6},{6,5},{7,8},{8,7},{9,10},{10,9},{11,... | collective-permute-start | bytes 1572872 | tf_op jit(solution)/shard_map/ppermute | solution.py:315
  28.1 8.7 %collective-permute-start.2 = (bf16[256,1024]{1,0:T(8,128)(2,1)S(1)}, bf16[256,1024]{1,0:T(8,128)(2,1)S(1)}, u32[]{:S(2)}, u32[]{:S(2)}) collective-permute-start(bf16[256,1024]{1,0:T(8,128)(2,1)S(1)} %get-tuple-element.29.normed), channel_id=1, source_target_pairs={{0,1},{1,0},{2,3},{3,2},{4,5},{5,4},{6,7},{7,6},{8,9},{9,8},{10,11... | collective-permute-start | bytes 1572872 | tf_op jit(solution)/shard_map/ppermute | solution.py:307
  42.6 13.6 %collective-permute-start.4 = (bf16[128,1024]{1,0:T(8,128)(2,1)S(1)}, bf16[128,1024]{1,0:T(8,128)(2,1)S(1)}, u32[]{:S(2)}, u32[]{:S(2)}) collective-permute-start(bf16[128,1024]{1,0:T(8,128)(2,1)S(1)} %get-tuple-element.38.outer), channel_id=1, source_target_pairs={{1,2},{2,1},{3,4},{4,3},{5,6},{6,5},{7,8},{8,7},{9,10},{10,9},{11,... | collective-permute-start | bytes 786440 | tf_op jit(solution)/shard_map/ppermute | solution.py:315
  52.2 4.0 %collective-permute-start.5 = (bf16[128,1024]{1,0:T(8,128)(2,1)S(1)}, bf16[128,1024]{1,0:T(8,128)(2,1)S(1)}, u32[]{:S(2)}, u32[]{:S(2)}) collective-permute-start(bf16[128,1024]{1,0:T(8,128)(2,1)S(1)} %window_inner.1.inner), channel_id=1, source_target_pairs={{0,1},{1,0},{2,3},{3,2},{4,5},{5,4},{6,7},{7,6},{8,9},{9,8},{10,11... | collective-permute-start | bytes 786440 | tf_op jit(solution)/shard_map/ppermute | solution.py:307

commit v9 on v8

--- a/solution.py
+++ b/solution.py
@@ -136,9 +136,28 @@
         copy.wait()
 
 
+def attend_pair(both, keys, values, bias):
+    low = low_half((1, 128))
+    zero = jnp.zeros_like(both)
+    rows = both.shape[0]
+    stacked = jnp.concatenate([jnp.where(low, both, zero), jnp.where(low, zero, both)], axis=0)
+    score = dot_t(stacked, keys)
+    if bias is not None:
+        score = (score.reshape(2, rows, -1) + bias[None]).reshape(2 * rows, -1)
+    highest = jnp.max(score, axis=1, keepdims=True)
+    expo = jnp.exp2(score - highest).astype(BF)
+    total = dot(expo, jnp.concatenate([values, jnp.ones_like(values)], axis=1))
+    highest = jnp.broadcast_to(highest, (2 * rows, 128))
+    return (
+        jnp.where(low, total[:rows, :128], total[rows:, :128]),
+        jnp.where(low, total[:rows, 128:], total[rows:, 128:]),
+        jnp.where(low, highest[:rows], highest[rows:]),
+    )
+
+
 def project_kernel(
     normed, win, wout, scale, wq, wk, wv, proc_w, dec_w,
-    q, k, v, aq, bo, co, pw3, dw1, dw2, dw0, dw3, sems,
+    q, num, den, top, aq, bo, co, pw3, dw1, dw2, k, v, dw0, dw3, sems,
 ):
     got = fetch(dec_w, (0, 3), (dw0, dw3), sems.at[pl.ds(0, 2)])
     later = fetch(proc_w, (3,), (pw3,), sems.at[pl.ds(2, 1)])
@@ -147,6 +166,9 @@
     q[...] = (dot(rows, wq[...]) * scale[1:2, :]).astype(BF)
     k[...] = dot(rows, wk[...]).astype(BF)
     v[...] = dot(rows, wv[...]).astype(BF)
+    for pair in range(PAIRS):
+        at = slice(pair * 128, pair * 128 + 128)
+        num[:, at], den[:, at], top[:, at] = attend_pair(q[:, at], k[:, at], v[:, at], None)
     co[...] = dot_t(wout[...], win[...]).astype(BF)
     got[0].wait()
     aq[...] = (dot(win[...], dw0[...]) * scale[2:3, :]).astype(BF)
@@ -156,59 +178,50 @@
         copy.wait()
 
 
-def window_half(side, ends, q, keys, values, latent, wo, bias, mixed, out):
+def window_half(side, ends, q, keys, values, num, den, top, latent, wo, bias, mixed, out):
     half, span = bias.shape
     row = lax.broadcasted_iota(jnp.int32, (half, span), 0)
     col = lax.broadcasted_iota(jnp.int32, (half, span), 1)
     begin = pl.multiple_of(side * half, half)
     place = col + begin
-    inside = (col >= row) & (col - row <= WIN) & (place >= ends[0]) & (place < ends[1])
+    place = jnp.where(place < WIN // 2, place, place + 2 * half)
+    far = place - begin - row
+    inside = (far >= 0) & (far <= WIN) & (place >= ends[0]) & (place < ends[1])
     bias[...] = jnp.where(inside, 0.0, NEG)
     these = pl.ds(begin, half)
     band = pl.ds(begin, span)
-    low = low_half((1, 128))
-    for first in range(0, PAIRS, 2):
-        lanes = [slice(pair * 128, pair * 128 + 128) for pair in (first, first + 1)]
-        score = []
-        for at in lanes:
-            both = q[these, at]
-            zero = jnp.zeros_like(both)
-            stacked = jnp.concatenate(
-                [jnp.where(low, both, zero), jnp.where(low, zero, both)], axis=0
-            )
-            part = dot_t(stacked, keys[band, at])
-            score.append(
-                (part.reshape(2, half, span) + bias[...][None]).reshape(2 * half, span)
-            )
-        expo = [
-            jnp.exp2(part - jnp.max(part, axis=1, keepdims=True)).astype(BF) for part in score
-        ]
-        for at, weights in zip(lanes, expo):
-            near_values = values[band, at]
-            total = dot(
-                weights, jnp.concatenate([near_values, jnp.ones_like(near_values)], axis=1)
-            )
-            part = total[:, :128] * (1.0 / total[:, 128:])
-            mixed[:, at] = jnp.where(low, part[:half], part[half:]).astype(BF)
+    for pair in range(PAIRS):
+        at = slice(pair * 128, pair * 128 + 128)
+        more, weight, highest = attend_pair(
+            q[these, at], keys[band, at], values[band, at], bias[...]
+        )
+        own = top[these, at]
+        joint = jnp.maximum(own, highest)
+        own = jnp.exp2(own - joint)
+        other = jnp.exp2(highest - joint)
+        mixed[:, at] = (
+            (num[these, at] * own + more * other) / (den[these, at] * own + weight * other)
+        ).astype(BF)
     out[...] = (latent[these, :].astype(F32) + dot(mixed[...], wo[...])).astype(BF)
 
 
 def window_outer_kernel(
-    ends, q, k, v, near, far, latent, wk, wv, wo, outer, keys, values, bias, mixed
+    ends, q, num, den, top, near, far, latent, wk, wv, wo, outer, keys, values, bias, mixed
 ):
-    rows = q.shape[0]
-    keys[rows : 2 * rows, :] = k[...]
-    values[rows : 2 * rows, :] = v[...]
     halo = jnp.concatenate(sides(ends[2], near[...], far[...]), axis=0)
-    for weight, wide in ((wk, keys), (wv, values)):
-        both = dot(halo, weight[...]).astype(BF)
-        wide[:rows, :] = both[:rows]
-        wide[2 * rows :, :] = both[rows:]
-    window_half(ends[2], ends, q, keys, values, latent, wo, bias, mixed, outer)
-
-
-def window_inner_kernel(ends, q, keys, values, latent, wo, inner, bias, mixed):
-    window_half(1 - ends[2], ends, q, keys, values, latent, wo, bias, mixed, inner)
+    keys[...] = dot(halo, wk[...]).astype(BF)
+    values[...] = dot(halo, wv[...]).astype(BF)
+    window_half(
+        ends[2], ends, q, keys, values, num, den, top, latent, wo, bias, mixed, outer
+    )
+
+
+def window_inner_kernel(
+    ends, q, num, den, top, keys, values, latent, wo, inner, bias, mixed
+):
+    window_half(
+        1 - ends[2], ends, q, keys, values, num, den, top, latent, wo, bias, mixed, inner
+    )
 
 
 CHUNK = 128
@@ -386,43 +399,44 @@
     )(ends, enc_idx, grid_near, grid, grid_far, qt, bias, av, latent_init, enc_w, proc_w)
     normed_far = swap_far(normed)
     normed_near = swap_near(normed)
-    q, k, v, aq, bo, co, pw3, dw1, dw2 = pl.pallas_call(
+    q, num, den, top, aq, bo, co, pw3, dw1, dw2 = pl.pallas_call(
         project_kernel,
-        out_shape=(shape((rows, width)),) * 3
+        out_shape=(shape((rows, width)),)
+        + (shape((rows, width), F32),) * 3
         + (shape((CPAD, width)), shape((width, CPAD)), shape((CPAD, CPAD)))
         + (square,) * 3,
         in_specs=[VM] * 7 + [HBM] * 2,
-        out_specs=(VM,) * 9,
-        scratch_shapes=[weight] * 2 + [dma((5,))],
+        out_specs=(VM,) * 10,
+        scratch_shapes=[pltpu.VMEM((rows, width), BF)] * 2 + [weight] * 2 + [dma((5,))],
         compiler_params=params(36),
         cost_estimate=pl.CostEstimate(flops=3 * 10**9, bytes_accessed=12 * 2**20, transcendentals=0),
         name="project",
     )(normed, win, wout, scale, pw0, pw1, pw2, proc_w, dec_w)
     half_scratch = [
-        pltpu.VMEM((rows // 2, rows // 2 + WIN), F32),
+        pltpu.VMEM((rows // 2, WIN - rows // 2), F32),
         pltpu.VMEM((rows // 2, width), BF),
     ]
-    wide = shape((rows + WIN, width))
+    wide = shape((WIN, width))
     mesh_outer, keys, values = pl.pallas_call(
         window_outer_kernel,
         out_shape=(shape((BL, width)), wide, wide),
-        in_specs=[SM] + [VM] * 9,
+        in_specs=[SM] + [VM] * 10,
         out_specs=(VM,) * 3,
         scratch_shapes=half_scratch,
         compiler_params=params(24),
         name="window_outer",
-    )(ends, q, k, v, normed_near, normed_far, latent, pw1, pw2, pw3)
+    )(ends, q, num, den, top, normed_near, normed_far, latent, pw1, pw2, pw3)
     mesh_far = swap_far(mesh_outer)
     mesh_inner = pl.pallas_call(
         window_inner_kernel,
         out_shape=shape((BL, width)),
-        in_specs=[SM] + [VM] * 5,
+        in_specs=[SM] + [VM] * 8,
         out_specs=VM,
         scratch_shapes=half_scratch,
         compiler_params=params(24),
         cost_estimate=pl.CostEstimate(flops=3 * 10**9, bytes_accessed=12 * 2**20, transcendentals=0),
         name="window_inner",
-    )(ends, q, keys, values, latent, pw3)
+    )(ends, q, num, den, top, keys, values, latent, pw3)
     mesh_near = swap_near(mesh_inner)
     mesh_far = pl.pallas_call(
         pass_kernel,

time: 74.4 us -> 73.9 us (level)
  starting transfers between devices: 19 us -> 21 us
  waiting for transfers between devices: 2.73 us -> 1.3 us
    ppermute x3, starting transfers between devices: 18.4 us -> 20.5 us  [swap_far(): return lax.ppermute(outer, axes, pairs)]
    ppermute x3, waiting for transfers between devices: 2.72 us -> 1.29 us  [swap_far(): return lax.ppermute(outer, axes, pairs)]
    pallas_call x1, Pallas kernels: 5.71 us -> 6.57 us  [on_device(): pl.pallas_call(project_kernel, out_shape=(shape((rows, width)),) + (shape...]
    mul x1, other arithmetic: 0.02 us -> 0.78 us  [on_device(): jnp.clip(dec_src.T - (place * rows - BL), 0, rows + 2 * BL - 1).reshape(-1)]
  transfers between devices with their start and end apart: 6 -> 6, of which waited for: 1 -> 1; matrix products, arithmetic and copies ran while one was open for 3% -> 2% of each run, Pallas kernels for 23% -> 23%
where the time goes in v9:
time: 73.9 us; the launch traced here: 73 us
  Pallas kernels  47.3 us (64%)
  starting transfers between devices  21 us (28%)
  other arithmetic  2.34 us (3%)
  waiting for transfers between devices  1.3 us (2%)
    ppermute x3, starting transfers between devices, swap_far(): return lax.ppermute(outer, axes, pairs)  20.5 us
    pallas_call x1, Pallas kernels, on_device(): pl.pallas_call(decode_kernel, out_shape=shape((channels, points)), in_spe...  17.3 us
    pallas_call x1, Pallas kernels, on_device(): pl.pallas_call(encode_kernel, out_shape=(shape((rows, width)),) * 2 + (sq...  8.09 us
    pallas_call x1, Pallas kernels, on_device(): pl.pallas_call(project_kernel, out_shape=(shape((rows, width)),) + (shape...  6.57 us
    pallas_call x1, Pallas kernels, on_device(): pl.pallas_call(window_outer_kernel, out_shape=(shape((BL, width)), wide,...  5.09 us
    pallas_call x1, Pallas kernels, on_device(): pl.pallas_call(fold_kernel, out_shape=(shape((HEADS, rows, CPAD)), shape(...  3.69 us
    pallas_call x1, Pallas kernels, on_device(): pl.pallas_call(prepare_kernel, out_shape=(shape((points * 8, 128), F32),...  3.66 us
    pallas_call x1, Pallas kernels, on_device(): pl.pallas_call(window_inner_kernel, out_shape=shape((BL, width)), in_spec...  2.88 us
  transfers between devices with their start and end apart: 6, of which 1 were waited for; matrix products, arithmetic and copies ran while one was open for 2% of the time, Pallas kernels for 23%

profile of v9, /device:TPU:96, one launch (start us, length us, event | category | flops | bytes accessed | tf_op | source)
XLA Modules:
  0.0 73.0 jit_solution(1360639209887535288)
XLA Ops:
  0.0 0.0 copy-start.1
  0.0 0.0 copy-start.2
  0.0 0.0 copy-start.5
  0.0 0.0 copy-start.4
  0.0 0.0 copy-start.3
  0.0 0.0 copy-start
  0.1 0.1 pad.11.clone
  0.1 0.1 pad.10.clone
  0.2 1.5 %maximum_maximum_fusion.own.state.grid = bf16[128,2048]{1,0:T(8,128)(2,1)S(1)} fusion(bf16[100,2048]{1,0:T(8,128)(2,1)} %bitcast.15, bf16[128]{0:T(256)(128)(2,1)S(1)} %pad.11.clone, bf16[128]{0:T(256)(128)(2,1)S(1)} %pad.10.clone), kind=kLoop, calls=%fused_computation | loop fusion | flops 1572864 | bytes 934400 | tf_op jit(solution)/shard_map/concatenate | solution.py:352
  1.7 0.1 collective-permute-start
  1.8 7.0 %collective-permute-start.1 = (bf16[128,1024]{1,0:T(8,128)(2,1)S(1)}, bf16[128,1024]{1,0:T(8,128)(2,1)S(1)}, u32[]{:S(2)}, u32[]{:S(2)}) collective-permute-start(bf16[128,1024]{1,0:T(8,128)(2,1)S(1)} %get-tuple-element.51), channel_id=1, source_target_pairs={{1,2},{2,1},{3,4},{4,3},{5,6},{6,5},{7,8},{8,7},{9,10},{10,9},{11,... | collective-permute-start | bytes 786440 | tf_op jit(solution)/shard_map/ppermute | solution.py:328
  8.9 0.8 %multiply_bitcast_fusion = s32[3,2048]{1,0:T(4,128)S(1)} fusion(s32[2048,3]{0,1:T(4,128)} %param.15, s32[]{:T(128)S(6)} %sub.21), kind=kLoop, calls=%fused_computation.1 | loop fusion | flops 18432 | bytes 49156 | tf_op jit(solution)/shard_map/mul | solution.py:370
  9.7 0.0 copy-done.1
  9.7 0.0 copy-done.2
  9.8 0.0 copy-done.5
  9.8 0.1 lt.35
  9.9 0.1 lt.37
  10.0 0.1 lt.33
  10.1 0.0 copy-done.4
  10.1 0.1 broadcast_in_dim.21
  10.2 0.1 reshape.23.scale
  10.3 0.0 copy-done.3
  10.3 0.1 pad_add_fusion.others_4_.ends
  10.4 0.0 copy-done
  10.4 3.7 %fold.1 = (bf16[16,256,128]{2,1,0:T(8,128)(2,1)S(1)}, bf16[128,1024]{1,0:T(8,128)(2,1)S(1)}) custom-call(bf16[128,1024]{1,0:T(8,128)(2,1)S(1)} %pad.7.win, bf16[4,1024,1024]{2,1,0:T(8,128)(2,1)} %enc_w.3, bf16[256,1024]{1,0:T(8,128)(2,1)S(1)} %copy-done, f32[3,1024]{1,0:T(4,128)S(1)} %reshape.23.scale, bf16[128,1024]{1,0:T(8,128)(2,1)S(1)} %pad.8.others_0_.wout, ...), custom_call_target="tpu_custom_call" | custom-call | flops 2000000000 | bytes 8388608 | tf_op jit(solution)/shard_map/fold/pallas_call | solution.py:373
  14.1 0.0 collective-permute-done.near
  14.1 0.0 collective-permute-done.1.far
  14.1 8.1 %encode.1 = (bf16[256,1024]{1,0:T(8,128)(2,1)S(1)}, bf16[256,1024]{1,0:T(8,128)(2,1)S(1)}, bf16[1024,1024]{1,0:T(8,128)(2,1)S(1)}, bf16[1024,1024]{1,0:T(8,128)(2,1)S(1)}, bf16[1024,1024]{1,0:T(8,128)(2,1)S(1)}) custom-call(s32[3]{0:T(128)S(1)} %pad_add_fusion.others_4_.ends, s32[4096]{0:T(1024)S(1)} %bitcast.14, ...), custom_call_target="tpu_custom_call" | custom-call | tf_op jit(solution)/shard_map/encode/pallas_call | solution.py:384
  22.2 0.1 collective-permute-start.2
  22.3 6.8 %collective-permute-start.3 = (bf16[256,1024]{1,0:T(8,128)(2,1)S(1)}, bf16[256,1024]{1,0:T(8,128)(2,1)S(1)}, u32[]{:S(2)}, u32[]{:S(2)}) collective-permute-start(bf16[256,1024]{1,0:T(8,128)(2,1)S(1)} %get-tuple-element.30.normed), channel_id=1, source_target_pairs={{1,2},{2,1},{3,4},{4,3},{5,6},{6,5},{7,8},{8,7},{9,10},{10,9},{11,... | collective-permute-start | bytes 1572872 | tf_op jit(solution)/shard_map/ppermute | solution.py:328
  29.1 6.6 %project.1 = (bf16[256,1024]{1,0:T(8,128)(2,1)S(1)}, f32[256,1024]{1,0:T(8,128)S(1)}, f32[256,1024]{1,0:T(8,128)S(1)}, f32[256,1024]{1,0:T(8,128)S(1)}, bf16[128...) custom-call(bf16[256,1024]{1,0:T(8,128)(2,1)S(1)} %get-tuple-element, ...), custom_call_target="tpu_custom_call" | custom-call | flops 3000000000 | bytes 12582912 | tf_op jit(solution)/shard_map/project/pallas_call | solution.py:402
  35.7 0.0 collective-permute-done.2.near
  35.7 1.3 %collective-permute-done.3.far = bf16[256,1024]{1,0:T(8,128)(2,1)S(1)} collective-permute-done((bf16[256,1024]{1,0:T(8,128)(2,1)S(1)}, bf16[256,1024]{1,0:T(8,128)(2,1)S(1)}, u32[]{:S(2)}, u32[]{:S(2)}) %collective-permute-start.3) | collective-permute-done | bytes 524320 | tf_op jit(solution)/shard_map/ppermute | solution.py:328
  37.0 5.1 %window_outer.1 = (bf16[128,1024]{1,0:T(8,128)(2,1)S(1)}, bf16[512,1024]{1,0:T(8,128)(2,1)S(1)}, bf16[512,1024]{1,0:T(8,128)(2,1)S(1)}) custom-call(s32[3]{0:T(128)S(1)} %pad_add_fusion.others_4_.ends, bf16[256,1024]{1,0:T(8,128)(2,1)S(1)} %get-tuple-element.34.q, f32[256,1024]{1,0:T(8,128)S(1)} %get-tuple-element.35.num, ...), custom_call_target="tpu_custom_call" | custom-call | tf_op jit(solution)/shard_map/window_outer/pallas_call | solution.py:420
  42.1 6.7 %collective-permute-start.4 = (bf16[128,1024]{1,0:T(8,128)(2,1)S(1)}, bf16[128,1024]{1,0:T(8,128)(2,1)S(1)}, u32[]{:S(2)}, u32[]{:S(2)}) collective-permute-start(bf16[128,1024]{1,0:T(8,128)(2,1)S(1)} %get-tuple-element.40.outer), channel_id=1, source_target_pairs={{1,2},{2,1},{3,4},{4,3},{5,6},{6,5},{7,8},{8,7},{9,10},{10,9},{11,... | collective-permute-start | bytes 786440 | tf_op jit(solution)/shard_map/ppermute | solution.py:328
  48.8 2.9 %window_inner.1.inner = bf16[128,1024]{1,0:T(8,128)(2,1)S(1)} custom-call(s32[3]{0:T(128)S(1)} %pad_add_fusion.others_4_.ends, bf16[256,1024]{1,0:T(8,128)(2,1)S(1)} %get-tuple-element.34.q, f32[256,1024]{1,0:T(8,128)S(1)} %get-tuple-element.35.num, f32[256,1024]{1,0:T(8,128)S(1)} %get-tuple-element.36.den, f32[256,1024]{1,0:T(8,128)S(1)} %get-tuple-element.37.top, ...), custom_call_target="tpu_custom_call" | custom-call | flops 3000000000 | bytes 12582912 | tf_op jit(solution)/shard_map/window_inner/pallas_call | solution.py:430
  51.7 0.3 collective-permute-start.5
  52.0 3.7 %prepare.1 = (f32[16384,128]{1,0:T(8,128)S(1)}, f32[2048,128]{1,0:T(8,128)S(1)}, f32[2048,128]{1,0:T(8,128)S(1)}) custom-call(s32[3]{0:T(128)S(1)} %pad_add_fusion.others_4_.ends, bf16[128,1024]{1,0:T(8,128)(2,1)S(1)} %window_inner.1.inner, bf16[128,1024]{1,0:T(8,128)(2,1)S(1)} %get-tuple-element.40.outer, ...), custom_call_target="tpu_custom_call" | custom-call | flops 1000000 | bytes 65536 | tf_op jit(solution)/shard_map/prepare/pallas_call | solution.py:451
  55.6 0.0 collective-permute-done.4.given
  55.7 0.0 collective-permute-done.5.near
  55.7 17.3 %decode.1 = bf16[100,2048]{1,0:T(8,128)(2,1)} custom-call(s32[3]{0:T(128)S(1)} %pad_add_fusion.others_4_.ends, s32[6144]{0:T(1024)S(1)} %mul.35.others_3_.idx, bf16[128,1024]{1,0:T(8,128)(2,1)S(1)} %pass.1.far, bf16[128,1024]{1,0:T(8,128)(2,1)S(1)} %collective-permute-done.5.near, f32[2048,128]{1,0:T(8,128)S(1)} %get-tuple-element.46.ko, ...), custom_call_target="tpu_custom_call" | custom-call | tf_op jit(solution)/shard_map/decode/pallas_call | solution.py:464
  (12 shorter events, 0.2 us)
Async XLA Ops:
  0.0 9.7 %copy-start.1 = (bf16[100,1024]{1,0:T(8,128)(2,1)S(1)}, bf16[100,1024]{1,0:T(8,128)(2,1)}, u32[]{:S(2)}) copy-start(bf16[100,1024]{1,0:T(8,128)(2,1)} %param.16) | copy-start | bytes 614404
  0.0 9.7 %copy-start.2 = (bf16[1024,100]{0,1:T(8,128)(2,1)S(1)}, bf16[1024,100]{0,1:T(8,128)(2,1)}, u32[]{:S(2)}) copy-start(bf16[1024,100]{0,1:T(8,128)(2,1)} %param.20) | copy-start | bytes 614404
  0.0 9.8 %copy-start.5 = (s32[256]{0:T(256)S(1)}, s32[256]{0:T(256)}, u32[]{:S(2)}) copy-start(s32[256]{0:T(256)} %param.14) | copy-start | bytes 3076
  0.0 10.1 %copy-start.4 = (f32[3,16]{1,0:T(4,128)S(1)}, f32[3,16]{1,0:T(4,128)}, u32[]{:S(2)}) copy-start(f32[3,16]{1,0:T(4,128)} %param.21) | copy-start | bytes 580
  0.0 10.2 %copy-start.3 = (s32[256,16]{0,1:T(8,128)S(1)}, s32[256,16]{0,1:T(8,128)}, u32[]{:S(2)}) copy-start(s32[256,16]{0,1:T(8,128)} %param.13) | copy-start | bytes 49156
  0.0 10.4 %copy-start = (bf16[256,1024]{1,0:T(8,128)(2,1)S(1)}, bf16[256,1024]{1,0:T(8,128)(2,1)}, u32[]{:S(2)}) copy-start(bf16[256,1024]{1,0:T(8,128)(2,1)} %lat.3) | copy-start | bytes 1572868
  1.7 12.3 %collective-permute-start = (bf16[128,1024]{1,0:T(8,128)(2,1)S(1)}, bf16[128,1024]{1,0:T(8,128)(2,1)S(1)}, u32[]{:S(2)}, u32[]{:S(2)}) collective-permute-start(bf16[128,1024]{1,0:T(8,128)(2,1)S(1)} %get-tuple-element.52), channel_id=1, source_target_pairs={{0,1},{1,0},{2,3},{3,2},{4,5},{5,4},{6,7},{7,6},{8,9},{9,8},{10,11... | collective-permute-start | bytes 786440 | tf_op jit(solution)/shard_map/ppermute | solution.py:320
  1.8 12.3 %collective-permute-start.1 = (bf16[128,1024]{1,0:T(8,128)(2,1)S(1)}, bf16[128,1024]{1,0:T(8,128)(2,1)S(1)}, u32[]{:S(2)}, u32[]{:S(2)}) collective-permute-start(bf16[128,1024]{1,0:T(8,128)(2,1)S(1)} %get-tuple-element.51), channel_id=1, source_target_pairs={{1,2},{2,1},{3,4},{4,3},{5,6},{6,5},{7,8},{8,7},{9,10},{10,9},{11,... | collective-permute-start | bytes 786440 | tf_op jit(solution)/shard_map/ppermute | solution.py:328
  22.2 13.5 %collective-permute-start.2 = (bf16[256,1024]{1,0:T(8,128)(2,1)S(1)}, bf16[256,1024]{1,0:T(8,128)(2,1)S(1)}, u32[]{:S(2)}, u32[]{:S(2)}) collective-permute-start(bf16[256,1024]{1,0:T(8,128)(2,1)S(1)} %get-tuple-element.30.normed), channel_id=1, source_target_pairs={{0,1},{1,0},{2,3},{3,2},{4,5},{5,4},{6,7},{7,6},{8,9},{9,8},{10,11... | collective-permute-start | bytes 1572872 | tf_op jit(solution)/shard_map/ppermute | solution.py:320
  22.3 14.7 %collective-permute-start.3 = (bf16[256,1024]{1,0:T(8,128)(2,1)S(1)}, bf16[256,1024]{1,0:T(8,128)(2,1)S(1)}, u32[]{:S(2)}, u32[]{:S(2)}) collective-permute-start(bf16[256,1024]{1,0:T(8,128)(2,1)S(1)} %get-tuple-element.30.normed), channel_id=1, source_target_pairs={{1,2},{2,1},{3,4},{4,3},{5,6},{6,5},{7,8},{8,7},{9,10},{10,9},{11,... | collective-permute-start | bytes 1572872 | tf_op jit(solution)/shard_map/ppermute | solution.py:328
  42.1 13.5 %collective-permute-start.4 = (bf16[128,1024]{1,0:T(8,128)(2,1)S(1)}, bf16[128,1024]{1,0:T(8,128)(2,1)S(1)}, u32[]{:S(2)}, u32[]{:S(2)}) collective-permute-start(bf16[128,1024]{1,0:T(8,128)(2,1)S(1)} %get-tuple-element.40.outer), channel_id=1, source_target_pairs={{1,2},{2,1},{3,4},{4,3},{5,6},{6,5},{7,8},{8,7},{9,10},{10,9},{11,... | collective-permute-start | bytes 786440 | tf_op jit(solution)/shard_map/ppermute | solution.py:328
  51.7 4.0 %collective-permute-start.5 = (bf16[128,1024]{1,0:T(8,128)(2,1)S(1)}, bf16[128,1024]{1,0:T(8,128)(2,1)S(1)}, u32[]{:S(2)}, u32[]{:S(2)}) collective-permute-start(bf16[128,1024]{1,0:T(8,128)(2,1)S(1)} %window_inner.1.inner), channel_id=1, source_target_pairs={{0,1},{1,0},{2,3},{3,2},{4,5},{5,4},{6,7},{7,6},{8,9},{9,8},{10,11... | collective-permute-start | bytes 786440 | tf_op jit(solution)/shard_map/ppermute | solution.py:320

commit v10 on v9

--- a/solution.py
+++ b/solution.py
@@ -76,18 +76,21 @@
 def encode_kernel(
     ends, idx, near, own, far, qt, bias, av, lat, enc_w, proc_w,
     latent, normed, pw0, pw1, pw2,
-    grid, ge0, ge1, z, w3, sems,
+    grid, wide, ge0, ge1, z, w3, sems,
 ):
     got = fetch(enc_w, (3,), (w3,), sems.at[pl.ds(0, 1)])
     later = fetch(proc_w, (0, 1, 2), (pw0, pw1, pw2), sems.at[pl.ds(1, 3)])
     rows = lat.shape[0]
     groups = rows // 16
-    at = 0
-    left, right = sides(ends[2], near[...], far[...])
-    for piece in (left, own[...], right):
-        for begin in range(0, piece.shape[1], 512):
-            grid[at : at + 512, :] = piece[:, begin : begin + 512].astype(F32).T
-            at += 512
+    reach = near.shape[1]
+    wide[...] = jnp.zeros_like(wide)
+    for begin in (0, own.shape[1] + reach):
+        given = sides(ends[2], near[...], far[...])[begin > 0]
+        wide[0 : given.shape[0], :] = given.astype(F32)
+        for part in range(0, reach, 512):
+            grid[begin + part : begin + part + 512, :] = wide[:, part : part + 512].T
+    for part in range(0, own.shape[1], 512):
+        grid[reach + part : reach + part + 512, :] = own[:, part : part + 512].astype(F32).T
     row = lax.broadcasted_iota(jnp.int32, (256, 256), 0)
     col = lax.broadcasted_iota(jnp.int32, (256, 256), 1)
     diag = jnp.where(row % 16 == col % 16, 0.0, NEG)
@@ -349,17 +352,13 @@
     weight = pltpu.VMEM((width, width), BF)
     dma = pltpu.SemaphoreType.DMA
 
-    grid = jnp.concatenate(
-        [
-            grid_state.T,
-            jnp.ones((1, points), BF),
-            jnp.zeros((CPAD - channels - 1, points), BF),
-        ],
-        axis=0,
+    grid = jnp.pad(grid_state.T, ((0, CPAD - channels), (0, 0)))
+    core = lax.axis_index("narrow")
+    channel_rows = grid_state.T
+    grid_far = swap_far(lax.dynamic_slice_in_dim(channel_rows, core * (points - BG), BG, 1))
+    grid_near = swap_near(
+        lax.dynamic_slice_in_dim(channel_rows, (1 - core) * (points - BG), BG, 1)
     )
-    core = lax.axis_index("narrow")
-    grid_far = swap_far(lax.dynamic_slice_in_dim(grid, core * (points - BG), BG, 1))
-    grid_near = swap_near(lax.dynamic_slice_in_dim(grid, (1 - core) * (points - BG), BG, 1))
     win = jnp.pad(w_in, ((0, CPAD - channels), (0, 0)))
     wout = jnp.pad(w_out.T, ((0, CPAD - channels), (0, 0)))
     scale = jnp.repeat(logit_scale * (LOG2E / math.sqrt(SIZE)), SIZE, axis=1)
@@ -388,6 +387,7 @@
         out_specs=(VM,) * 5,
         scratch_shapes=[
             pltpu.VMEM((points + 2 * BG, CPAD), F32),
+            pltpu.VMEM((CPAD, BG), F32),
             pltpu.VMEM((slots * 16, CPAD), F32),
             pltpu.VMEM((slots * 16, CPAD), F32),
             pltpu.VMEM((HEADS, rows, CPAD), BF),

time: 73.9 us -> 75.1 us (1.016)
  starting transfers between devices: 21 us -> 13.4 us
  waiting for transfers between devices: 1.3 us -> 7.29 us
  local copies, waits for them, and re-layouts: 0.73 us -> 4.24 us
    ppermute x3, starting transfers between devices: 20.5 us -> 12.9 us  [swap_far(): return lax.ppermute(outer, axes, pairs)]
    ppermute x3, waiting for transfers between devices: 1.29 us -> 7.29 us  [swap_far(): return lax.ppermute(outer, axes, pairs)]
    concatenate x1 -> x0, other arithmetic: 1.47 us -> none  [on_device(): jnp.concatenate([grid_state.T, jnp.ones((1, points), BF), jnp.zeros((CPAD...]
    dynamic_slice x1, local copies, waits for them, and re-layouts: 0.05 us -> 1.15 us  [on_device(): lax.dynamic_slice_in_dim(channel_rows, core * (points - BG), BG, 1)]
    pad x1, local copies, waits for them, and re-layouts: 0.02 us -> 0.95 us  [on_device(): win = jnp.pad(w_in, ((0, CPAD - channels), (0, 0)))]
    pad x1, local copies, waits for them, and re-layouts: 0.02 us -> 0.95 us  [on_device(): wout = jnp.pad(w_out.T, ((0, CPAD - channels), (0, 0)))]
  transfers between devices with their start and end apart: 6 -> 6, of which waited for: 1 -> 2; matrix products, arithmetic and copies ran while one was open for 2% -> 7% of each run, Pallas kernels for 23% -> 23%
where the time goes in v10:
time: 75.1 us; the launch traced here: 74.7 us
  Pallas kernels  47.3 us (63%)
  starting transfers between devices  13.4 us (18%)
  waiting for transfers between devices  7.29 us (10%)
  local copies, waits for them, and re-layouts  4.24 us (6%)
  other arithmetic  2.27 us (3%)
    pallas_call x1, Pallas kernels, on_device(): pl.pallas_call(decode_kernel, out_shape=shape((channels, points)), in_spe...  17.3 us
    ppermute x3, starting transfers between devices, swap_far(): return lax.ppermute(outer, axes, pairs)  12.9 us
    pallas_call x1, Pallas kernels, on_device(): pl.pallas_call(encode_kernel, out_shape=(shape((rows, width)),) * 2 + (sq...  8.07 us
    ppermute x3, waiting for transfers between devices, swap_far(): return lax.ppermute(outer, axes, pairs)  7.29 us
    pallas_call x1, Pallas kernels, on_device(): pl.pallas_call(project_kernel, out_shape=(shape((rows, width)),) + (shape...  6.58 us
    pallas_call x1, Pallas kernels, on_device(): pl.pallas_call(window_outer_kernel, out_shape=(shape((BL, width)), wide,...  5.09 us
    pallas_call x1, Pallas kernels, on_device(): pl.pallas_call(fold_kernel, out_shape=(shape((HEADS, rows, CPAD)), shape(...  3.7 us
    pallas_call x1, Pallas kernels, on_device(): pl.pallas_call(prepare_kernel, out_shape=(shape((points * 8, 128), F32),...  3.67 us
  transfers between devices with their start and end apart: 6, of which 2 were waited for; matrix products, arithmetic and copies ran while one was open for 7% of the time, Pallas kernels for 23%

profile of v10, /device:TPU:96, one launch (start us, length us, event | category | flops | bytes accessed | tf_op | source)
XLA Modules:
  0.0 74.7 jit_solution(6861845348097237765)
XLA Ops:
  0.0 0.0 copy-start.1
  0.0 0.0 copy-start
  0.0 1.1 %dynamic-slice_bitcast_fusion = (bf16[100,1024]{1,0:T(8,128)(2,1)S(1)}, bf16[100,1024]{1,0:T(8,128)(2,1)S(1)}) fusion(bf16[2048,100]{0,1:T(8,128)(2,1)} %param.11, s32[]{:T(128)S(6)} %select_n.14, s32[]{:T(128)S(6)} %select_n.13), kind=kLoop, calls=%fused_computation | loop fusion | bytes 819208 | tf_op jit(solution)/shard_map/dynamic_slice | solution.py:358
  1.2 0.1 collective-permute-start
  1.2 7.0 %collective-permute-start.1 = (bf16[100,1024]{1,0:T(8,128)(2,1)S(1)}, bf16[100,1024]{1,0:T(8,128)(2,1)S(1)}, u32[]{:S(2)}, u32[]{:S(2)}) collective-permute-start(bf16[100,1024]{1,0:T(8,128)(2,1)S(1)} %get-tuple-element.51), channel_id=1, source_target_pairs={{1,2},{2,1},{3,4},{4,3},{5,6},{6,5},{7,8},{8,7},{9,10},{10,9},{11,... | collective-permute-start | bytes 614408 | tf_op jit(solution)/shard_map/ppermute | solution.py:331
  8.3 0.8 %lt.35 = s32[16,16]{1,0:T(8,128)S(1)} reshape(s32[256]{0:T(256)} %param.14) | data formatting | bytes 2048 | tf_op jit(solution)/shard_map/lt | solution.py:366
  9.1 0.1 lt.37
  9.2 0.1 lt.33
  9.3 0.7 broadcast_multiply_fusion
  10.0 0.7 clamp_bitcast_fusion
  10.7 0.8 %multiply_bitcast_fusion = s32[3,2048]{1,0:T(4,128)S(1)} fusion(s32[2048,3]{0,1:T(4,128)} %param.15, s32[]{:T(128)S(6)} %sub.21), kind=kLoop, calls=%fused_computation.2 | loop fusion | flops 18432 | bytes 49156 | tf_op jit(solution)/shard_map/mul | solution.py:369
  11.5 0.1 pad_add_fusion.others_4_.ends
  11.6 1.0 %pad.12.win = bf16[128,1024]{1,0:T(8,128)(2,1)S(1)} pad(bf16[100,1024]{1,0:T(8,128)(2,1)} %param.16, bf16[]{:T(256)} %constant.35.clone.1), padding=0_28x0_0 | pad | bytes 466946 | tf_op jit(solution)/shard_map/jit(_pad)/pad | solution.py:362
  12.5 1.0 %pad.13.others_0_.wout = bf16[128,1024]{1,0:T(8,128)(2,1)S(1)} pad(bf16[100,1024]{1,0:T(8,128)(2,1)} %bitcast.19, bf16[]{:T(256)} %constant.35.clone.1), padding=0_28x0_0 | pad | bytes 466946 | tf_op jit(solution)/shard_map/jit(_pad)/pad | solution.py:363
  13.5 0.1 broadcast_in_dim.13
  13.6 0.1 reshape.23.scale
  13.7 0.0 copy-done.1
  13.7 0.0 copy-done
  13.7 3.7 %fold.1 = (bf16[16,256,128]{2,1,0:T(8,128)(2,1)S(1)}, bf16[128,1024]{1,0:T(8,128)(2,1)S(1)}) custom-call(bf16[128,1024]{1,0:T(8,128)(2,1)S(1)} %pad.12.win, bf16[4,1024,1024]{2,1,0:T(8,128)(2,1)} %enc_w.3, bf16[256,1024]{1,0:T(8,128)(2,1)S(1)} %copy-done, f32[3,1024]{1,0:T(4,128)S(1)} %reshape.23.scale, bf16[128,1024]{1,0:T(8,128)(2,1)S(1)} %pad.13.others_0_.wout, ...), custom_call_target="tpu_custom_call" | custom-call | flops 2000000000 | bytes 8388608 | tf_op jit(solution)/shard_map/fold/pallas_call | solution.py:372
  17.5 0.0 collective-permute-done.near
  17.5 0.0 collective-permute-done.1.far
  17.5 8.1 %encode.1 = (bf16[256,1024]{1,0:T(8,128)(2,1)S(1)}, bf16[256,1024]{1,0:T(8,128)(2,1)S(1)}, bf16[1024,1024]{1,0:T(8,128)(2,1)S(1)}, bf16[1024,1024]{1,0:T(8,128)(2,1)S(1)}, bf16[1024,1024]{1,0:T(8,128)(2,1)S(1)}) custom-call(s32[3]{0:T(128)S(1)} %pad_add_fusion.others_4_.ends, s32[4096]{0:T(1024)S(1)} %bitcast.17, ...), custom_call_target="tpu_custom_call" | custom-call | tf_op jit(solution)/shard_map/encode/pallas_call | solution.py:383
  25.6 0.1 collective-permute-start.2
  25.7 3.0 %collective-permute-start.3 = (bf16[256,1024]{1,0:T(8,128)(2,1)S(1)}, bf16[256,1024]{1,0:T(8,128)(2,1)S(1)}, u32[]{:S(2)}, u32[]{:S(2)}) collective-permute-start(bf16[256,1024]{1,0:T(8,128)(2,1)S(1)} %get-tuple-element.30.normed), channel_id=1, source_target_pairs={{1,2},{2,1},{3,4},{4,3},{5,6},{6,5},{7,8},{8,7},{9,10},{10,9},{11,... | collective-permute-start | bytes 1572872 | tf_op jit(solution)/shard_map/ppermute | solution.py:331
  28.7 6.6 %project.1 = (bf16[256,1024]{1,0:T(8,128)(2,1)S(1)}, f32[256,1024]{1,0:T(8,128)S(1)}, f32[256,1024]{1,0:T(8,128)S(1)}, f32[256,1024]{1,0:T(8,128)S(1)}, bf16[128...) custom-call(bf16[256,1024]{1,0:T(8,128)(2,1)S(1)} %get-tuple-element, ...), custom_call_target="tpu_custom_call" | custom-call | flops 3000000000 | bytes 12582912 | tf_op jit(solution)/shard_map/project/pallas_call | solution.py:402
  35.3 0.0 collective-permute-done.2.near
  35.3 5.1 %collective-permute-done.3.far = bf16[256,1024]{1,0:T(8,128)(2,1)S(1)} collective-permute-done((bf16[256,1024]{1,0:T(8,128)(2,1)S(1)}, bf16[256,1024]{1,0:T(8,128)(2,1)S(1)}, u32[]{:S(2)}, u32[]{:S(2)}) %collective-permute-start.3) | collective-permute-done | bytes 524320 | tf_op jit(solution)/shard_map/ppermute | solution.py:331
  40.4 5.1 %window_outer.1 = (bf16[128,1024]{1,0:T(8,128)(2,1)S(1)}, bf16[512,1024]{1,0:T(8,128)(2,1)S(1)}, bf16[512,1024]{1,0:T(8,128)(2,1)S(1)}) custom-call(s32[3]{0:T(128)S(1)} %pad_add_fusion.others_4_.ends, bf16[256,1024]{1,0:T(8,128)(2,1)S(1)} %get-tuple-element.34.q, f32[256,1024]{1,0:T(8,128)S(1)} %get-tuple-element.35.num, ...), custom_call_target="tpu_custom_call" | custom-call | tf_op jit(solution)/shard_map/window_outer/pallas_call | solution.py:420
  45.5 2.8 %collective-permute-start.4 = (bf16[128,1024]{1,0:T(8,128)(2,1)S(1)}, bf16[128,1024]{1,0:T(8,128)(2,1)S(1)}, u32[]{:S(2)}, u32[]{:S(2)}) collective-permute-start(bf16[128,1024]{1,0:T(8,128)(2,1)S(1)} %get-tuple-element.40.outer), channel_id=1, source_target_pairs={{1,2},{2,1},{3,4},{4,3},{5,6},{6,5},{7,8},{8,7},{9,10},{10,9},{11,... | collective-permute-start | bytes 786440 | tf_op jit(solution)/shard_map/ppermute | solution.py:331
  48.3 2.9 %window_inner.1.inner = bf16[128,1024]{1,0:T(8,128)(2,1)S(1)} custom-call(s32[3]{0:T(128)S(1)} %pad_add_fusion.others_4_.ends, bf16[256,1024]{1,0:T(8,128)(2,1)S(1)} %get-tuple-element.34.q, f32[256,1024]{1,0:T(8,128)S(1)} %get-tuple-element.35.num, f32[256,1024]{1,0:T(8,128)S(1)} %get-tuple-element.36.den, f32[256,1024]{1,0:T(8,128)S(1)} %get-tuple-element.37.top, ...), custom_call_target="tpu_custom_call" | custom-call | flops 3000000000 | bytes 12582912 | tf_op jit(solution)/shard_map/window_inner/pallas_call | solution.py:430
  51.2 0.3 collective-permute-start.5
  51.5 3.7 %prepare.1 = (f32[16384,128]{1,0:T(8,128)S(1)}, f32[2048,128]{1,0:T(8,128)S(1)}, f32[2048,128]{1,0:T(8,128)S(1)}) custom-call(s32[3]{0:T(128)S(1)} %pad_add_fusion.others_4_.ends, bf16[128,1024]{1,0:T(8,128)(2,1)S(1)} %window_inner.1.inner, bf16[128,1024]{1,0:T(8,128)(2,1)S(1)} %get-tuple-element.40.outer, bf16[128,2048]{1,0:T(8,128)(2,1)S(1)} %pad.11.own.state.grid, ...), custom_call_target="tpu_custom_call" | custom-call | flops 1000000 | bytes 65536 | tf_op jit(solution)/shard_map/prepare/pallas_call | solution.py:451
  55.2 2.2 %collective-permute-done.4.given = bf16[128,1024]{1,0:T(8,128)(2,1)S(1)} collective-permute-done((bf16[128,1024]{1,0:T(8,128)(2,1)S(1)}, bf16[128,1024]{1,0:T(8,128)(2,1)S(1)}, u32[]{:S(2)}, u32[]{:S(2)}) %collective-permute-start.4) | collective-permute-done | bytes 262176 | tf_op jit(solution)/shard_map/ppermute | solution.py:331
  57.4 0.0 collective-permute-done.5.near
  57.4 17.3 %decode.1 = bf16[100,2048]{1,0:T(8,128)(2,1)} custom-call(s32[3]{0:T(128)S(1)} %pad_add_fusion.others_4_.ends, s32[6144]{0:T(1024)S(1)} %mul.35.others_3_.idx, bf16[128,1024]{1,0:T(8,128)(2,1)S(1)} %pass.1.far, bf16[128,1024]{1,0:T(8,128)(2,1)S(1)} %collective-permute-done.5.near, f32[2048,128]{1,0:T(8,128)S(1)} %get-tuple-element.46.ko, ...), custom_call_target="tpu_custom_call" | custom-call | tf_op jit(solution)/shard_map/decode/pallas_call | solution.py:464
  (7 shorter events, 0.1 us)
Async XLA Ops:
  0.0 13.7 %copy-start.1 = (bf16[2048,100]{0,1:T(8,128)(2,1)S(1)}, bf16[2048,100]{0,1:T(8,128)(2,1)}, u32[]{:S(2)}) copy-start(bf16[2048,100]{0,1:T(8,128)(2,1)} %param.11) | copy-start | bytes 1228804
  0.0 13.7 %copy-start = (bf16[256,1024]{1,0:T(8,128)(2,1)S(1)}, bf16[256,1024]{1,0:T(8,128)(2,1)}, u32[]{:S(2)}) copy-start(bf16[256,1024]{1,0:T(8,128)(2,1)} %lat.3) | copy-start | bytes 1572868
  1.2 16.3 %collective-permute-start = (bf16[100,1024]{1,0:T(8,128)(2,1)S(1)}, bf16[100,1024]{1,0:T(8,128)(2,1)S(1)}, u32[]{:S(2)}, u32[]{:S(2)}) collective-permute-start(bf16[100,1024]{1,0:T(8,128)(2,1)S(1)} %get-tuple-element.52), channel_id=1, source_target_pairs={{0,1},{1,0},{2,3},{3,2},{4,5},{5,4},{6,7},{7,6},{8,9},{9,8},{10,11... | collective-permute-start | bytes 614408 | tf_op jit(solution)/shard_map/ppermute | solution.py:323
  1.2 16.2 %collective-permute-start.1 = (bf16[100,1024]{1,0:T(8,128)(2,1)S(1)}, bf16[100,1024]{1,0:T(8,128)(2,1)S(1)}, u32[]{:S(2)}, u32[]{:S(2)}) collective-permute-start(bf16[100,1024]{1,0:T(8,128)(2,1)S(1)} %get-tuple-element.51), channel_id=1, source_target_pairs={{1,2},{2,1},{3,4},{4,3},{5,6},{6,5},{7,8},{8,7},{9,10},{10,9},{11,... | collective-permute-start | bytes 614408 | tf_op jit(solution)/shard_map/ppermute | solution.py:331
  25.6 9.7 %collective-permute-start.2 = (bf16[256,1024]{1,0:T(8,128)(2,1)S(1)}, bf16[256,1024]{1,0:T(8,128)(2,1)S(1)}, u32[]{:S(2)}, u32[]{:S(2)}) collective-permute-start(bf16[256,1024]{1,0:T(8,128)(2,1)S(1)} %get-tuple-element.30.normed), channel_id=1, source_target_pairs={{0,1},{1,0},{2,3},{3,2},{4,5},{5,4},{6,7},{7,6},{8,9},{9,8},{10,11... | collective-permute-start | bytes 1572872 | tf_op jit(solution)/shard_map/ppermute | solution.py:323
  25.7 14.7 %collective-permute-start.3 = (bf16[256,1024]{1,0:T(8,128)(2,1)S(1)}, bf16[256,1024]{1,0:T(8,128)(2,1)S(1)}, u32[]{:S(2)}, u32[]{:S(2)}) collective-permute-start(bf16[256,1024]{1,0:T(8,128)(2,1)S(1)} %get-tuple-element.30.normed), channel_id=1, source_target_pairs={{1,2},{2,1},{3,4},{4,3},{5,6},{6,5},{7,8},{8,7},{9,10},{10,9},{11,... | collective-permute-start | bytes 1572872 | tf_op jit(solution)/shard_map/ppermute | solution.py:331
  45.5 11.9 %collective-permute-start.4 = (bf16[128,1024]{1,0:T(8,128)(2,1)S(1)}, bf16[128,1024]{1,0:T(8,128)(2,1)S(1)}, u32[]{:S(2)}, u32[]{:S(2)}) collective-permute-start(bf16[128,1024]{1,0:T(8,128)(2,1)S(1)} %get-tuple-element.40.outer), channel_id=1, source_target_pairs={{1,2},{2,1},{3,4},{4,3},{5,6},{6,5},{7,8},{8,7},{9,10},{10,9},{11,... | collective-permute-start | bytes 786440 | tf_op jit(solution)/shard_map/ppermute | solution.py:331
  51.2 6.2 %collective-permute-start.5 = (bf16[128,1024]{1,0:T(8,128)(2,1)S(1)}, bf16[128,1024]{1,0:T(8,128)(2,1)S(1)}, u32[]{:S(2)}, u32[]{:S(2)}) collective-permute-start(bf16[128,1024]{1,0:T(8,128)(2,1)S(1)} %window_inner.1.inner), channel_id=1, source_target_pairs={{0,1},{1,0},{2,3},{3,2},{4,5},{5,4},{6,7},{7,6},{8,9},{9,8},{10,11... | collective-permute-start | bytes 786440 | tf_op jit(solution)/shard_map/ppermute | solution.py:323

commit v11 on v10

--- a/solution.py
+++ b/solution.py
@@ -54,13 +54,29 @@
     return copies
 
 
-def fold_kernel(win, enc_w, lat, scale, *others):
-    qt, av, w0, w1, w2, sems = others[-6:]
+def lane_scale(scale, row):
+    low = low_half((1, 128))
+    factor = LOG2E / math.sqrt(SIZE)
+    return jnp.concatenate(
+        [
+            jnp.where(low, scale[row, 2 * pair] * factor, scale[row, 2 * pair + 1] * factor)
+            for pair in range(PAIRS)
+        ],
+        axis=1,
+    )
+
+
+def fold_kernel(w_in, w_out, enc_w, lat, scale, *others):
+    qt, av, win, wout, wide, w0, w1, w2, sems = others[-9:]
     got = fetch(enc_w, (1, 0, 2), (w1, w0, w2), sems)
+    wide[...] = jnp.zeros_like(wide)
+    for given, padded in ((w_in, win), (w_out, wout)):
+        wide[0 : given.shape[0], :] = given[...].astype(F32)
+        padded[...] = wide[...].astype(BF)
     got[0].wait()
     ak = dot(win[...], w1[...]).astype(BF)
     got[1].wait()
-    q = (dot(lat[...], w0[...]) * scale[0:1, :]).astype(BF)
+    q = (dot(lat[...], w0[...]) * lane_scale(scale, 0)).astype(BF)
     low = low_half((1, 128))
     for pair in range(PAIRS):
         at = slice(pair * 128, pair * 128 + 128)
@@ -166,7 +182,7 @@
     later = fetch(proc_w, (3,), (pw3,), sems.at[pl.ds(2, 1)])
     later += fetch(dec_w, (1, 2), (dw1, dw2), sems.at[pl.ds(3, 2)])
     rows = normed[...]
-    q[...] = (dot(rows, wq[...]) * scale[1:2, :]).astype(BF)
+    q[...] = (dot(rows, wq[...]) * lane_scale(scale, 1)).astype(BF)
     k[...] = dot(rows, wk[...]).astype(BF)
     v[...] = dot(rows, wv[...]).astype(BF)
     for pair in range(PAIRS):
@@ -174,7 +190,7 @@
         num[:, at], den[:, at], top[:, at] = attend_pair(q[:, at], k[:, at], v[:, at], None)
     co[...] = dot_t(wout[...], win[...]).astype(BF)
     got[0].wait()
-    aq[...] = (dot(win[...], dw0[...]) * scale[2:3, :]).astype(BF)
+    aq[...] = (dot(win[...], dw0[...]) * lane_scale(scale, 2)).astype(BF)
     got[1].wait()
     bo[...] = dot_t(dw3[...], wout[...]).astype(BF)
     for copy in later:
@@ -359,9 +375,6 @@
     grid_near = swap_near(
         lax.dynamic_slice_in_dim(channel_rows, (1 - core) * (points - BG), BG, 1)
     )
-    win = jnp.pad(w_in, ((0, CPAD - channels), (0, 0)))
-    wout = jnp.pad(w_out.T, ((0, CPAD - channels), (0, 0)))
-    scale = jnp.repeat(logit_scale * (LOG2E / math.sqrt(SIZE)), SIZE, axis=1)
     enc_idx = jnp.clip(enc_src.T, 0, points + 2 * BG - 1).reshape(-1)
     live = jnp.arange(slots, dtype=jnp.int32)[:, None] < enc_count[None, :]
     bias = jnp.where(live, 0.0, NEG).astype(F32)
@@ -369,16 +382,17 @@
     dec_idx = jnp.clip(dec_src.T - (place * rows - BL), 0, rows + 2 * BL - 1).reshape(-1) * 8
     ends = jnp.stack([WIN // 2 - place * rows, total + WIN // 2 - place * rows, core])
 
-    qt, av = pl.pallas_call(
+    padded = shape((CPAD, width))
+    qt, av, win, wout = pl.pallas_call(
         fold_kernel,
-        out_shape=(shape((HEADS, rows, CPAD)), shape((CPAD, width))),
-        in_specs=[VM, HBM, VM, VM] + [pl.BlockSpec(memory_space=pl.ANY)] * 5,
-        out_specs=(VM, VM),
-        scratch_shapes=[weight] * 3 + [dma((3,))],
+        out_shape=(shape((HEADS, rows, CPAD)), padded, padded, padded),
+        in_specs=[VM, VM, HBM, VM, SM] + [pl.BlockSpec(memory_space=pl.ANY)] * 5,
+        out_specs=(VM,) * 4,
+        scratch_shapes=[pltpu.VMEM((CPAD, width), F32)] + [weight] * 3 + [dma((3,))],
         compiler_params=params(50),
         cost_estimate=pl.CostEstimate(flops=2 * 10**9, bytes_accessed=8 * 2**20, transcendentals=0),
         name="fold",
-    )(win, enc_w, latent_init, scale, wout, enc_idx, bias, dec_idx, ends)
+    )(w_in, w_out.T, enc_w, latent_init, logit_scale, enc_idx, bias, dec_idx, ends, grid)
     square = shape((width, width))
     latent, normed, pw0, pw1, pw2 = pl.pallas_call(
         encode_kernel,
@@ -405,13 +419,13 @@
         + (shape((rows, width), F32),) * 3
         + (shape((CPAD, width)), shape((width, CPAD)), shape((CPAD, CPAD)))
         + (square,) * 3,
-        in_specs=[VM] * 7 + [HBM] * 2,
+        in_specs=[VM] * 3 + [SM] + [VM] * 3 + [HBM] * 2,
         out_specs=(VM,) * 10,
         scratch_shapes=[pltpu.VMEM((rows, width), BF)] * 2 + [weight] * 2 + [dma((5,))],
         compiler_params=params(36),
         cost_estimate=pl.CostEstimate(flops=3 * 10**9, bytes_accessed=12 * 2**20, transcendentals=0),
         name="project",
-    )(normed, win, wout, scale, pw0, pw1, pw2, proc_w, dec_w)
+    )(normed, win, wout, logit_scale, pw0, pw1, pw2, proc_w, dec_w)
     half_scratch = [
         pltpu.VMEM((rows // 2, WIN - rows // 2), F32),
         pltpu.VMEM((rows // 2, width), BF),

time: 75.1 us -> 73.9 us (0.984)
  waiting for transfers between devices: 7.29 us -> 5.33 us
  Pallas kernels: 47.3 us -> 48.8 us
  local copies, waits for them, and re-layouts: 4.24 us -> 3.2 us
  starting transfers between devices: 13.4 us -> 14.4 us
    ppermute x3, waiting for transfers between devices: 7.29 us -> 5.32 us  [swap_far(): return lax.ppermute(outer, axes, pairs)]
    pad x2 -> x0, local copies, waits for them, and re-layouts: 1.91 us -> none  [the longest x1 0.95 us: on_device(): win = jnp.pad(w_in, ((0, CPAD - channels), (0, 0)))]
    ppermute x3, starting transfers between devices: 12.9 us -> 14 us  [swap_far(): return lax.ppermute(outer, axes, pairs)]
    pad x1, local copies, waits for them, and re-layouts: 0.04 us -> 1.05 us  [on_device(): grid = jnp.pad(grid_state.T, ((0, CPAD - channels), (0, 0)))]
    pallas_call x1, Pallas kernels: 6.58 us -> 7.48 us  [on_device(): pl.pallas_call(project_kernel, out_shape=(shape((rows, width)),) + (shape...]
  transfers between devices with their start and end apart: 6 -> 6, of which waited for: 2 -> 2; matrix products, arithmetic and copies ran while one was open for 7% -> 5% of each run, Pallas kernels for 23% -> 25%
where the time goes in v11:
time: 73.9 us; the launch traced here: 73.6 us
  Pallas kernels  48.8 us (66%)
  starting transfers between devices  14.4 us (19%)
  waiting for transfers between devices  5.33 us (7%)
  local copies, waits for them, and re-layouts  3.2 us (4%)
  other arithmetic  1.58 us (2%)
    pallas_call x1, Pallas kernels, on_device(): pl.pallas_call(decode_kernel, out_shape=shape((channels, points)), in_spe...  17.3 us
    ppermute x3, starting transfers between devices, swap_far(): return lax.ppermute(outer, axes, pairs)  14 us
    pallas_call x1, Pallas kernels, on_device(): pl.pallas_call(encode_kernel, out_shape=(shape((rows, width)),) * 2 + (sq...  8.06 us
    pallas_call x1, Pallas kernels, on_device(): pl.pallas_call(project_kernel, out_shape=(shape((rows, width)),) + (shape...  7.48 us
    ppermute x3, waiting for transfers between devices, swap_far(): return lax.ppermute(outer, axes, pairs)  5.32 us
    pallas_call x1, Pallas kernels, on_device(): pl.pallas_call(window_outer_kernel, out_shape=(shape((BL, width)), wide,...  5.13 us
    pallas_call x1, Pallas kernels, on_device(): pl.pallas_call(fold_kernel, out_shape=(shape((HEADS, rows, CPAD)), padded...  4.26 us
    pallas_call x1, Pallas kernels, on_device(): pl.pallas_call(prepare_kernel, out_shape=(shape((points * 8, 128), F32),...  3.65 us
  transfers between devices with their start and end apart: 6, of which 2 were waited for; matrix products, arithmetic and copies ran while one was open for 5% of the time, Pallas kernels for 25%

profile of v11, /device:TPU:96, one launch (start us, length us, event | category | flops | bytes accessed | tf_op | source)
XLA Modules:
  0.0 73.6 jit_solution(2271731286725873795)
XLA Ops:
  0.0 0.0 copy-start.2
  0.0 0.0 copy-start
  0.0 0.0 copy-start.1
  0.0 0.0 copy-start.3
  0.0 1.1 %dynamic-slice_bitcast_fusion = (bf16[100,1024]{1,0:T(8,128)(2,1)S(1)}, bf16[100,1024]{1,0:T(8,128)(2,1)S(1)}) fusion(bf16[2048,100]{0,1:T(8,128)(2,1)} %param.11, s32[]{:T(128)S(6)} %select_n.14, s32[]{:T(128)S(6)} %select_n.13), kind=kLoop, calls=%fused_computation | loop fusion | bytes 819208 | tf_op jit(solution)/shard_map/dynamic_slice | solution.py:374
  1.2 0.1 collective-permute-start
  1.3 7.0 %collective-permute-start.1 = (bf16[100,1024]{1,0:T(8,128)(2,1)S(1)}, bf16[100,1024]{1,0:T(8,128)(2,1)S(1)}, u32[]{:S(2)}, u32[]{:S(2)}) collective-permute-start(bf16[100,1024]{1,0:T(8,128)(2,1)S(1)} %get-tuple-element.55), channel_id=1, source_target_pairs={{1,2},{2,1},{3,4},{4,3},{5,6},{6,5},{7,8},{8,7},{9,10},{10,9},{11,... | collective-permute-start | bytes 614408 | tf_op jit(solution)/shard_map/ppermute | solution.py:347
  8.3 0.8 %lt.35 = s32[16,16]{1,0:T(8,128)S(1)} reshape(s32[256]{0:T(256)} %param.14) | data formatting | bytes 2048 | tf_op jit(solution)/shard_map/lt | solution.py:379
  9.1 0.1 lt.37
  9.2 0.1 lt.33
  9.3 0.7 clamp_bitcast_fusion
  10.0 0.8 %multiply_bitcast_fusion = s32[3,2048]{1,0:T(4,128)S(1)} fusion(s32[2048,3]{0,1:T(4,128)} %param.15, s32[]{:T(128)S(6)} %sub.21), kind=kLoop, calls=%fused_computation.2 | loop fusion | flops 18432 | bytes 49156 | tf_op jit(solution)/shard_map/mul | solution.py:382
  10.8 0.1 pad_add_fusion.others_3_.ends
  10.9 1.0 %pad.4.others_4_.own.state.grid = bf16[128,2048]{1,0:T(8,128)(2,1)S(1)} pad(bf16[100,2048]{1,0:T(8,128)(2,1)} %bitcast.19, bf16[]{:T(256)} %constant.34.clone.1), padding=0_28x0_0 | pad | bytes 933890 | tf_op jit(solution)/shard_map/jit(_pad)/pad | solution.py:371
  12.0 0.0 copy-done.2
  12.0 0.0 copy-done
  12.0 0.0 copy-done.1
  12.0 0.0 copy-done.3
  12.0 4.3 %fold.1 = (bf16[16,256,128]{2,1,0:T(8,128)(2,1)S(1)}, bf16[128,1024]{1,0:T(8,128)(2,1)S(1)}, bf16[128,1024]{1,0:T(8,128)(2,1)S(1)}, bf16[128,1024]{1,0:T(8,128)(2,1)S(1)}) custom-call(bf16[100,1024]{1,0:T(8,128)(2,1)S(1)} %copy-done.1, bf16[100,1024]{1,0:T(8,128)(2,1)S(1)} %bitcast.16, bf16[4,1024,1024]{2,1,0:T(8,128)(2,1)} %enc_w.3, ...), custom_call_target="tpu_custom_call" | custom-call | flops 2000000000 | bytes 8388608 | tf_op jit(solution)/shard_map/fold/pallas_call | solution.py:386
  16.3 0.0 collective-permute-done.near
  16.3 0.0 collective-permute-done.1.far
  16.3 8.1 %encode.1 = (bf16[256,1024]{1,0:T(8,128)(2,1)S(1)}, bf16[256,1024]{1,0:T(8,128)(2,1)S(1)}, bf16[1024,1024]{1,0:T(8,128)(2,1)S(1)}, bf16[1024,1024]{1,0:T(8,128)(2,1)S(1)}, bf16[1024,1024]{1,0:T(8,128)(2,1)S(1)}) custom-call(s32[3]{0:T(128)S(1)} %pad_add_fusion.others_3_.ends, s32[4096]{0:T(1024)S(1)} %bitcast.18, ...), custom_call_target="tpu_custom_call" | custom-call | tf_op jit(solution)/shard_map/encode/pallas_call | solution.py:397
  24.4 0.1 collective-permute-start.2
  24.5 3.5 %collective-permute-start.3 = (bf16[256,1024]{1,0:T(8,128)(2,1)S(1)}, bf16[256,1024]{1,0:T(8,128)(2,1)S(1)}, u32[]{:S(2)}, u32[]{:S(2)}) collective-permute-start(bf16[256,1024]{1,0:T(8,128)(2,1)S(1)} %get-tuple-element.32.normed), channel_id=1, source_target_pairs={{1,2},{2,1},{3,4},{4,3},{5,6},{6,5},{7,8},{8,7},{9,10},{10,9},{11,... | collective-permute-start | bytes 1572872 | tf_op jit(solution)/shard_map/ppermute | solution.py:347
  28.0 7.5 %project.1 = (bf16[256,1024]{1,0:T(8,128)(2,1)S(1)}, f32[256,1024]{1,0:T(8,128)S(1)}, f32[256,1024]{1,0:T(8,128)S(1)}, f32[256,1024]{1,0:T(8,128)S(1)}, bf16[128...) custom-call(bf16[256,1024]{1,0:T(8,128)(2,1)S(1)} %get-tuple-element, ...), custom_call_target="tpu_custom_call" | custom-call | flops 3000000000 | bytes 12582912 | tf_op jit(solution)/shard_map/project/pallas_call | solution.py:416
  35.5 0.0 collective-permute-done.2.near
  35.5 3.7 %collective-permute-done.3.far = bf16[256,1024]{1,0:T(8,128)(2,1)S(1)} collective-permute-done((bf16[256,1024]{1,0:T(8,128)(2,1)S(1)}, bf16[256,1024]{1,0:T(8,128)(2,1)S(1)}, u32[]{:S(2)}, u32[]{:S(2)}) %collective-permute-start.3) | collective-permute-done | bytes 524320 | tf_op jit(solution)/shard_map/ppermute | solution.py:347
  39.2 5.1 %window_outer.1 = (bf16[128,1024]{1,0:T(8,128)(2,1)S(1)}, bf16[512,1024]{1,0:T(8,128)(2,1)S(1)}, bf16[512,1024]{1,0:T(8,128)(2,1)S(1)}) custom-call(s32[3]{0:T(128)S(1)} %pad_add_fusion.others_3_.ends, bf16[256,1024]{1,0:T(8,128)(2,1)S(1)} %get-tuple-element.38.q, f32[256,1024]{1,0:T(8,128)S(1)} %get-tuple-element.39.num, ...), custom_call_target="tpu_custom_call" | custom-call | tf_op jit(solution)/shard_map/window_outer/pallas_call | solution.py:434
  44.4 3.4 %collective-permute-start.4 = (bf16[128,1024]{1,0:T(8,128)(2,1)S(1)}, bf16[128,1024]{1,0:T(8,128)(2,1)S(1)}, u32[]{:S(2)}, u32[]{:S(2)}) collective-permute-start(bf16[128,1024]{1,0:T(8,128)(2,1)S(1)} %get-tuple-element.44.outer), channel_id=1, source_target_pairs={{1,2},{2,1},{3,4},{4,3},{5,6},{6,5},{7,8},{8,7},{9,10},{10,9},{11,... | collective-permute-start | bytes 786440 | tf_op jit(solution)/shard_map/ppermute | solution.py:347
  47.7 2.9 %window_inner.1.inner = bf16[128,1024]{1,0:T(8,128)(2,1)S(1)} custom-call(s32[3]{0:T(128)S(1)} %pad_add_fusion.others_3_.ends, bf16[256,1024]{1,0:T(8,128)(2,1)S(1)} %get-tuple-element.38.q, f32[256,1024]{1,0:T(8,128)S(1)} %get-tuple-element.39.num, f32[256,1024]{1,0:T(8,128)S(1)} %get-tuple-element.40.den, f32[256,1024]{1,0:T(8,128)S(1)} %get-tuple-element.41.top, ...), custom_call_target="tpu_custom_call" | custom-call | flops 3000000000 | bytes 12582912 | tf_op jit(solution)/shard_map/window_inner/pallas_call | solution.py:444
  50.6 0.3 collective-permute-start.5
  50.9 3.7 %prepare.1 = (f32[16384,128]{1,0:T(8,128)S(1)}, f32[2048,128]{1,0:T(8,128)S(1)}, f32[2048,128]{1,0:T(8,128)S(1)}) custom-call(s32[3]{0:T(128)S(1)} %pad_add_fusion.others_3_.ends, bf16[128,1024]{1,0:T(8,128)(2,1)S(1)} %window_inner.1.inner, bf16[128,1024]{1,0:T(8,128)(2,1)S(1)} %get-tuple-element.44.outer, ...), custom_call_target="tpu_custom_call" | custom-call | flops 1000000 | bytes 65536 | tf_op jit(solution)/shard_map/prepare/pallas_call | solution.py:465
  54.6 1.7 %collective-permute-done.4.given = bf16[128,1024]{1,0:T(8,128)(2,1)S(1)} collective-permute-done((bf16[128,1024]{1,0:T(8,128)(2,1)S(1)}, bf16[128,1024]{1,0:T(8,128)(2,1)S(1)}, u32[]{:S(2)}, u32[]{:S(2)}) %collective-permute-start.4) | collective-permute-done | bytes 262176 | tf_op jit(solution)/shard_map/ppermute | solution.py:347
  56.3 0.0 collective-permute-done.5.near
  56.3 17.3 %decode.1 = bf16[100,2048]{1,0:T(8,128)(2,1)} custom-call(s32[3]{0:T(128)S(1)} %pad_add_fusion.others_3_.ends, s32[6144]{0:T(1024)S(1)} %mul.29.others_2_.idx, bf16[128,1024]{1,0:T(8,128)(2,1)S(1)} %pass.1.far, bf16[128,1024]{1,0:T(8,128)(2,1)S(1)} %collective-permute-done.5.near, f32[2048,128]{1,0:T(8,128)S(1)} %get-tuple-element.50.ko, ...), custom_call_target="tpu_custom_call" | custom-call | tf_op jit(solution)/shard_map/decode/pallas_call | solution.py:478
  (6 shorter events, 0.1 us)
Async XLA Ops:
  0.0 12.0 %copy-start.2 = (bf16[1024,100]{0,1:T(8,128)(2,1)S(1)}, bf16[1024,100]{0,1:T(8,128)(2,1)}, u32[]{:S(2)}) copy-start(bf16[1024,100]{0,1:T(8,128)(2,1)} %param.20) | copy-start | bytes 614404
  0.0 12.0 %copy-start = (bf16[256,1024]{1,0:T(8,128)(2,1)S(1)}, bf16[256,1024]{1,0:T(8,128)(2,1)}, u32[]{:S(2)}) copy-start(bf16[256,1024]{1,0:T(8,128)(2,1)} %lat.3) | copy-start | bytes 1572868
  0.0 12.0 %copy-start.1 = (bf16[100,1024]{1,0:T(8,128)(2,1)S(1)}, bf16[100,1024]{1,0:T(8,128)(2,1)}, u32[]{:S(2)}) copy-start(bf16[100,1024]{1,0:T(8,128)(2,1)} %w_in.1) | copy-start | bytes 614404
  0.0 12.0 %copy-start.3 = (f32[3,16]{1,0:T(4,128)S(1)}, f32[3,16]{1,0:T(4,128)}, u32[]{:S(2)}) copy-start(f32[3,16]{1,0:T(4,128)} %scale.3) | copy-start | bytes 580
  1.2 15.1 %collective-permute-start = (bf16[100,1024]{1,0:T(8,128)(2,1)S(1)}, bf16[100,1024]{1,0:T(8,128)(2,1)S(1)}, u32[]{:S(2)}, u32[]{:S(2)}) collective-permute-start(bf16[100,1024]{1,0:T(8,128)(2,1)S(1)} %get-tuple-element.56), channel_id=1, source_target_pairs={{0,1},{1,0},{2,3},{3,2},{4,5},{5,4},{6,7},{7,6},{8,9},{9,8},{10,11... | collective-permute-start | bytes 614408 | tf_op jit(solution)/shard_map/ppermute | solution.py:339
  1.3 15.1 %collective-permute-start.1 = (bf16[100,1024]{1,0:T(8,128)(2,1)S(1)}, bf16[100,1024]{1,0:T(8,128)(2,1)S(1)}, u32[]{:S(2)}, u32[]{:S(2)}) collective-permute-start(bf16[100,1024]{1,0:T(8,128)(2,1)S(1)} %get-tuple-element.55), channel_id=1, source_target_pairs={{1,2},{2,1},{3,4},{4,3},{5,6},{6,5},{7,8},{8,7},{9,10},{10,9},{11,... | collective-permute-start | bytes 614408 | tf_op jit(solution)/shard_map/ppermute | solution.py:347
  24.4 11.1 %collective-permute-start.2 = (bf16[256,1024]{1,0:T(8,128)(2,1)S(1)}, bf16[256,1024]{1,0:T(8,128)(2,1)S(1)}, u32[]{:S(2)}, u32[]{:S(2)}) collective-permute-start(bf16[256,1024]{1,0:T(8,128)(2,1)S(1)} %get-tuple-element.32.normed), channel_id=1, source_target_pairs={{0,1},{1,0},{2,3},{3,2},{4,5},{5,4},{6,7},{7,6},{8,9},{9,8},{10,11... | collective-permute-start | bytes 1572872 | tf_op jit(solution)/shard_map/ppermute | solution.py:339
  24.5 14.7 %collective-permute-start.3 = (bf16[256,1024]{1,0:T(8,128)(2,1)S(1)}, bf16[256,1024]{1,0:T(8,128)(2,1)S(1)}, u32[]{:S(2)}, u32[]{:S(2)}) collective-permute-start(bf16[256,1024]{1,0:T(8,128)(2,1)S(1)} %get-tuple-element.32.normed), channel_id=1, source_target_pairs={{1,2},{2,1},{3,4},{4,3},{5,6},{6,5},{7,8},{8,7},{9,10},{10,9},{11,... | collective-permute-start | bytes 1572872 | tf_op jit(solution)/shard_map/ppermute | solution.py:347
  44.4 11.9 %collective-permute-start.4 = (bf16[128,1024]{1,0:T(8,128)(2,1)S(1)}, bf16[128,1024]{1,0:T(8,128)(2,1)S(1)}, u32[]{:S(2)}, u32[]{:S(2)}) collective-permute-start(bf16[128,1024]{1,0:T(8,128)(2,1)S(1)} %get-tuple-element.44.outer), channel_id=1, source_target_pairs={{1,2},{2,1},{3,4},{4,3},{5,6},{6,5},{7,8},{8,7},{9,10},{10,9},{11,... | collective-permute-start | bytes 786440 | tf_op jit(solution)/shard_map/ppermute | solution.py:347
  50.6 5.6 %collective-permute-start.5 = (bf16[128,1024]{1,0:T(8,128)(2,1)S(1)}, bf16[128,1024]{1,0:T(8,128)(2,1)S(1)}, u32[]{:S(2)}, u32[]{:S(2)}) collective-permute-start(bf16[128,1024]{1,0:T(8,128)(2,1)S(1)} %window_inner.1.inner), channel_id=1, source_target_pairs={{0,1},{1,0},{2,3},{3,2},{4,5},{5,4},{6,7},{7,6},{8,9},{9,8},{10,11... | collective-permute-start | bytes 786440 | tf_op jit(solution)/shard_map/ppermute | solution.py:339

commit v12 on v10

--- a/solution.py
+++ b/solution.py
@@ -54,9 +54,17 @@
     return copies
 
 
-def fold_kernel(win, enc_w, lat, scale, *others):
-    qt, av, w0, w1, w2, sems = others[-6:]
+def fold_kernel(w_in, w_out, state, enc_w, lat, scale, *others):
+    qt, av, win, wout, grid, wide, w0, w1, w2, sems = others[-10:]
     got = fetch(enc_w, (1, 0, 2), (w1, w0, w2), sems)
+    wide[...] = jnp.zeros_like(wide)
+    for given, padded in ((w_in, win), (w_out, wout)):
+        wide[0 : given.shape[0], :] = given[...].astype(F32)
+        padded[...] = wide[...].astype(BF)
+    reach = wide.shape[1]
+    for begin in range(0, state.shape[1], reach):
+        wide[0 : state.shape[0], :] = state[:, begin : begin + reach].astype(F32)
+        grid[:, begin : begin + reach] = wide[...].astype(BF)
     got[0].wait()
     ak = dot(win[...], w1[...]).astype(BF)
     got[1].wait()
@@ -352,15 +360,12 @@
     weight = pltpu.VMEM((width, width), BF)
     dma = pltpu.SemaphoreType.DMA
 
-    grid = jnp.pad(grid_state.T, ((0, CPAD - channels), (0, 0)))
     core = lax.axis_index("narrow")
     channel_rows = grid_state.T
     grid_far = swap_far(lax.dynamic_slice_in_dim(channel_rows, core * (points - BG), BG, 1))
     grid_near = swap_near(
         lax.dynamic_slice_in_dim(channel_rows, (1 - core) * (points - BG), BG, 1)
     )
-    win = jnp.pad(w_in, ((0, CPAD - channels), (0, 0)))
-    wout = jnp.pad(w_out.T, ((0, CPAD - channels), (0, 0)))
     scale = jnp.repeat(logit_scale * (LOG2E / math.sqrt(SIZE)), SIZE, axis=1)
     enc_idx = jnp.clip(enc_src.T, 0, points + 2 * BG - 1).reshape(-1)
     live = jnp.arange(slots, dtype=jnp.int32)[:, None] < enc_count[None, :]
@@ -369,16 +374,17 @@
     dec_idx = jnp.clip(dec_src.T - (place * rows - BL), 0, rows + 2 * BL - 1).reshape(-1) * 8
     ends = jnp.stack([WIN // 2 - place * rows, total + WIN // 2 - place * rows, core])
 
-    qt, av = pl.pallas_call(
+    padded = shape((CPAD, width))
+    qt, av, win, wout, grid = pl.pallas_call(
         fold_kernel,
-        out_shape=(shape((HEADS, rows, CPAD)), shape((CPAD, width))),
-        in_specs=[VM, HBM, VM, VM] + [pl.BlockSpec(memory_space=pl.ANY)] * 5,
-        out_specs=(VM, VM),
-        scratch_shapes=[weight] * 3 + [dma((3,))],
+        out_shape=(shape((HEADS, rows, CPAD)), padded, padded, padded, shape((CPAD, points))),
+        in_specs=[VM, VM, VM, HBM, VM, VM] + [pl.BlockSpec(memory_space=pl.ANY)] * 4,
+        out_specs=(VM,) * 5,
+        scratch_shapes=[pltpu.VMEM((CPAD, width), F32)] + [weight] * 3 + [dma((3,))],
         compiler_params=params(50),
         cost_estimate=pl.CostEstimate(flops=2 * 10**9, bytes_accessed=8 * 2**20, transcendentals=0),
         name="fold",
-    )(win, enc_w, latent_init, scale, wout, enc_idx, bias, dec_idx, ends)
+    )(w_in, w_out.T, grid_state.T, enc_w, latent_init, scale, enc_idx, bias, dec_idx, ends)
     square = shape((width, width))
     latent, normed, pw0, pw1, pw2 = pl.pallas_call(
         encode_kernel,

time: 75.1 us -> 77.1 us (1.027)
  local copies, waits for them, and re-layouts: 4.24 us -> 6.12 us
    unnamed x5 -> x11, local copies, waits for them, and re-layouts: 0.02 us -> 3.92 us
    pad x3 -> x0, local copies, waits for them, and re-layouts: 1.95 us -> none  [the longest x1 0.95 us: on_device(): win = jnp.pad(w_in, ((0, CPAD - channels), (0, 0)))]
  transfers between devices with their start and end apart: 6 -> 6, of which waited for: 2 -> 2; matrix products, arithmetic and copies ran while one was open for 7% -> 4% of each run, Pallas kernels for 23% -> 22%
where the time goes in v12:
time: 77.1 us; the launch traced here: 76.7 us
  Pallas kernels  47.4 us (61%)
  starting transfers between devices  13.4 us (17%)
  waiting for transfers between devices  7.25 us (9%)
  local copies, waits for them, and re-layouts  6.12 us (8%)
  other arithmetic  2.27 us (3%)
    pallas_call x1, Pallas kernels, on_device(): pl.pallas_call(decode_kernel, out_shape=shape((channels, points)), in_spe...  17.4 us
    ppermute x3, starting transfers between devices, swap_far(): return lax.ppermute(outer, axes, pairs)  12.9 us
    pallas_call x1, Pallas kernels, on_device(): pl.pallas_call(encode_kernel, out_shape=(shape((rows, width)),) * 2 + (sq...  8.07 us
    ppermute x3, waiting for transfers between devices, swap_far(): return lax.ppermute(outer, axes, pairs)  7.25 us
    pallas_call x1, Pallas kernels, on_device(): pl.pallas_call(project_kernel, out_shape=(shape((rows, width)),) + (shape...  6.59 us
    pallas_call x1, Pallas kernels, on_device(): pl.pallas_call(window_outer_kernel, out_shape=(shape((BL, width)), wide,...  5.11 us
    unnamed x11, local copies, waits for them, and re-layouts  3.92 us
    pallas_call x1, Pallas kernels, on_device(): pl.pallas_call(fold_kernel, out_shape=(shape((HEADS, rows, CPAD)), padded...  3.75 us
  transfers between devices with their start and end apart: 6, of which 2 were waited for; matrix products, arithmetic and copies ran while one was open for 4% of the time, Pallas kernels for 22%

profile of v12, /device:TPU:96, one launch (start us, length us, event | category | flops | bytes accessed | tf_op | source)
XLA Modules:
  0.0 76.7 jit_solution(4960084429037002222)
XLA Ops:
  0.0 1.1 %dynamic-slice_bitcast_fusion = (bf16[100,1024]{1,0:T(8,128)(2,1)S(1)}, bf16[100,1024]{1,0:T(8,128)(2,1)S(1)}) fusion(bf16[2048,100]{0,1:T(8,128)(2,1)} %param.11, s32[]{:T(128)S(6)} %select_n.15, s32[]{:T(128)S(6)} %select_n.13), kind=kLoop, calls=%fused_computation | loop fusion | bytes 819208 | tf_op jit(solution)/shard_map/dynamic_slice | solution.py:365
  1.1 0.1 collective-permute-start
  1.2 7.0 %collective-permute-start.1 = (bf16[100,1024]{1,0:T(8,128)(2,1)S(1)}, bf16[100,1024]{1,0:T(8,128)(2,1)S(1)}, u32[]{:S(2)}, u32[]{:S(2)}) collective-permute-start(bf16[100,1024]{1,0:T(8,128)(2,1)S(1)} %get-tuple-element.57), channel_id=1, source_target_pairs={{1,2},{2,1},{3,4},{4,3},{5,6},{6,5},{7,8},{8,7},{9,10},{10,9},{11,... | collective-permute-start | bytes 614408 | tf_op jit(solution)/shard_map/ppermute | solution.py:339
  8.2 0.8 lt.34
  9.0 0.1 lt.36
  9.1 0.1 lt.32
  9.2 0.7 broadcast_multiply_fusion
  9.9 0.7 clamp_bitcast_fusion
  10.6 0.8 %multiply_bitcast_fusion = s32[3,2048]{1,0:T(4,128)S(1)} fusion(s32[2048,3]{0,1:T(4,128)} %param.15, s32[]{:T(128)S(6)} %sub.21), kind=kLoop, calls=%fused_computation.2 | loop fusion | flops 18432 | bytes 49156 | tf_op jit(solution)/shard_map/mul | solution.py:374
  11.4 0.1 pad_add_fusion.others_3_.ends
  11.5 0.1 broadcast_in_dim.13
  11.6 0.1 reshape.23.scale
  11.7 0.0 copy-start
  11.7 1.0 %copy-done = bf16[256,1024]{1,0:T(8,128)(2,1)S(1)} copy-done((bf16[256,1024]{1,0:T(8,128)(2,1)S(1)}, bf16[256,1024]{1,0:T(8,128)(2,1)}, u32[]{:S(2)}) %copy-start) | copy-done | bytes 524312
  12.7 0.0 copy-start.2
  12.7 1.0 %copy-done.2 = bf16[2048,100]{0,1:T(8,128)(2,1)S(1)} copy-done((bf16[2048,100]{0,1:T(8,128)(2,1)S(1)}, bf16[2048,100]{0,1:T(8,128)(2,1)}, u32[]{:S(2)}) %copy-start.2) | copy-done | bytes 409624
  13.7 0.0 copy-start.3
  13.7 0.9 %copy-done.3 = bf16[100,1024]{1,0:T(8,128)(2,1)S(1)} copy-done((bf16[100,1024]{1,0:T(8,128)(2,1)S(1)}, bf16[100,1024]{1,0:T(8,128)(2,1)}, u32[]{:S(2)}) %copy-start.3) | copy-done | bytes 204824
  14.7 0.0 copy-start.4
  14.7 0.9 %copy-done.4 = bf16[1024,100]{0,1:T(8,128)(2,1)S(1)} copy-done((bf16[1024,100]{0,1:T(8,128)(2,1)S(1)}, bf16[1024,100]{0,1:T(8,128)(2,1)}, u32[]{:S(2)}) %copy-start.4) | copy-done | bytes 204824
  15.6 0.0 copy-start.1
  15.6 3.8 %fold.1 = (bf16[16,256,128]{2,1,0:T(8,128)(2,1)S(1)}, bf16[128,1024]{1,0:T(8,128)(2,1)S(1)}, bf16[128,1024]{1,0:T(8,128)(2,1)S(1)}, bf16[128,1024]{1,0:T(8,128)(2,1)S(1)}, bf16[128,2048]{1,0:T(8,128)(2,1)S(1)}) custom-call(bf16[100,1024]{1,0:T(8,128)(2,1)S(1)} %copy-done.3, bf16[100,1024]{1,0:T(8,128)(2,1)S(1)} %bitcast.17, bf16[100,2048]{1,0:T(8,128)(2,1)S(1)} %bitcast.16, ...), custom_call_target="tpu_custom_call" | custom-call | flops 2000000000 | bytes 8388608 | tf_op jit(solution)/shard_map/fold/pallas_call | solution.py:378
  19.4 0.0 collective-permute-done.near
  19.4 0.0 collective-permute-done.1.far
  19.4 0.0 copy-done.1
  19.4 8.1 %encode.1 = (bf16[256,1024]{1,0:T(8,128)(2,1)S(1)}, bf16[256,1024]{1,0:T(8,128)(2,1)S(1)}, bf16[1024,1024]{1,0:T(8,128)(2,1)S(1)}, bf16[1024,1024]{1,0:T(8,128)(2,1)S(1)}, bf16[1024,1024]{1,0:T(8,128)(2,1)S(1)}) custom-call(s32[3]{0:T(128)S(1)} %pad_add_fusion.others_3_.ends, s32[4096]{0:T(1024)S(1)} %bitcast.19, ...), custom_call_target="tpu_custom_call" | custom-call | tf_op jit(solution)/shard_map/encode/pallas_call | solution.py:389
  27.5 0.1 collective-permute-start.2
  27.6 3.0 %collective-permute-start.3 = (bf16[256,1024]{1,0:T(8,128)(2,1)S(1)}, bf16[256,1024]{1,0:T(8,128)(2,1)S(1)}, u32[]{:S(2)}, u32[]{:S(2)}) collective-permute-start(bf16[256,1024]{1,0:T(8,128)(2,1)S(1)} %get-tuple-element.34.normed), channel_id=1, source_target_pairs={{1,2},{2,1},{3,4},{4,3},{5,6},{6,5},{7,8},{8,7},{9,10},{10,9},{11,... | collective-permute-start | bytes 1572872 | tf_op jit(solution)/shard_map/ppermute | solution.py:339
  30.6 6.6 %project.1 = (bf16[256,1024]{1,0:T(8,128)(2,1)S(1)}, f32[256,1024]{1,0:T(8,128)S(1)}, f32[256,1024]{1,0:T(8,128)S(1)}, f32[256,1024]{1,0:T(8,128)S(1)}, bf16[128...) custom-call(bf16[256,1024]{1,0:T(8,128)(2,1)S(1)} %get-tuple-element, ...), custom_call_target="tpu_custom_call" | custom-call | flops 3000000000 | bytes 12582912 | tf_op jit(solution)/shard_map/project/pallas_call | solution.py:408
  37.2 0.0 collective-permute-done.2.near
  37.2 5.1 %collective-permute-done.3.far = bf16[256,1024]{1,0:T(8,128)(2,1)S(1)} collective-permute-done((bf16[256,1024]{1,0:T(8,128)(2,1)S(1)}, bf16[256,1024]{1,0:T(8,128)(2,1)S(1)}, u32[]{:S(2)}, u32[]{:S(2)}) %collective-permute-start.3) | collective-permute-done | bytes 524320 | tf_op jit(solution)/shard_map/ppermute | solution.py:339
  42.3 5.1 %window_outer.1 = (bf16[128,1024]{1,0:T(8,128)(2,1)S(1)}, bf16[512,1024]{1,0:T(8,128)(2,1)S(1)}, bf16[512,1024]{1,0:T(8,128)(2,1)S(1)}) custom-call(s32[3]{0:T(128)S(1)} %pad_add_fusion.others_3_.ends, bf16[256,1024]{1,0:T(8,128)(2,1)S(1)} %get-tuple-element.40.q, f32[256,1024]{1,0:T(8,128)S(1)} %get-tuple-element.41.num, ...), custom_call_target="tpu_custom_call" | custom-call | tf_op jit(solution)/shard_map/window_outer/pallas_call | solution.py:426
  47.4 2.8 %collective-permute-start.4 = (bf16[128,1024]{1,0:T(8,128)(2,1)S(1)}, bf16[128,1024]{1,0:T(8,128)(2,1)S(1)}, u32[]{:S(2)}, u32[]{:S(2)}) collective-permute-start(bf16[128,1024]{1,0:T(8,128)(2,1)S(1)} %get-tuple-element.46.outer), channel_id=1, source_target_pairs={{1,2},{2,1},{3,4},{4,3},{5,6},{6,5},{7,8},{8,7},{9,10},{10,9},{11,... | collective-permute-start | bytes 786440 | tf_op jit(solution)/shard_map/ppermute | solution.py:339
  50.2 2.9 %window_inner.1.inner = bf16[128,1024]{1,0:T(8,128)(2,1)S(1)} custom-call(s32[3]{0:T(128)S(1)} %pad_add_fusion.others_3_.ends, bf16[256,1024]{1,0:T(8,128)(2,1)S(1)} %get-tuple-element.40.q, f32[256,1024]{1,0:T(8,128)S(1)} %get-tuple-element.41.num, f32[256,1024]{1,0:T(8,128)S(1)} %get-tuple-element.42.den, f32[256,1024]{1,0:T(8,128)S(1)} %get-tuple-element.43.top, ...), custom_call_target="tpu_custom_call" | custom-call | flops 3000000000 | bytes 12582912 | tf_op jit(solution)/shard_map/window_inner/pallas_call | solution.py:436
  53.1 0.3 collective-permute-start.5
  53.5 3.7 %prepare.1 = (f32[16384,128]{1,0:T(8,128)S(1)}, f32[2048,128]{1,0:T(8,128)S(1)}, f32[2048,128]{1,0:T(8,128)S(1)}) custom-call(s32[3]{0:T(128)S(1)} %pad_add_fusion.others_3_.ends, bf16[128,1024]{1,0:T(8,128)(2,1)S(1)} %window_inner.1.inner, bf16[128,1024]{1,0:T(8,128)(2,1)S(1)} %get-tuple-element.46.outer, ...), custom_call_target="tpu_custom_call" | custom-call | flops 1000000 | bytes 65536 | tf_op jit(solution)/shard_map/prepare/pallas_call | solution.py:457
  57.1 2.2 %collective-permute-done.4.given = bf16[128,1024]{1,0:T(8,128)(2,1)S(1)} collective-permute-done((bf16[128,1024]{1,0:T(8,128)(2,1)S(1)}, bf16[128,1024]{1,0:T(8,128)(2,1)S(1)}, u32[]{:S(2)}, u32[]{:S(2)}) %collective-permute-start.4) | collective-permute-done | bytes 262176 | tf_op jit(solution)/shard_map/ppermute | solution.py:339
  59.3 0.0 collective-permute-done.5.near
  59.3 17.4 %decode.1 = bf16[100,2048]{1,0:T(8,128)(2,1)} custom-call(s32[3]{0:T(128)S(1)} %pad_add_fusion.others_3_.ends, s32[6144]{0:T(1024)S(1)} %mul.35.others_2_.idx, bf16[128,1024]{1,0:T(8,128)(2,1)S(1)} %pass.1.far, bf16[128,1024]{1,0:T(8,128)(2,1)S(1)} %collective-permute-done.5.near, f32[2048,128]{1,0:T(8,128)S(1)} %get-tuple-element.52.ko, ...), custom_call_target="tpu_custom_call" | custom-call | tf_op jit(solution)/shard_map/decode/pallas_call | solution.py:470
  (6 shorter events, 0.0 us)
Async XLA Ops:
  1.1 18.3 %collective-permute-start = (bf16[100,1024]{1,0:T(8,128)(2,1)S(1)}, bf16[100,1024]{1,0:T(8,128)(2,1)S(1)}, u32[]{:S(2)}, u32[]{:S(2)}) collective-permute-start(bf16[100,1024]{1,0:T(8,128)(2,1)S(1)} %get-tuple-element.58), channel_id=1, source_target_pairs={{0,1},{1,0},{2,3},{3,2},{4,5},{5,4},{6,7},{7,6},{8,9},{9,8},{10,11... | collective-permute-start | bytes 614408 | tf_op jit(solution)/shard_map/ppermute | solution.py:331
  1.2 18.2 %collective-permute-start.1 = (bf16[100,1024]{1,0:T(8,128)(2,1)S(1)}, bf16[100,1024]{1,0:T(8,128)(2,1)S(1)}, u32[]{:S(2)}, u32[]{:S(2)}) collective-permute-start(bf16[100,1024]{1,0:T(8,128)(2,1)S(1)} %get-tuple-element.57), channel_id=1, source_target_pairs={{1,2},{2,1},{3,4},{4,3},{5,6},{6,5},{7,8},{8,7},{9,10},{10,9},{11,... | collective-permute-start | bytes 614408 | tf_op jit(solution)/shard_map/ppermute | solution.py:339
  11.7 1.0 %copy-start = (bf16[256,1024]{1,0:T(8,128)(2,1)S(1)}, bf16[256,1024]{1,0:T(8,128)(2,1)}, u32[]{:S(2)}) copy-start(bf16[256,1024]{1,0:T(8,128)(2,1)} %lat.3) | copy-start | bytes 1572868
  12.7 1.0 %copy-start.2 = (bf16[2048,100]{0,1:T(8,128)(2,1)S(1)}, bf16[2048,100]{0,1:T(8,128)(2,1)}, u32[]{:S(2)}) copy-start(bf16[2048,100]{0,1:T(8,128)(2,1)} %param.11) | copy-start | bytes 1228804
  13.7 0.9 %copy-start.3 = (bf16[100,1024]{1,0:T(8,128)(2,1)S(1)}, bf16[100,1024]{1,0:T(8,128)(2,1)}, u32[]{:S(2)}) copy-start(bf16[100,1024]{1,0:T(8,128)(2,1)} %w_in.1) | copy-start | bytes 614404
  14.7 0.9 %copy-start.4 = (bf16[1024,100]{0,1:T(8,128)(2,1)S(1)}, bf16[1024,100]{0,1:T(8,128)(2,1)}, u32[]{:S(2)}) copy-start(bf16[1024,100]{0,1:T(8,128)(2,1)} %param.20) | copy-start | bytes 614404
  15.6 3.8 %copy-start.1 = (bf16[256,1024]{1,0:T(8,128)(2,1)S(1)}, bf16[256,1024]{1,0:T(8,128)(2,1)}, u32[]{:S(2)}) copy-start(bf16[256,1024]{1,0:T(8,128)(2,1)} %lat.3) | copy-start | bytes 1572868
  27.5 9.7 %collective-permute-start.2 = (bf16[256,1024]{1,0:T(8,128)(2,1)S(1)}, bf16[256,1024]{1,0:T(8,128)(2,1)S(1)}, u32[]{:S(2)}, u32[]{:S(2)}) collective-permute-start(bf16[256,1024]{1,0:T(8,128)(2,1)S(1)} %get-tuple-element.34.normed), channel_id=1, source_target_pairs={{0,1},{1,0},{2,3},{3,2},{4,5},{5,4},{6,7},{7,6},{8,9},{9,8},{10,11... | collective-permute-start | bytes 1572872 | tf_op jit(solution)/shard_map/ppermute | solution.py:331
  27.6 14.7 %collective-permute-start.3 = (bf16[256,1024]{1,0:T(8,128)(2,1)S(1)}, bf16[256,1024]{1,0:T(8,128)(2,1)S(1)}, u32[]{:S(2)}, u32[]{:S(2)}) collective-permute-start(bf16[256,1024]{1,0:T(8,128)(2,1)S(1)} %get-tuple-element.34.normed), channel_id=1, source_target_pairs={{1,2},{2,1},{3,4},{4,3},{5,6},{6,5},{7,8},{8,7},{9,10},{10,9},{11,... | collective-permute-start | bytes 1572872 | tf_op jit(solution)/shard_map/ppermute | solution.py:339
  47.4 11.9 %collective-permute-start.4 = (bf16[128,1024]{1,0:T(8,128)(2,1)S(1)}, bf16[128,1024]{1,0:T(8,128)(2,1)S(1)}, u32[]{:S(2)}, u32[]{:S(2)}) collective-permute-start(bf16[128,1024]{1,0:T(8,128)(2,1)S(1)} %get-tuple-element.46.outer), channel_id=1, source_target_pairs={{1,2},{2,1},{3,4},{4,3},{5,6},{6,5},{7,8},{8,7},{9,10},{10,9},{11,... | collective-permute-start | bytes 786440 | tf_op jit(solution)/shard_map/ppermute | solution.py:339
  53.1 6.2 %collective-permute-start.5 = (bf16[128,1024]{1,0:T(8,128)(2,1)S(1)}, bf16[128,1024]{1,0:T(8,128)(2,1)S(1)}, u32[]{:S(2)}, u32[]{:S(2)}) collective-permute-start(bf16[128,1024]{1,0:T(8,128)(2,1)S(1)} %window_inner.1.inner), channel_id=1, source_target_pairs={{0,1},{1,0},{2,3},{3,2},{4,5},{5,4},{6,7},{7,6},{8,9},{9,8},{10,11... | collective-permute-start | bytes 786440 | tf_op jit(solution)/shard_map/ppermute | solution.py:331
